TPU v7x, 256 devices: a whole 4x4x8 slice. The times are simulated.
256 devices in a mesh: ctx: 16 (over y_hi, z), tp: 4 (over y_lo, core), row: 4 (over x).
Axes of the slice: x: 4, y: 4 (y_hi: 2, y_lo: 2; y = y_hi * 2 + y_lo), z: 8, core: 2. Of those that a mesh axis runs over, the one named last changes fastest.
Arguments:
- queries: bfloat16 [512, 8, 8192], P('ctx', 'row', 'tp'), may hold values from -8 to 8
- new_keys: bfloat16 [512, 8, 1024], P('ctx', 'row', 'tp'), may hold values from -4 to 4
- new_values: bfloat16 [512, 8, 1024], P('ctx', 'row', 'tp'), may hold values from -6 to 6
- cache_keys: bfloat16 [8, 4096, 1024], P('row', 'ctx', 'tp'), may hold values from -4 to 4
- cache_values: bfloat16 [8, 4096, 1024], P('row', 'ctx', 'tp'), may hold values from -6 to 6
- out_proj: bfloat16 [8192, 8192], P('tp', ('ctx', 'row')), may hold values from -0.0625 to 0.0625
- skip_blocks: int32 [8], P('row'), may hold values from 1 to 4, 12 in all
- cache_len: int32 [8], P('row'), may hold values from 2048 to 4096, as said below
Outputs:
- projected: float32 [512, 8, 8192], P('tp', 'row', 'ctx')
Inputs may be any that keep to these rules, and one draw needn't show every extreme that they name: `skip_blocks`: the counts sum to 12 and the largest is 4. `cache_len`: some row has exactly 4096.
All inputs are finite; a program needn't handle non-finite values. No bound on the sum of `skip_blocks` on one device may be relied on, other than what follows from the above.
Results may differ from a plain program's by a relative error of at most 0.008.
Values may be sent and summed in bfloat16 or wider, within the bound.
No kernel may reach another device: no remote copies, remote signals or barrier semaphores. Data moves between devices by JAX's collectives and lax.ppermute only.
A program may use at most 128 MiB of HBM per device.

v0:
```python
import jax
import jax.numpy as jnp
from jax import lax
from jax.sharding import PartitionSpec as P

DH = 128
BLOCK = 128


masked_score = -1e30


def attend_block(query_rows, key_rows, value_rows, allowed):
    query_count = query_rows.shape[0]
    head_width = key_rows.shape[1]
    flat_rows = query_rows.reshape(-1, head_width)
    scores = jnp.einsum(
        "qd,kd->qk", flat_rows, key_rows, preferred_element_type=jnp.float32
    ) * head_width ** (-0.5)
    scores = jnp.where(allowed, scores, masked_score)
    highest = jnp.max(scores, axis=1)
    weights = jnp.where(allowed, jnp.exp(scores - highest[:, None]), 0.0)
    totals = jnp.sum(weights, axis=1)
    summed = jnp.dot(weights.astype(jnp.bfloat16), value_rows, preferred_element_type=jnp.float32)
    group_size = flat_rows.shape[0] // query_count
    return (
        highest.reshape(query_count, group_size),
        totals.reshape(query_count, group_size),
        summed.reshape(query_count, group_size * head_width),
    )


def attend_rows(query_rows, key_list, value_list, allowed_list):
    kv_heads = key_list[0].shape[1] // DH
    group_width = query_rows.shape[2] // kv_heads
    maxima, totals, summed = ([], [], [])
    for row_index in range(len(key_list)):
        outcomes = [
            attend_block(
                query_rows[:, row_index, kv_index * group_width : (kv_index + 1) * group_width],
                key_list[row_index][:, kv_index * DH : (kv_index + 1) * DH],
                value_list[row_index][:, kv_index * DH : (kv_index + 1) * DH],
                allowed_list[row_index],
            )
            for kv_index in range(kv_heads)
        ]
        maxima.append(jnp.concatenate([outcome[0] for outcome in outcomes], axis=1))
        totals.append(jnp.concatenate([outcome[1] for outcome in outcomes], axis=1))
        summed.append(jnp.concatenate([outcome[2] for outcome in outcomes], axis=1))
    return (jnp.stack(maxima, axis=1), jnp.stack(totals, axis=1), jnp.stack(summed, axis=1))


def cache_part(query_rows, cache_keys, cache_values, first_slot, offset):
    rows_here = cache_keys.shape[0]
    positions = offset + jnp.arange(cache_keys.shape[1], dtype=jnp.int32)
    allowed_list = [(positions < first_slot[row_index])[None, :] for row_index in range(rows_here)]
    return attend_rows(
        query_rows,
        [cache_keys[row_index] for row_index in range(rows_here)],
        [cache_values[row_index] for row_index in range(rows_here)],
        allowed_list,
    )


def new_part(query_rows, token_base, all_keys, all_values):
    group_size = query_rows.shape[2] // all_keys.shape[2]
    query_index = token_base + jnp.repeat(
        jnp.arange(query_rows.shape[0], dtype=jnp.int32), group_size
    )
    allowed = jnp.arange(all_keys.shape[0], dtype=jnp.int32)[None, :] <= query_index[:, None]
    rows_here = all_keys.shape[1]
    return attend_rows(
        query_rows,
        [all_keys[:, row_index] for row_index in range(rows_here)],
        [all_values[:, row_index] for row_index in range(rows_here)],
        [allowed] * rows_here,
    )


def merge_parts(earlier, incoming):
    common_peak = jnp.maximum(earlier[0], incoming[0])
    early_factor = jnp.exp(earlier[0] - common_peak)
    later_factor = jnp.exp(incoming[0] - common_peak)
    full_shape = earlier[2].shape
    split_shape = common_peak.shape + (-1,)
    summed = (
        earlier[2].reshape(split_shape) * early_factor[..., None]
        + incoming[2].reshape(split_shape) * later_factor[..., None]
    )
    return (
        common_peak,
        earlier[1] * early_factor + incoming[1] * later_factor,
        summed.reshape(full_shape),
    )


def fold_sources(peaks, totals, summed):
    common_peak = jnp.max(peaks, axis=0)
    factors = jnp.exp(peaks - common_peak[None])
    merged_totals = jnp.sum(totals * factors, axis=0)
    split_shape = peaks.shape + (-1,)
    merged_summed = jnp.sum(summed.reshape(split_shape) * factors[..., None], axis=0)
    return (common_peak, merged_totals, merged_summed.reshape(summed.shape[1:]))


def finish(merged, token_base, token_count):
    totals = merged[1]
    query_count, rows_here, head_count = totals.shape
    attended = merged[2].reshape(query_count, rows_here, head_count, -1) / totals[..., None]
    valid = (token_base + jnp.arange(query_count, dtype=jnp.int32))[:, None] < token_count[None, :]
    attended = jnp.where(valid[:, :, None, None], attended, 0.0)
    return attended.reshape(query_count, rows_here, -1).astype(jnp.bfloat16)


def on_device(
    queries, new_keys, new_values, cache_keys, cache_values, out_proj, skip_blocks, cache_len
):
    local_tokens = queries.shape[0]
    cache_slots = cache_keys.shape[1]
    position = lax.axis_index("ctx")
    token_count = skip_blocks * BLOCK
    first_slot = cache_len - token_count
    token_base = position * local_tokens
    slot_base = position * cache_slots
    all_queries, all_keys, all_values = (
        lax.all_gather(queries, "ctx", axis=0, tiled=True),
        lax.all_gather(new_keys, "ctx", axis=0, tiled=True),
        lax.all_gather(new_values, "ctx", axis=0, tiled=True),
    )
    local_peaks, local_totals, local_summed = cache_part(
        all_queries, cache_keys, cache_values, first_slot, slot_base
    )
    got_peaks, got_totals, got_summed = (
        lax.all_to_all(local_peaks[None], "ctx", split_axis=1, concat_axis=0, tiled=True),
        lax.all_to_all(local_totals[None], "ctx", split_axis=1, concat_axis=0, tiled=True),
        lax.all_to_all(local_summed[None], "ctx", split_axis=1, concat_axis=0, tiled=True),
    )
    merged = fold_sources(got_peaks, got_totals, got_summed)
    merged = merge_parts(merged, new_part(queries, token_base, all_keys, all_values))
    attended = finish(merged, token_base, token_count)
    all_attended = lax.all_gather(attended, "ctx", axis=0, tiled=True)
    column_block = lax.all_gather(out_proj, "row", axis=1, tiled=True)
    rows_total = all_attended.shape[1]
    row_count = lax.axis_size("tp") * (all_attended.shape[0] // lax.axis_size("tp"))
    product = jnp.dot(
        all_attended.reshape(row_count * rows_total, -1),
        column_block,
        preferred_element_type=jnp.float32,
    )
    return lax.psum_scatter(
        product.reshape(row_count, rows_total, -1), "tp", scatter_dimension=0, tiled=True
    )


def solution(mesh):
    placed = (
        P("ctx", "row", "tp"),
        P("ctx", "row", "tp"),
        P("ctx", "row", "tp"),
        P("row", "ctx", "tp"),
        P("row", "ctx", "tp"),
        P("tp", ("ctx", "row")),
        P("row"),
        P("row"),
    )
    return jax.shard_map(
        on_device, mesh=mesh, in_specs=placed, out_specs=P("tp", "row", "ctx"), check_vma=False
    )
```

profile of v0, /device:TPU:2, one launch (start us, length us, event | category | flops | bytes accessed | tf_op | source)
XLA Modules:
  0.0 674.2 jit_solution(4015562140230732718)
XLA Ops:
  9.9 1.9 fusion.89
  15.0 98.7 %all-gather.4.cloned.1.call-done = bf16[512,2,2048]{2,1,0:T(2,128)(2,1)} async-done(((bf16[32,2,2048]{2,1,0:T(2,128)(2,1)}), bf16[512,2,2048]{2,1,0:T(2,128)(2,1)}) %all-gather.4.cloned.1.call-update) | async-done | bytes 4194320 | tf_op jit(solution)/shard_map/all_gather | solution.py:126
  113.8 22.5 %slice_reduce_fusion.3 = (bf16[512,1024]{1,0:T(8,128)(2,1)}, bf16[512,1024]{1,0:T(8,128)(2,1)}, bf16[512,1024]{1,0:T(8,128)(2,1)S(1)}, bf16[512,1024]{1,0:T(8,128)(2,1)S(1)}) fusion(bf16[512,2,2048]{2,1,0:T(2,128)(2,1)} %all-gather.4.cloned.1.call-done), kind=kLoop, calls=%fused_computation.31 | loop fusion | bytes 8388608 | tf_op jit(solution)/shard_map/slice | solution.py:40
  138.3 2.7 fusion.107
  141.0 2.7 fusion.108
  144.7 5.7 fusion.8
  150.5 2.4 fusion.12
  153.0 2.5 fusion.14
  156.6 3.6 fusion.109
  160.2 2.7 fusion.110
  164.6 5.1 fusion.4
  169.8 2.4 fusion.16
  172.3 2.5 fusion.18
  177.5 4.1 all-to-all-start.2
  186.6 2.9 reshape.281
  191.0 2.9 reshape.279
  193.9 4.1 pad_maximum_fusion.1
  198.0 2.5 pad_maximum_fusion
  201.9 6.4 stack.55
  208.2 3.9 stack.54
  212.1 9.6 %all-to-all-start.1 = ((f32[16,1,1024]{2,1,0:T(1,128)}), f32[16,1,1024]{2,1,0:T(1,128)S(1)}, u32[]{:S(2)}, u32[]{:S(2)}) async-start(f32[16,1,1024]{2,1,0:T(1,128)} %reshape.312), calls=%async_computation.1 | async-start | bytes 131072 | tf_op jit(solution)/shard_map/all_to_all | solution.py:134
  221.8 9.9 %maximum_bitcast_fusion = f32[1,512,2,2048]{3,2,0,1:T(2,128)} fusion(f32[512,1,2048]{2,1,0:T(1,128)} %stack.55, f32[512,1,2048]{2,1,0:T(1,128)} %stack.54), kind=kLoop, calls=%fused_computation | loop fusion | flops 2097152 | bytes 16777216 | tf_op jit(solution)/shard_map/broadcast_in_dim | solution.py:136
  231.8 9.7 %all-to-all-start = ((f32[1,512,2,2048]{3,2,0,1:T(2,128)}), f32[1,512,2,2048]{3,2,0,1:T(2,128)}, u32[]{:S(2)}, u32[]{:S(2)}) async-start(f32[1,512,2,2048]{3,2,0,1:T(2,128)} %maximum_bitcast_fusion), calls=%async_computation | async-start | bytes 16777216 | tf_op jit(solution)/shard_map/all_to_all | solution.py:136
  243.8 214.1 %all_gather.16 = bf16[512,2,256]{2,0,1:T(8,128)(2,1)S(1)} all-gather(bf16[32,2,256]{2,0,1:T(8,128)(2,1)S(1)} %copy.49), channel_id=1, replica_groups=mesh['ctx'=16,'tp'=4,'row'=4] {'ctx'}, dimensions={0}, use_global_device_ids=true | all-gather | bytes 557056 | tf_op jit(solution)/shard_map/all_gather | solution.py:127
  459.3 38.5 %all_gather.17 = bf16[512,2,256]{2,0,1:T(8,128)(2,1)S(1)} all-gather(bf16[32,2,256]{2,0,1:T(8,128)(2,1)S(1)} %copy.58), channel_id=1, replica_groups=mesh['ctx'=16,'tp'=4,'row'=4] {'ctx'}, dimensions={0}, use_global_device_ids=true | all-gather | bytes 557056 | tf_op jit(solution)/shard_map/all_gather | solution.py:128
  506.9 4.6 mul.102
  511.5 10.7 %mul.103 = f32[1,16,32,2,2048]{4,3,2,1,0:T(2,128)} reshape(f32[16,32,2,16,128]{4,3,2,1,0:T(8,128)} %mul.102) | data formatting | bytes 16777216 | tf_op jit(solution)/shard_map/mul | solution.py:102
  522.2 9.8 %multiply_reduce_fusion = f32[32,2,2048]{2,1,0:T(2,128)S(1)} fusion(f32[1,16,32,2,2048]{4,3,2,1,0:T(2,128)} %bitcast.7, f32[1,16,32,2,2048]{4,3,2,1,0:T(2,128)} %mul.103), kind=kLoop, calls=%fused_computation.1 | loop fusion | flops 4063232 | bytes 17301504 | tf_op jit(solution)/shard_map/reduce_sum | solution.py:102
  533.3 96.6 %all-gather.6.cloned.1.call-done = bf16[512,2,2048]{2,0,1:T(8,128)(2,1)} async-done(((bf16[32,2,2048]{2,0,1:T(8,128)(2,1)}), bf16[512,2,2048]{2,0,1:T(8,128)(2,1)}) %all-gather.6.cloned.1.call-update) | async-done | bytes 4194320 | tf_op jit(solution)/shard_map/all_gather | solution.py:141
  629.9 6.5 fusion.20
  636.5 27.7 %reduce-scatter.2.cloned.1.call-done = f32[128,2,512]{2,0,1:T(8,128)} async-done(((f32[512,2,512]{2,0,1:T(8,128)}), f32[128,2,512]{2,0,1:T(8,128)}) %reduce-scatter.2.cloned.1.call-update) | async-done | bytes 524304 | tf_op jit(solution)/shard_map/reduce_scatter | solution.py:150
  664.2 2.2 copy.71
  (159 shorter events, 36.3 us)
Async XLA Ops:
  7.4 106.4 %all-gather.4.cloned.1.call-start = ((), (), s32[]{:S(2)}) async-start(), calls=%async_computation.4 | async-start | bytes 4456448 | tf_op jit(solution)/shard_map/all_gather | solution.py:126
  11.8 129.2 %copy-start.17 = (pred[256]{0:T(512)(128)(4,1)}, pred[256]{0:T(512)(128)(4,1)S(1)}, u32[]{:S(2)}) copy-start(pred[256]{0:T(512)(128)(4,1)S(1)} %get-tuple-element.54) | copy-start | bytes 772
  144.7 5.7 copy-start.3
  144.7 5.7 copy-start.13
  144.7 5.7 copy-start.18
  150.4 2.5 copy-start.1
  153.0 2.5 copy-start.10
  155.5 1.2 copy-start.16
  156.6 3.6 copy-start.12
  164.6 5.1 copy-start.2
  169.8 2.5 copy-start
  172.3 2.5 copy-start.15
  172.3 2.7 copy-start.14
  174.7 10.4 %copy-start.5 = (f32[4096,128]{1,0:T(8,128)S(1)}, f32[4096,128]{1,0:T(8,128)}, u32[]{:S(2)}) copy-start(f32[4096,128]{1,0:T(8,128)} %fusion.12) | copy-start | bytes 6291460
  177.5 34.7 %all-to-all-start.2 = ((f32[16,1,1024]{2,1,0:T(1,128)}), f32[16,1,1024]{2,1,0:T(1,128)S(1)}, u32[]{:S(2)}, u32[]{:S(2)}) async-start(f32[16,1,1024]{2,1,0:T(1,128)} %reshape.314), calls=%async_computation.2 | async-start | bytes 131072 | tf_op jit(solution)/shard_map/all_to_all | solution.py:135
  186.6 2.9 copy-start.6
  191.0 2.9 copy-start.7
  193.9 4.1 copy-start.8
  193.9 4.1 copy-start.9
  201.9 6.4 copy-start.4
  212.1 19.7 %all-to-all-start.1 = ((f32[16,1,1024]{2,1,0:T(1,128)}), f32[16,1,1024]{2,1,0:T(1,128)S(1)}, u32[]{:S(2)}, u32[]{:S(2)}) async-start(f32[16,1,1024]{2,1,0:T(1,128)} %reshape.312), calls=%async_computation.1 | async-start | bytes 131072 | tf_op jit(solution)/shard_map/all_to_all | solution.py:134
  231.7 10.7 %copy-start.11 = (bf16[32,2,2048]{2,1,0:T(2,128)(2,1)S(1)}, bf16[32,2,2048]{2,1,0:T(2,128)(2,1)}, u32[]{:S(2)}) copy-start(bf16[32,2,2048]{2,1,0:T(2,128)(2,1)} %param.8) | copy-start | bytes 786436
  231.7 11.9 %copy-start.19 = (bf16[32,2,256]{2,1,0:T(2,128)(2,1)S(1)}, bf16[32,2,256]{2,1,0:T(2,128)(2,1)}, u32[]{:S(2)}) copy-start(bf16[32,2,256]{2,1,0:T(2,128)(2,1)} %param.9) | copy-start | bytes 98308
  231.7 12.1 %copy-start.20 = (bf16[32,2,256]{2,1,0:T(2,128)(2,1)S(1)}, bf16[32,2,256]{2,1,0:T(2,128)(2,1)}, u32[]{:S(2)}) copy-start(bf16[32,2,256]{2,1,0:T(2,128)(2,1)} %param.10) | copy-start | bytes 98308
  231.8 290.4 %all-to-all-start = ((f32[1,512,2,2048]{3,2,0,1:T(2,128)}), f32[1,512,2,2048]{3,2,0,1:T(2,128)}, u32[]{:S(2)}, u32[]{:S(2)}) async-start(f32[1,512,2,2048]{3,2,0,1:T(2,128)} %maximum_bitcast_fusion), calls=%async_computation | async-start | bytes 16777216 | tf_op jit(solution)/shard_map/all_to_all | solution.py:136
  241.5 291.8 %all-gather.8.cloned.1.call-start = ((), (), s32[]{:S(2)}) async-start(), calls=%async_computation.6 | async-start | bytes 2621440 | tf_op jit(solution)/shard_map/all_gather | solution.py:142
  242.1 387.8 %all-gather.6.cloned.1.call-start = ((), (), s32[]{:S(2)}) async-start(), calls=%async_computation.5 | async-start | bytes 4456448 | tf_op jit(solution)/shard_map/all_gather | solution.py:141
  497.7 3.5 copy-start.21
  533.3 130.9 %reduce-scatter.2.cloned.1.call-start = ((), (), s32[]{:S(2)}) async-start(), calls=%async_computation.7 | async-start | bytes 2621440 | tf_op jit(solution)/shard_map/reduce_scatter | solution.py:150
Sparse Core Ops, SparseCore 0:
  10.8 102.9 all-gather.3
  636.6 27.5 reduce-scatter.1
Sparse Core Ops, SparseCore 1:
  243.8 37.8 all-gather.7
  533.3 96.5 all-gather.5
where the time goes:
time: 685 us; the launch traced here: 674 us
  blocking collectives  253 us (37%)
  waiting for transfers between devices  224 us (33%)
  local copies, waits for them, and re-layouts  82.6 us (12%)
  other arithmetic  44.7 us (7%)
  matrix products  30.3 us (4%)
  starting transfers between devices  23.8 us (3%)
  between operations  15.8 us (2%)
    all_gather x1, blocking collectives, on_device(): lax.all_gather(new_keys, 'ctx', axis=0, tiled=True)  214 us
    all_gather x1, waiting for transfers between devices, on_device(): lax.all_gather(queries, 'ctx', axis=0, tiled=True)  98.7 us
    all_gather x1, waiting for transfers between devices, on_device(): all_attended = lax.all_gather(attended, 'ctx', axis=0, tiled=True)  96.6 us
    all_gather x1, blocking collectives, on_device(): lax.all_gather(new_values, 'ctx', axis=0, tiled=True)  38.5 us
    reduce_scatter x1, waiting for transfers between devices, on_device(): lax.psum_scatter(product.reshape(row_count, rows_total, -1), 'tp', scatte...  27.7 us
    slice x2, local copies, waits for them, and re-layouts, attend_rows(): query_rows[:, row_index, kv_index * group_width:(kv_index + 1) * group_wi...  23.6 us
    mul x2, local copies, waits for them, and re-layouts, fold_sources(): summed.reshape(split_shape) * factors[..., None]  15.3 us
  transfers between devices with their start and end apart: 7, of which 4 were waited for; matrix products, arithmetic and copies ran while one was open for 13% of the time, Pallas kernels for 0%

commit v1 on v0

v1 whole, which is shorter than its diff:
```python
import jax
import jax.numpy as jnp
from jax import lax
from jax.experimental import pallas as pl
from jax.experimental.pallas import tpu as pltpu
from jax.sharding import Mesh, PartitionSpec as P

DH = 128
BLOCK = 128
SLOTS = 256
PART = 1152
masked_score = -1e30
exp2_scale = DH ** -0.5 * 1.4426950408889634

VMEM = pl.BlockSpec(memory_space=pltpu.VMEM)
SMEM = pl.BlockSpec(memory_space=pltpu.SMEM)
PARAMS = pltpu.CompilerParams(vmem_limit_bytes=48 * 1024 * 1024)


def columns_of(index):
    return pl.ds(pl.multiple_of(index * DH, DH), DH)


def pack_kernel(place, cache_keys, cache_values, new_keys, new_values, own, other):
    high = place[0]
    for target, head in ((own, high), (other, 1 - high)):
        columns = columns_of(head)
        for row in range(2):
            target[SLOTS * row : SLOTS * (row + 1)] = cache_keys[row, :, columns]
            target[512 + SLOTS * row : 512 + SLOTS * (row + 1)] = cache_values[row, :, columns]
        target[1024:1088] = new_keys[:, columns]
        target[1088:1152] = new_values[:, columns]


def pack(place, cache_keys, cache_values, new_keys, new_values):
    shape = jax.ShapeDtypeStruct((PART, DH), jnp.bfloat16)
    return pl.pallas_call(
        pack_kernel,
        out_shape=(shape, shape),
        in_specs=[SMEM] + [VMEM] * 4,
        out_specs=(VMEM, VMEM),
        compiler_params=PARAMS,
    )(place, cache_keys, cache_values, new_keys, new_values)


def attend_kernel(offsets, place, queries, *refs):
    parts = refs[: len(offsets)]
    out, flat_keys, flat_values, sorted_queries, new_keys, new_values, scores = refs[len(offsets) :]
    high, ring = place[0], place[1]
    sources = []
    for distance, is_own in offsets:
        source_ring = lax.rem(ring + distance, 8)
        sources.append((high if is_own else 1 - high) * 8 + source_ring)
    for part, source in zip(parts, sources):
        where = pl.ds(pl.multiple_of(source * 64, 64), 64)
        flat_keys[where] = part[1024:1088]
        flat_values[where] = part[1088:1152]
    target = lax.broadcasted_iota(jnp.int32, (256, 256), 0)
    origin = lax.broadcasted_iota(jnp.int32, (256, 256), 1)
    wanted = jnp.where(target < 128, 2 * target, 2 * target - 255)
    permute = (origin == wanted).astype(jnp.float32).astype(jnp.bfloat16)
    for block in range(4):
        for flat, split in ((queries, sorted_queries), (flat_keys, new_keys), (flat_values, new_values)):
            moved = jnp.dot(
                permute, flat[256 * block : 256 * (block + 1)], preferred_element_type=jnp.float32
            ).astype(jnp.bfloat16)
            split[0, 128 * block : 128 * (block + 1)] = moved[:128]
            split[1, 128 * block : 128 * (block + 1)] = moved[128:]
    out[...] = jnp.zeros_like(out)
    larger = (place[3] > place[2]).astype(jnp.int32)

    def score(query, key):
        return lax.dot_general(
            query, key, (((1,), (1,)), ((), ())), preferred_element_type=jnp.float32
        )

    for row in range(2):
        count, first = place[2 + row], place[4 + row]

        def unit(block, carry):
            query = sorted_queries[row, pl.ds(pl.multiple_of(block * 128, 128), 128), :]
            lane = lax.broadcasted_iota(jnp.int32, (128, 256), 1)
            peak = jnp.full((128, 128), masked_score, jnp.float32)
            for index, (part, source) in enumerate(zip(parts, sources)):
                found = score(query, part[SLOTS * row : SLOTS * (row + 1)])
                found = jnp.where(lane < first - source * SLOTS, found, masked_score)
                scores[:, SLOTS * index : SLOTS * (index + 1)] = found
                peak = jnp.maximum(peak, jnp.maximum(found[:, :128], found[:, 128:]))
            base = SLOTS * len(parts)
            token = lax.broadcasted_iota(jnp.int32, (128, 128), 0) + block * 128
            fresh = lax.broadcasted_iota(jnp.int32, (128, 128), 1)
            for index in range(4):
                found = score(query, new_keys[row, 128 * index : 128 * (index + 1)])
                found = jnp.where(fresh + 128 * index <= token, found, masked_score)
                scores[:, base + 128 * index : base + 128 * (index + 1)] = found
                peak = jnp.maximum(peak, found)
            top = jnp.max(peak, axis=1, keepdims=True)
            total = jnp.zeros((128, 128), jnp.float32)
            mixed = jnp.zeros((128, DH), jnp.float32)
            for index, part in enumerate(parts):
                weight = jnp.exp2(
                    (scores[:, SLOTS * index : SLOTS * (index + 1)] - top) * exp2_scale
                )
                total = total + (weight[:, :128] + weight[:, 128:])
                mixed = mixed + jnp.dot(
                    weight.astype(jnp.bfloat16),
                    part[512 + SLOTS * row : 512 + SLOTS * (row + 1)],
                    preferred_element_type=jnp.float32,
                )
            for index in range(4):
                weight = jnp.exp2(
                    (scores[:, base + 128 * index : base + 128 * (index + 1)] - top) * exp2_scale
                )
                total = total + weight
                mixed = mixed + jnp.dot(
                    weight.astype(jnp.bfloat16),
                    new_values[row, 128 * index : 128 * (index + 1)],
                    preferred_element_type=jnp.float32,
                )
            result = (mixed / jnp.sum(total, axis=1, keepdims=True)).astype(jnp.bfloat16)
            slot = jnp.where(block < 2, block * 3 + row, block * 3 - 4)
            out[pl.ds(pl.multiple_of(slot * 128, 128), 128), :] = result
            return carry

        lax.fori_loop(0, jnp.where(larger == row, count, jnp.minimum(count, 2)), unit, 0)


def attend(place, queries, parts, offsets):
    keys = SLOTS * len(parts) + 512
    return pl.pallas_call(
        lambda *refs: attend_kernel(offsets, *refs),
        out_shape=jax.ShapeDtypeStruct((768, DH), jnp.bfloat16),
        in_specs=[SMEM] + [VMEM] * (1 + len(parts)),
        out_specs=VMEM,
        scratch_shapes=[
            pltpu.VMEM((1024, DH), jnp.bfloat16),
            pltpu.VMEM((1024, DH), jnp.bfloat16),
            pltpu.VMEM((2, 512, DH), jnp.bfloat16),
            pltpu.VMEM((2, 512, DH), jnp.bfloat16),
            pltpu.VMEM((2, 512, DH), jnp.bfloat16),
            pltpu.VMEM((128, keys), jnp.float32),
        ],
        compiler_params=PARAMS,
    )(place, queries, *parts)


def project_kernel(place, *refs):
    attended = refs[:8]
    weights, kept, sent, gathered = refs[8:]
    ring, core = place[1], place[6]
    for distance in range(8):
        gathered[:, columns_of(lax.rem(ring + distance, 8))] = attended[distance][...]
    for target, owner in ((sent, 1 - core), (kept, core)):
        rows = gathered[pl.ds(pl.multiple_of(owner * 384, 128), 384), :]
        for side in range(2):
            for pair in range(2):
                block = jnp.concatenate(
                    [weights[2 * pair, side], weights[2 * pair + 1, side]], axis=1
                )
                target[side, :, 256 * pair : 256 * (pair + 1)] = jnp.dot(
                    rows, block, preferred_element_type=jnp.float32
                ).astype(target.dtype)


def project(place, attended, weights):
    return pl.pallas_call(
        project_kernel,
        out_shape=(
            jax.ShapeDtypeStruct((2, 384, 512), jnp.float32),
            jax.ShapeDtypeStruct((2, 384, 512), jnp.bfloat16),
        ),
        in_specs=[SMEM] + [VMEM] * 9,
        out_specs=(VMEM, VMEM),
        scratch_shapes=[pltpu.VMEM((768, 1024), jnp.bfloat16)],
        compiler_params=PARAMS,
    )(place, *attended, weights)


def add_kernel(place, kept, arrived, out):
    high = place[0]
    for side in range(2):
        owner = high if side == 0 else 1 - high
        total = kept[side] + arrived[side].astype(jnp.float32)
        out[owner * 2] = total[:256].astype(jnp.bfloat16)
        out[owner * 2 + 1, :128] = total[256:].astype(jnp.bfloat16)
        out[owner * 2 + 1, 128:] = jnp.zeros((128, 512), jnp.bfloat16)


def add_cores(place, kept, arrived):
    return pl.pallas_call(
        add_kernel,
        out_shape=jax.ShapeDtypeStruct((4, 256, 512), jnp.bfloat16),
        in_specs=[SMEM, VMEM, VMEM],
        out_specs=VMEM,
        compiler_params=PARAMS,
    )(place, kept, arrived)


def final_kernel(place, arrived, out):
    low = place[7]
    total = arrived[0].astype(jnp.float32)
    for source in range(1, 4):
        total = total + arrived[source].astype(jnp.float32)
    larger = place[3] > place[2]
    first, second = total[:128], total[128:]
    zero = jnp.zeros_like(first)
    first_row = jnp.where(low == 0, first, jnp.where(larger, zero, first))
    second_row = jnp.where(low == 0, second, jnp.where(larger, first, zero))
    out[:, 0, :] = first_row
    out[:, 1, :] = second_row


def finish(place, arrived):
    return pl.pallas_call(
        final_kernel,
        out_shape=jax.ShapeDtypeStruct((128, 2, 512), jnp.float32),
        in_specs=[SMEM, VMEM],
        out_specs=VMEM,
        compiler_params=PARAMS,
    )(place, arrived)


UP = [(index, (index + 1) % 8) for index in range(8)]
DOWN = [(index, (index + 7) % 8) for index in range(8)]
SWAP = [(0, 1), (1, 0)]


def on_device(
    queries, new_keys, new_values, cache_keys, cache_values, out_proj, skip_blocks, cache_len
):
    high, ring = lax.axis_index("yh"), lax.axis_index("z")
    low, core = lax.axis_index("yl"), lax.axis_index("co")
    first_slot = cache_len - skip_blocks * BLOCK
    place = jnp.concatenate(
        [
            jnp.stack([high, ring]).astype(jnp.int32),
            skip_blocks,
            first_slot,
            jnp.stack([core, low]).astype(jnp.int32),
        ]
    )
    own, other = pack(
        place,
        cache_keys,
        cache_values,
        new_keys.reshape(64, 256),
        new_values.reshape(64, 256),
    )
    partner = lax.ppermute(other, "yh", SWAP)
    split_queries = jnp.transpose(queries.reshape(32, 2, 16, DH), (2, 0, 1, 3)).reshape(16, 64, DH)
    got_queries = lax.all_to_all(
        split_queries, ("yh", "z"), split_axis=0, concat_axis=0, tiled=True
    ).reshape(1024, DH)

    half = lax.dynamic_slice_in_dim(out_proj, (1 - high) * 1024, 1024, 0)
    kept_half = lax.dynamic_slice_in_dim(out_proj, high * 1024, 1024, 0)
    got_half = lax.ppermute(half, "yh", SWAP)
    weights = lax.all_gather(jnp.stack([kept_half, got_half]), "row", axis=0, tiled=False)

    parts, offsets = [own, partner], [(0, True), (0, False)]
    own_up, own_down, partner_up, partner_down = own, own, partner, partner
    for step in range(1, 5):
        own_down = lax.ppermute(own_down, "z", DOWN)
        parts.append(own_down)
        offsets.append((step, True))
        partner_up = lax.ppermute(partner_up, "z", UP)
        parts.append(partner_up)
        offsets.append((8 - step, False))
        if step < 4:
            own_up = lax.ppermute(own_up, "z", UP)
            parts.append(own_up)
            offsets.append((8 - step, True))
            partner_down = lax.ppermute(partner_down, "z", DOWN)
            parts.append(partner_down)
            offsets.append((step, False))
    attended = attend(place, got_queries, parts, offsets)

    gathered = [attended] + [None] * 7
    going_up, going_down = attended, attended
    for step in range(1, 5):
        going_down = lax.ppermute(going_down, "z", DOWN)
        gathered[step] = going_down
        if step < 4:
            going_up = lax.ppermute(going_up, "z", UP)
            gathered[8 - step] = going_up
    kept, sent = project(place, gathered, weights)
    arrived = lax.ppermute(sent, "co", SWAP)
    merged = add_cores(place, kept, arrived)
    shares = lax.all_to_all(merged, ("yh", "yl"), split_axis=0, concat_axis=0, tiled=True)
    return finish(place, shares)


def solution(mesh):
    split = Mesh(mesh.devices.reshape(2, 8, 2, 2, 4), ("yh", "z", "yl", "co", "row"))
    ctx, tp = ("yh", "z"), ("yl", "co")
    placed = (
        P(ctx, "row", tp),
        P(ctx, "row", tp),
        P(ctx, "row", tp),
        P("row", ctx, tp),
        P("row", ctx, tp),
        P(tp, ("yh", "z", "row")),
        P("row"),
        P("row"),
    )
    return jax.shard_map(
        on_device, mesh=split, in_specs=placed, out_specs=P(tp, "row", ctx), check_vma=False
    )
```

time: 685 us -> 157 us (0.23); the launches traced: 674 us -> 157 us
  blocking collectives: 253 us -> 19.8 us
  waiting for transfers between devices: 224 us -> 51.7 us
  local copies, waits for them, and re-layouts: 82.6 us -> 4.95 us
  other arithmetic: 44.7 us -> 0.85 us
  matrix products: 30.3 us -> 0 us
  starting transfers between devices: 23.8 us -> 51.6 us
  Pallas kernels: 0 us -> 14.7 us
    all_gather x2 -> x0, blocking collectives: 253 us -> none  [the longest x1 214 us: on_device(): lax.all_gather(new_keys, 'ctx', axis=0, tiled=True)]
    all_gather x3 -> x1, waiting for transfers between devices: 195 us -> 0.01 us  [on_device(): lax.all_gather(jnp.stack([kept_half, got_half]), 'row', axis=0, tiled=False)]
    ppermute x0 -> x24, waiting for transfers between devices: none -> 45.1 us  [the longest x4 15.7 us: on_device(): going_down = lax.ppermute(going_down, 'z', DOWN)]
    ppermute x0 -> x24, starting transfers between devices: none -> 42.4 us  [the longest x4 14.1 us: on_device(): own_down = lax.ppermute(own_down, 'z', DOWN)]
    dot_general x17 -> x0, matrix products: 30.3 us -> none  [the longest x8 12.9 us: attend_block(): jnp.einsum('qd,kd->qk', flat_rows, key_rows, preferred_element_type=jnp.f...]
    reduce_scatter x1 -> x0, waiting for transfers between devices: 27.7 us -> none  [on_device(): lax.psum_scatter(product.reshape(row_count, rows_total, -1), 'tp', scatte...]
    slice x3 -> x0, local copies, waits for them, and re-layouts: 24.2 us -> none  [the longest x2 23.6 us: attend_rows(): query_rows[:, row_index, kv_index * group_width:(kv_index + 1) * group_wi...]
    reduce_sum x5 -> x0, other arithmetic: 22 us -> none  [the longest x3 11.6 us: attend_block(): totals = jnp.sum(weights, axis=1)]
  transfers between devices with their start and end apart: 7 -> 26, of which waited for: 4 -> 17; matrix products, arithmetic and copies ran while one was open for 13% -> 1% of each run, Pallas kernels for 0% -> 6%
where the time goes in v1:
time: 157 us
  waiting for transfers between devices  51.7 us (33%)
  starting transfers between devices  51.6 us (33%)
  blocking collectives  19.8 us (13%)
  Pallas kernels  14.7 us (9%)
  between operations  13.6 us (9%)
  local copies, waits for them, and re-layouts  4.95 us (3%)
    all_to_all x1, blocking collectives, on_device(): lax.all_to_all(merged, ('yh', 'yl'), split_axis=0, concat_axis=0, tiled=T...  19.8 us
    ppermute x4, waiting for transfers between devices, on_device(): going_down = lax.ppermute(going_down, 'z', DOWN)  15.7 us
    ppermute x4, starting transfers between devices, on_device(): own_down = lax.ppermute(own_down, 'z', DOWN)  14.1 us
    ppermute x4, starting transfers between devices, on_device(): going_down = lax.ppermute(going_down, 'z', DOWN)  12.6 us
    ppermute x4, waiting for transfers between devices, on_device(): partner_up = lax.ppermute(partner_up, 'z', UP)  9.98 us
    all_to_all x1, starting transfers between devices, on_device(): lax.all_to_all(split_queries, ('yh', 'z'), split_axis=0, concat_axis=0, t...  9.14 us
    pallas_call x1, Pallas kernels, attend(): pl.pallas_call(lambda *refs: attend_kernel(offsets, *refs), out_shape=jax...  8.93 us
    ppermute x3, waiting for transfers between devices, on_device(): own_up = lax.ppermute(own_up, 'z', UP)  8.24 us
  transfers between devices with their start and end apart: 26, of which 17 were waited for; matrix products, arithmetic and copies ran while one was open for 1% of the time, Pallas kernels for 6%

profile of v1, /device:TPU:2, one launch (start us, length us, event | category | flops | bytes accessed | tf_op | source)
XLA Modules:
  0.0 157.2 jit_solution(5013763961872555560)
XLA Ops:
  7.8 3.3 %collective-permute-start.22 = (bf16[1024,128]{1,0:T(8,128)(2,1)S(1)}, bf16[1024,128]{1,0:T(8,128)(2,1)S(1)}, u32[]{:S(2)}, u32[]{:S(2)}) collective-permute-start(bf16[1024,128]{1,0:T(8,128)(2,1)S(1)} %get-tuple-element.14), channel_id=1, source_target_pairs={{0,128},{128,0},{1,129},{129,1},{2,130},{130,2},{3,131},{131,3},{4... | collective-permute-start | bytes 786440 | tf_op jit(solution)/shard_map/ppermute | solution.py:257
  11.0 6.4 %collective-permute-done.22 = bf16[1024,128]{1,0:T(8,128)(2,1)S(1)} collective-permute-done((bf16[1024,128]{1,0:T(8,128)(2,1)S(1)}, bf16[1024,128]{1,0:T(8,128)(2,1)S(1)}, u32[]{:S(2)}, u32[]{:S(2)}) %collective-permute-start.22) | collective-permute-done | bytes 262176 | tf_op jit(solution)/shard_map/ppermute | solution.py:257
  19.1 3.3 %collective-permute-start = (bf16[1152,128]{1,0:T(8,128)(2,1)S(1)}, bf16[1152,128]{1,0:T(8,128)(2,1)S(1)}, u32[]{:S(2)}, u32[]{:S(2)}) collective-permute-start(bf16[1152,128]{1,0:T(8,128)(2,1)S(1)} %get-tuple-element.10), channel_id=1, source_target_pairs={{0,128},{128,0},{1,129},{129,1},{2,130},{130,2},{3,131},{131,3},{4... | collective-permute-start | bytes 884744 | tf_op jit(solution)/shard_map/ppermute | solution.py:249
  22.4 5.9 %collective-permute-start.1 = (bf16[1152,128]{1,0:T(8,128)(2,1)S(1)}, bf16[1152,128]{1,0:T(8,128)(2,1)S(1)}, u32[]{:S(2)}, u32[]{:S(2)}) collective-permute-start(bf16[1152,128]{1,0:T(8,128)(2,1)S(1)} %get-tuple-element.9.refs_2_), channel_id=1, source_target_pairs={{0,112},{16,0},{32,16},{48,32},{64,48},{80,64},{96,80},{112,96},{1... | collective-permute-start | bytes 884744 | tf_op jit(solution)/shard_map/ppermute | solution.py:263
  28.6 1.9 %collective-permute-start.2 = (bf16[1152,128]{1,0:T(8,128)(2,1)S(1)}, bf16[1152,128]{1,0:T(8,128)(2,1)S(1)}, u32[]{:S(2)}, u32[]{:S(2)}) collective-permute-start(bf16[1152,128]{1,0:T(8,128)(2,1)S(1)} %collective-permute-done.refs_3_), channel_id=1, source_target_pairs={{0,16},{16,32},{32,48},{48,64},{64,80},{80,96},{96,112},{112,0},{1... | collective-permute-start | bytes 884744 | tf_op jit(solution)/shard_map/ppermute | solution.py:266
  30.5 1.9 %collective-permute-start.3 = (bf16[1152,128]{1,0:T(8,128)(2,1)S(1)}, bf16[1152,128]{1,0:T(8,128)(2,1)S(1)}, u32[]{:S(2)}, u32[]{:S(2)}) collective-permute-start(bf16[1152,128]{1,0:T(8,128)(2,1)S(1)} %get-tuple-element.9.refs_2_), channel_id=1, source_target_pairs={{0,16},{16,32},{32,48},{48,64},{64,80},{80,96},{96,112},{112,0},{1... | collective-permute-start | bytes 884744 | tf_op jit(solution)/shard_map/ppermute | solution.py:270
  33.4 3.7 %collective-permute-start.5 = (bf16[1152,128]{1,0:T(8,128)(2,1)S(1)}, bf16[1152,128]{1,0:T(8,128)(2,1)S(1)}, u32[]{:S(2)}, u32[]{:S(2)}) collective-permute-start(bf16[1152,128]{1,0:T(8,128)(2,1)S(1)} %collective-permute-done.1.refs_4_), channel_id=1, source_target_pairs={{0,112},{16,0},{32,16},{48,32},{64,48},{80,64},{96,80},{112,96},{1... | collective-permute-start | bytes 884744 | tf_op jit(solution)/shard_map/ppermute | solution.py:263
  37.1 5.3 %collective-permute-done.2.refs_5_ = bf16[1152,128]{1,0:T(8,128)(2,1)S(1)} collective-permute-done((bf16[1152,128]{1,0:T(8,128)(2,1)S(1)}, bf16[1152,128]{1,0:T(8,128)(2,1)S(1)}, u32[]{:S(2)}, u32[]{:S(2)}) %collective-permute-start.2) | collective-permute-done | bytes 294944 | tf_op jit(solution)/shard_map/ppermute | solution.py:266
  42.4 6.3 %collective-permute-done.3.refs_6_ = bf16[1152,128]{1,0:T(8,128)(2,1)S(1)} collective-permute-done((bf16[1152,128]{1,0:T(8,128)(2,1)S(1)}, bf16[1152,128]{1,0:T(8,128)(2,1)S(1)}, u32[]{:S(2)}, u32[]{:S(2)}) %collective-permute-start.3) | collective-permute-done | bytes 294944 | tf_op jit(solution)/shard_map/ppermute | solution.py:270
  48.7 3.2 %collective-permute-start.9 = (bf16[1152,128]{1,0:T(8,128)(2,1)S(1)}, bf16[1152,128]{1,0:T(8,128)(2,1)S(1)}, u32[]{:S(2)}, u32[]{:S(2)}) collective-permute-start(bf16[1152,128]{1,0:T(8,128)(2,1)S(1)} %collective-permute-done.5.refs_8_), channel_id=1, source_target_pairs={{0,112},{16,0},{32,16},{48,32},{64,48},{80,64},{96,80},{112,96},{1... | collective-permute-start | bytes 884744 | tf_op jit(solution)/shard_map/ppermute | solution.py:263
  52.7 2.3 %collective-permute-done.6.refs_9_ = bf16[1152,128]{1,0:T(8,128)(2,1)S(1)} collective-permute-done((bf16[1152,128]{1,0:T(8,128)(2,1)S(1)}, bf16[1152,128]{1,0:T(8,128)(2,1)S(1)}, u32[]{:S(2)}, u32[]{:S(2)}) %collective-permute-start.6) | collective-permute-done | bytes 294944 | tf_op jit(solution)/shard_map/ppermute | solution.py:266
  57.1 9.1 %all-to-all-start = ((bf16[16,64,128]{2,1,0:T(8,128)(2,1)}), bf16[16,64,128]{2,1,0:T(8,128)(2,1)S(1)}, u32[]{:S(2)}, u32[]{:S(2)}) async-start(bf16[16,64,128]{2,1,0:T(8,128)(2,1)} %bitcast.13), calls=%async_computation | async-start | bytes 524288 | tf_op jit(solution)/shard_map/all_to_all | solution.py:251
  66.2 2.0 %collective-permute-start.11 = (bf16[1152,128]{1,0:T(8,128)(2,1)S(1)}, bf16[1152,128]{1,0:T(8,128)(2,1)}, u32[]{:S(2)}, u32[]{:S(2)}) collective-permute-start(bf16[1152,128]{1,0:T(8,128)(2,1)S(1)} %collective-permute-done.7.refs_10_), channel_id=1, source_target_pairs={{0,16},{16,32},{32,48},{48,64},{64,80},{80,96},{96,112},{112,0},{1... | collective-permute-start | bytes 884744 | tf_op jit(solution)/shard_map/ppermute | solution.py:270
  68.2 1.3 collective-permute-start.13
  69.6 1.9 %collective-permute-start.12 = (bf16[1152,128]{1,0:T(8,128)(2,1)}, bf16[1152,128]{1,0:T(8,128)(2,1)}, u32[]{:S(2)}, u32[]{:S(2)}) collective-permute-start(bf16[1152,128]{1,0:T(8,128)(2,1)} %collective-permute-done.8.refs_11_), channel_id=1, source_target_pairs={{0,112},{16,0},{32,16},{48,32},{64,48},{80,64},{96,80},{112,96},{1... | collective-permute-start | bytes 884744 | tf_op jit(solution)/shard_map/ppermute | solution.py:273
  71.6 6.6 %all-to-all-done = bf16[16,64,128]{2,1,0:T(8,128)(2,1)S(1)} async-done(((bf16[16,64,128]{2,1,0:T(8,128)(2,1)}), bf16[16,64,128]{2,1,0:T(8,128)(2,1)S(1)}, u32[]{:S(2)}, u32[]{:S(2)}) %all-to-all-start) | async-done | bytes 262176 | tf_op jit(solution)/shard_map/all_to_all | solution.py:251
  78.2 1.9 %collective-permute-done.11.refs_14_ = bf16[1152,128]{1,0:T(8,128)(2,1)} collective-permute-done((bf16[1152,128]{1,0:T(8,128)(2,1)S(1)}, bf16[1152,128]{1,0:T(8,128)(2,1)}, u32[]{:S(2)}, u32[]{:S(2)}) %collective-permute-start.11) | collective-permute-done | bytes 294944 | tf_op jit(solution)/shard_map/ppermute | solution.py:270
  80.9 2.4 %collective-permute-done.14.refs_17_ = bf16[1152,128]{1,0:T(8,128)(2,1)} collective-permute-done((bf16[1152,128]{1,0:T(8,128)(2,1)}, bf16[1152,128]{1,0:T(8,128)(2,1)}, u32[]{:S(2)}, u32[]{:S(2)}) %collective-permute-start.14) | collective-permute-done | bytes 294944 | tf_op jit(solution)/shard_map/ppermute | solution.py:266
  83.3 8.9 %shard_map.83.refs_0_ = bf16[768,128]{1,0:T(8,128)(2,1)S(1)} custom-call(s32[8]{0:T(128)S(1)} %concatenate.3.place.refs_0_, bf16[1024,128]{1,0:T(8,128)(2,1)S(1)} %bitcast.12, bf16[1152,128]{1,0:T(8,128)(2,1)S(1)} %get-tuple-element.9.refs_2_, bf16[1152,128]{1,0:T(8,128)(2,1)S(1)} %collective-permute-done.refs_3_, ...), custom_call_target="tpu_custom_call" | custom-call | tf_op jit(solution)/shard_map/pallas_call | solution.py:130
  92.2 1.8 %collective-permute-start.15 = (bf16[768,128]{1,0:T(8,128)(2,1)S(1)}, bf16[768,128]{1,0:T(8,128)(2,1)S(1)}, u32[]{:S(2)}, u32[]{:S(2)}) collective-permute-start(bf16[768,128]{1,0:T(8,128)(2,1)S(1)} %shard_map.83.refs_0_), channel_id=1, source_target_pairs={{0,112},{16,0},{32,16},{48,32},{64,48},{80,64},{96,80},{112,96},{1... | collective-permute-start | bytes 589832 | tf_op jit(solution)/shard_map/ppermute | solution.py:281
  94.3 4.9 %collective-permute-done.15.refs_1_ = bf16[768,128]{1,0:T(8,128)(2,1)S(1)} collective-permute-done((bf16[768,128]{1,0:T(8,128)(2,1)S(1)}, bf16[768,128]{1,0:T(8,128)(2,1)S(1)}, u32[]{:S(2)}, u32[]{:S(2)}) %collective-permute-start.15) | collective-permute-done | bytes 196640 | tf_op jit(solution)/shard_map/ppermute | solution.py:281
  99.3 3.4 %collective-permute-start.16 = (bf16[768,128]{1,0:T(8,128)(2,1)S(1)}, bf16[768,128]{1,0:T(8,128)(2,1)S(1)}, u32[]{:S(2)}, u32[]{:S(2)}) collective-permute-start(bf16[768,128]{1,0:T(8,128)(2,1)S(1)} %collective-permute-done.15.refs_1_), channel_id=1, source_target_pairs={{0,112},{16,0},{32,16},{48,32},{64,48},{80,64},{96,80},{112,96},{1... | collective-permute-start | bytes 589832 | tf_op jit(solution)/shard_map/ppermute | solution.py:281
  103.0 4.2 %collective-permute-done.16.refs_2_ = bf16[768,128]{1,0:T(8,128)(2,1)S(1)} collective-permute-done((bf16[768,128]{1,0:T(8,128)(2,1)S(1)}, bf16[768,128]{1,0:T(8,128)(2,1)S(1)}, u32[]{:S(2)}, u32[]{:S(2)}) %collective-permute-start.16) | collective-permute-done | bytes 196640 | tf_op jit(solution)/shard_map/ppermute | solution.py:281
  107.2 3.7 %collective-permute-start.17 = (bf16[768,128]{1,0:T(8,128)(2,1)S(1)}, bf16[768,128]{1,0:T(8,128)(2,1)S(1)}, u32[]{:S(2)}, u32[]{:S(2)}) collective-permute-start(bf16[768,128]{1,0:T(8,128)(2,1)S(1)} %collective-permute-done.16.refs_2_), channel_id=1, source_target_pairs={{0,112},{16,0},{32,16},{48,32},{64,48},{80,64},{96,80},{112,96},{1... | collective-permute-start | bytes 589832 | tf_op jit(solution)/shard_map/ppermute | solution.py:281
  111.1 3.4 %collective-permute-done.17.refs_3_ = bf16[768,128]{1,0:T(8,128)(2,1)S(1)} collective-permute-done((bf16[768,128]{1,0:T(8,128)(2,1)S(1)}, bf16[768,128]{1,0:T(8,128)(2,1)S(1)}, u32[]{:S(2)}, u32[]{:S(2)}) %collective-permute-start.17) | collective-permute-done | bytes 196640 | tf_op jit(solution)/shard_map/ppermute | solution.py:281
  114.5 3.7 %collective-permute-start.18 = (bf16[768,128]{1,0:T(8,128)(2,1)S(1)}, bf16[768,128]{1,0:T(8,128)(2,1)S(1)}, u32[]{:S(2)}, u32[]{:S(2)}) collective-permute-start(bf16[768,128]{1,0:T(8,128)(2,1)S(1)} %collective-permute-done.17.refs_3_), channel_id=1, source_target_pairs={{0,112},{16,0},{32,16},{48,32},{64,48},{80,64},{96,80},{112,96},{1... | collective-permute-start | bytes 589832 | tf_op jit(solution)/shard_map/ppermute | solution.py:281
  118.2 3.2 %collective-permute-done.18.refs_4_ = bf16[768,128]{1,0:T(8,128)(2,1)S(1)} collective-permute-done((bf16[768,128]{1,0:T(8,128)(2,1)S(1)}, bf16[768,128]{1,0:T(8,128)(2,1)S(1)}, u32[]{:S(2)}, u32[]{:S(2)}) %collective-permute-start.18) | collective-permute-done | bytes 196640 | tf_op jit(solution)/shard_map/ppermute | solution.py:281
  121.4 1.6 %copy-done = bf16[8,1024,128]{2,1,0:T(8,128)(2,1)S(1)} copy-done((bf16[8,1024,128]{2,1,0:T(8,128)(2,1)S(1)}, bf16[8,1024,128]{2,1,0:T(8,128)(2,1)}, u32[]{:S(2)}) %copy-start) | copy-done | bytes 2097176
  123.0 2.8 %shard_map.84 = (f32[2,384,512]{2,1,0:T(8,128)S(1)}, bf16[2,384,512]{2,1,0:T(8,128)(2,1)S(1)}) custom-call(s32[8]{0:T(128)S(1)} %concatenate.3.place.refs_0_, bf16[768,128]{1,0:T(8,128)(2,1)S(1)} %shard_map.83.refs_0_, bf16[768,128]{1,0:T(8,128)(2,1)S(1)} %collective-permute-done.15.refs_1_, bf16[768,128]{1,0:T(8,128)(2,1)S(1)} %collective-permute-done.16.refs_2_, ...), custom_call_target="tpu_custom_call" | custom-call | tf_op jit(solution)/shard_map/pallas_call | solution.py:166
  125.9 2.3 %collective-permute-done.23.arrived = bf16[2,384,512]{2,1,0:T(8,128)(2,1)S(1)} collective-permute-done((bf16[2,384,512]{2,1,0:T(8,128)(2,1)S(1)}, bf16[2,384,512]{2,1,0:T(8,128)(2,1)S(1)}, u32[]{:S(2)}, u32[]{:S(2)}) %collective-permute-start.23) | collective-permute-done | bytes 786464 | tf_op jit(solution)/shard_map/ppermute | solution.py:287
  128.9 19.8 %all_to_all.10.arrived = bf16[4,256,512]{2,1,0:T(8,128)(2,1)S(1)} all-to-all(bf16[4,256,512]{2,1,0:T(8,128)(2,1)S(1)} %shard_map.85), channel_id=1, replica_groups=mesh['yh'=2,'z'=8,'yl'=2,'co'=2,'row'=4] {'yh','yl'}, dimensions={0} | all-to-all | bytes 2097152 | tf_op jit(solution)/shard_map/all_to_all | solution.py:289
  148.7 1.6 %shard_map.86 = f32[128,2,512]{2,1,0:T(2,128)} custom-call(s32[8]{0:T(128)S(1)} %concatenate.3.place.refs_0_, bf16[4,256,512]{2,1,0:T(8,128)(2,1)S(1)} %all_to_all.10.arrived), custom_call_target="tpu_custom_call" | custom-call | tf_op jit(solution)/shard_map/pallas_call | solution.py:214
  (49 shorter events, 9.5 us)
Async XLA Ops:
  6.5 11.7 %copy-start.3 = (bf16[32,2,256]{2,1,0:T(2,128)(2,1)S(1)}, bf16[32,2,256]{2,1,0:T(2,128)(2,1)}, u32[]{:S(2)}) copy-start(bf16[32,2,256]{2,1,0:T(2,128)(2,1)} %param.9) | copy-start | bytes 98308
  6.5 11.8 %copy-start.4 = (bf16[32,2,256]{2,1,0:T(2,128)(2,1)S(1)}, bf16[32,2,256]{2,1,0:T(2,128)(2,1)}, u32[]{:S(2)}) copy-start(bf16[32,2,256]{2,1,0:T(2,128)(2,1)} %param.10) | copy-start | bytes 98308
  6.5 11.8 %copy-start.5 = (s32[2]{0:T(128)S(1)}, s32[2]{0:T(128)}, u32[]{:S(2)}) copy-start(s32[2]{0:T(128)} %param.14) | copy-start | bytes 28
  6.5 11.8 %copy-start.6 = (s32[2]{0:T(128)S(1)}, s32[2]{0:T(128)}, u32[]{:S(2)}) copy-start(s32[2]{0:T(128)} %param.15) | copy-start | bytes 28
  6.5 11.9 %copy-start.1 = (bf16[2,256,256]{2,1,0:T(8,128)(2,1)S(1)}, bf16[2,256,256]{2,1,0:T(8,128)(2,1)}, u32[]{:S(2)}) copy-start(bf16[2,256,256]{2,1,0:T(8,128)(2,1)} %cache_keys.1) | copy-start | bytes 786436
  6.5 11.9 %copy-start.2 = (bf16[2,256,256]{2,1,0:T(8,128)(2,1)S(1)}, bf16[2,256,256]{2,1,0:T(8,128)(2,1)}, u32[]{:S(2)}) copy-start(bf16[2,256,256]{2,1,0:T(8,128)(2,1)} %cache_values.1) | copy-start | bytes 786436
  6.6 114.8 %all-gather.3.cloned.1.call-start = ((), (), s32[]{:S(2)}) async-start(), calls=%async_computation.2 | async-start | bytes 2621440 | tf_op jit(solution)/shard_map/all_gather | solution.py:258
  7.8 9.6 %collective-permute-start.22 = (bf16[1024,128]{1,0:T(8,128)(2,1)S(1)}, bf16[1024,128]{1,0:T(8,128)(2,1)S(1)}, u32[]{:S(2)}, u32[]{:S(2)}) collective-permute-start(bf16[1024,128]{1,0:T(8,128)(2,1)S(1)} %get-tuple-element.14), channel_id=1, source_target_pairs={{0,128},{128,0},{1,129},{129,1},{2,130},{130,2},{3,131},{131,3},{4... | collective-permute-start | bytes 786440 | tf_op jit(solution)/shard_map/ppermute | solution.py:257
  19.1 9.5 %collective-permute-start = (bf16[1152,128]{1,0:T(8,128)(2,1)S(1)}, bf16[1152,128]{1,0:T(8,128)(2,1)S(1)}, u32[]{:S(2)}, u32[]{:S(2)}) collective-permute-start(bf16[1152,128]{1,0:T(8,128)(2,1)S(1)} %get-tuple-element.10), channel_id=1, source_target_pairs={{0,128},{128,0},{1,129},{129,1},{2,130},{130,2},{3,131},{131,3},{4... | collective-permute-start | bytes 884744 | tf_op jit(solution)/shard_map/ppermute | solution.py:249
  22.4 11.0 %collective-permute-start.1 = (bf16[1152,128]{1,0:T(8,128)(2,1)S(1)}, bf16[1152,128]{1,0:T(8,128)(2,1)S(1)}, u32[]{:S(2)}, u32[]{:S(2)}) collective-permute-start(bf16[1152,128]{1,0:T(8,128)(2,1)S(1)} %get-tuple-element.9.refs_2_), channel_id=1, source_target_pairs={{0,112},{16,0},{32,16},{48,32},{64,48},{80,64},{96,80},{112,96},{1... | collective-permute-start | bytes 884744 | tf_op jit(solution)/shard_map/ppermute | solution.py:263
  28.6 13.8 %collective-permute-start.2 = (bf16[1152,128]{1,0:T(8,128)(2,1)S(1)}, bf16[1152,128]{1,0:T(8,128)(2,1)S(1)}, u32[]{:S(2)}, u32[]{:S(2)}) collective-permute-start(bf16[1152,128]{1,0:T(8,128)(2,1)S(1)} %collective-permute-done.refs_3_), channel_id=1, source_target_pairs={{0,16},{16,32},{32,48},{48,64},{64,80},{80,96},{96,112},{112,0},{1... | collective-permute-start | bytes 884744 | tf_op jit(solution)/shard_map/ppermute | solution.py:266
  30.5 18.2 %collective-permute-start.3 = (bf16[1152,128]{1,0:T(8,128)(2,1)S(1)}, bf16[1152,128]{1,0:T(8,128)(2,1)S(1)}, u32[]{:S(2)}, u32[]{:S(2)}) collective-permute-start(bf16[1152,128]{1,0:T(8,128)(2,1)S(1)} %get-tuple-element.9.refs_2_), channel_id=1, source_target_pairs={{0,16},{16,32},{32,48},{48,64},{64,80},{80,96},{96,112},{112,0},{1... | collective-permute-start | bytes 884744 | tf_op jit(solution)/shard_map/ppermute | solution.py:270
  33.4 15.3 %collective-permute-start.5 = (bf16[1152,128]{1,0:T(8,128)(2,1)S(1)}, bf16[1152,128]{1,0:T(8,128)(2,1)S(1)}, u32[]{:S(2)}, u32[]{:S(2)}) collective-permute-start(bf16[1152,128]{1,0:T(8,128)(2,1)S(1)} %collective-permute-done.1.refs_4_), channel_id=1, source_target_pairs={{0,112},{16,0},{32,16},{48,32},{64,48},{80,64},{96,80},{112,96},{1... | collective-permute-start | bytes 884744 | tf_op jit(solution)/shard_map/ppermute | solution.py:263
  37.1 14.9 %collective-permute-start.4 = (bf16[1152,128]{1,0:T(8,128)(2,1)S(1)}, bf16[1152,128]{1,0:T(8,128)(2,1)S(1)}, u32[]{:S(2)}, u32[]{:S(2)}) collective-permute-start(bf16[1152,128]{1,0:T(8,128)(2,1)S(1)} %collective-permute-done.refs_3_), channel_id=1, source_target_pairs={{0,112},{16,0},{32,16},{48,32},{64,48},{80,64},{96,80},{112,96},{1... | collective-permute-start | bytes 884744 | tf_op jit(solution)/shard_map/ppermute | solution.py:273
  42.4 12.6 %collective-permute-start.6 = (bf16[1152,128]{1,0:T(8,128)(2,1)S(1)}, bf16[1152,128]{1,0:T(8,128)(2,1)S(1)}, u32[]{:S(2)}, u32[]{:S(2)}) collective-permute-start(bf16[1152,128]{1,0:T(8,128)(2,1)S(1)} %collective-permute-done.2.refs_5_), channel_id=1, source_target_pairs={{0,16},{16,32},{32,48},{48,64},{64,80},{80,96},{96,112},{112,0},{1... | collective-permute-start | bytes 884744 | tf_op jit(solution)/shard_map/ppermute | solution.py:266
  48.7 17.5 %collective-permute-start.7 = (bf16[1152,128]{1,0:T(8,128)(2,1)S(1)}, bf16[1152,128]{1,0:T(8,128)(2,1)S(1)}, u32[]{:S(2)}, u32[]{:S(2)}) collective-permute-start(bf16[1152,128]{1,0:T(8,128)(2,1)S(1)} %collective-permute-done.3.refs_6_), channel_id=1, source_target_pairs={{0,16},{16,32},{32,48},{48,64},{64,80},{80,96},{96,112},{112,0},{1... | collective-permute-start | bytes 884744 | tf_op jit(solution)/shard_map/ppermute | solution.py:270
  48.7 19.5 %collective-permute-start.9 = (bf16[1152,128]{1,0:T(8,128)(2,1)S(1)}, bf16[1152,128]{1,0:T(8,128)(2,1)S(1)}, u32[]{:S(2)}, u32[]{:S(2)}) collective-permute-start(bf16[1152,128]{1,0:T(8,128)(2,1)S(1)} %collective-permute-done.5.refs_8_), channel_id=1, source_target_pairs={{0,112},{16,0},{32,16},{48,32},{64,48},{80,64},{96,80},{112,96},{1... | collective-permute-start | bytes 884744 | tf_op jit(solution)/shard_map/ppermute | solution.py:263
  51.9 17.6 %collective-permute-start.8 = (bf16[1152,128]{1,0:T(8,128)(2,1)S(1)}, bf16[1152,128]{1,0:T(8,128)(2,1)}, u32[]{:S(2)}, u32[]{:S(2)}) collective-permute-start(bf16[1152,128]{1,0:T(8,128)(2,1)S(1)} %collective-permute-done.4.refs_7_), channel_id=1, source_target_pairs={{0,112},{16,0},{32,16},{48,32},{64,48},{80,64},{96,80},{112,96},{1... | collective-permute-start | bytes 884744 | tf_op jit(solution)/shard_map/ppermute | solution.py:273
  55.0 16.5 %collective-permute-start.10 = (bf16[1152,128]{1,0:T(8,128)(2,1)S(1)}, bf16[1152,128]{1,0:T(8,128)(2,1)}, u32[]{:S(2)}, u32[]{:S(2)}) collective-permute-start(bf16[1152,128]{1,0:T(8,128)(2,1)S(1)} %collective-permute-done.6.refs_9_), channel_id=1, source_target_pairs={{0,16},{16,32},{32,48},{48,64},{64,80},{80,96},{96,112},{112,0},{1... | collective-permute-start | bytes 884744 | tf_op jit(solution)/shard_map/ppermute | solution.py:266
  57.1 21.1 %all-to-all-start = ((bf16[16,64,128]{2,1,0:T(8,128)(2,1)}), bf16[16,64,128]{2,1,0:T(8,128)(2,1)S(1)}, u32[]{:S(2)}, u32[]{:S(2)}) async-start(bf16[16,64,128]{2,1,0:T(8,128)(2,1)} %bitcast.13), calls=%async_computation | async-start | bytes 524288 | tf_op jit(solution)/shard_map/all_to_all | solution.py:251
  66.2 13.9 %collective-permute-start.11 = (bf16[1152,128]{1,0:T(8,128)(2,1)S(1)}, bf16[1152,128]{1,0:T(8,128)(2,1)}, u32[]{:S(2)}, u32[]{:S(2)}) collective-permute-start(bf16[1152,128]{1,0:T(8,128)(2,1)S(1)} %collective-permute-done.7.refs_10_), channel_id=1, source_target_pairs={{0,16},{16,32},{32,48},{48,64},{64,80},{80,96},{96,112},{112,0},{1... | collective-permute-start | bytes 884744 | tf_op jit(solution)/shard_map/ppermute | solution.py:270
  68.2 11.9 %collective-permute-start.13 = (bf16[1152,128]{1,0:T(8,128)(2,1)S(1)}, bf16[1152,128]{1,0:T(8,128)(2,1)}, u32[]{:S(2)}, u32[]{:S(2)}) collective-permute-start(bf16[1152,128]{1,0:T(8,128)(2,1)S(1)} %collective-permute-done.9.refs_12_), channel_id=1, source_target_pairs={{0,112},{16,0},{32,16},{48,32},{64,48},{80,64},{96,80},{112,96},{1... | collective-permute-start | bytes 884744 | tf_op jit(solution)/shard_map/ppermute | solution.py:263
  69.6 11.3 %collective-permute-start.12 = (bf16[1152,128]{1,0:T(8,128)(2,1)}, bf16[1152,128]{1,0:T(8,128)(2,1)}, u32[]{:S(2)}, u32[]{:S(2)}) collective-permute-start(bf16[1152,128]{1,0:T(8,128)(2,1)} %collective-permute-done.8.refs_11_), channel_id=1, source_target_pairs={{0,112},{16,0},{32,16},{48,32},{64,48},{80,64},{96,80},{112,96},{1... | collective-permute-start | bytes 884744 | tf_op jit(solution)/shard_map/ppermute | solution.py:273
  71.5 11.8 %collective-permute-start.14 = (bf16[1152,128]{1,0:T(8,128)(2,1)}, bf16[1152,128]{1,0:T(8,128)(2,1)}, u32[]{:S(2)}, u32[]{:S(2)}) collective-permute-start(bf16[1152,128]{1,0:T(8,128)(2,1)} %collective-permute-done.10.refs_13_), channel_id=1, source_target_pairs={{0,16},{16,32},{32,48},{48,64},{64,80},{80,96},{96,112},{112,0},{1... | collective-permute-start | bytes 884744 | tf_op jit(solution)/shard_map/ppermute | solution.py:266
  92.2 7.0 %collective-permute-start.15 = (bf16[768,128]{1,0:T(8,128)(2,1)S(1)}, bf16[768,128]{1,0:T(8,128)(2,1)S(1)}, u32[]{:S(2)}, u32[]{:S(2)}) collective-permute-start(bf16[768,128]{1,0:T(8,128)(2,1)S(1)} %shard_map.83.refs_0_), channel_id=1, source_target_pairs={{0,112},{16,0},{32,16},{48,32},{64,48},{80,64},{96,80},{112,96},{1... | collective-permute-start | bytes 589832 | tf_op jit(solution)/shard_map/ppermute | solution.py:281
  94.1 8.9 %collective-permute-start.19 = (bf16[768,128]{1,0:T(8,128)(2,1)S(1)}, bf16[768,128]{1,0:T(8,128)(2,1)S(1)}, u32[]{:S(2)}, u32[]{:S(2)}) collective-permute-start(bf16[768,128]{1,0:T(8,128)(2,1)S(1)} %shard_map.83.refs_0_), channel_id=1, source_target_pairs={{0,16},{16,32},{32,48},{48,64},{64,80},{80,96},{96,112},{112,0},{1... | collective-permute-start | bytes 589832 | tf_op jit(solution)/shard_map/ppermute | solution.py:284
  99.3 7.9 %collective-permute-start.16 = (bf16[768,128]{1,0:T(8,128)(2,1)S(1)}, bf16[768,128]{1,0:T(8,128)(2,1)S(1)}, u32[]{:S(2)}, u32[]{:S(2)}) collective-permute-start(bf16[768,128]{1,0:T(8,128)(2,1)S(1)} %collective-permute-done.15.refs_1_), channel_id=1, source_target_pairs={{0,112},{16,0},{32,16},{48,32},{64,48},{80,64},{96,80},{112,96},{1... | collective-permute-start | bytes 589832 | tf_op jit(solution)/shard_map/ppermute | solution.py:281
  103.0 8.1 %collective-permute-start.20 = (bf16[768,128]{1,0:T(8,128)(2,1)S(1)}, bf16[768,128]{1,0:T(8,128)(2,1)S(1)}, u32[]{:S(2)}, u32[]{:S(2)}) collective-permute-start(bf16[768,128]{1,0:T(8,128)(2,1)S(1)} %collective-permute-done.19.refs_7_), channel_id=1, source_target_pairs={{0,16},{16,32},{32,48},{48,64},{64,80},{80,96},{96,112},{112,0},{1... | collective-permute-start | bytes 589832 | tf_op jit(solution)/shard_map/ppermute | solution.py:284
  107.2 7.3 %collective-permute-start.17 = (bf16[768,128]{1,0:T(8,128)(2,1)S(1)}, bf16[768,128]{1,0:T(8,128)(2,1)S(1)}, u32[]{:S(2)}, u32[]{:S(2)}) collective-permute-start(bf16[768,128]{1,0:T(8,128)(2,1)S(1)} %collective-permute-done.16.refs_2_), channel_id=1, source_target_pairs={{0,112},{16,0},{32,16},{48,32},{64,48},{80,64},{96,80},{112,96},{1... | collective-permute-start | bytes 589832 | tf_op jit(solution)/shard_map/ppermute | solution.py:281
  111.1 7.1 %collective-permute-start.21 = (bf16[768,128]{1,0:T(8,128)(2,1)S(1)}, bf16[768,128]{1,0:T(8,128)(2,1)S(1)}, u32[]{:S(2)}, u32[]{:S(2)}) collective-permute-start(bf16[768,128]{1,0:T(8,128)(2,1)S(1)} %collective-permute-done.20.refs_6_), channel_id=1, source_target_pairs={{0,16},{16,32},{32,48},{48,64},{64,80},{80,96},{96,112},{112,0},{1... | collective-permute-start | bytes 589832 | tf_op jit(solution)/shard_map/ppermute | solution.py:284
  114.5 6.9 %collective-permute-start.18 = (bf16[768,128]{1,0:T(8,128)(2,1)S(1)}, bf16[768,128]{1,0:T(8,128)(2,1)S(1)}, u32[]{:S(2)}, u32[]{:S(2)}) collective-permute-start(bf16[768,128]{1,0:T(8,128)(2,1)S(1)} %collective-permute-done.17.refs_3_), channel_id=1, source_target_pairs={{0,112},{16,0},{32,16},{48,32},{64,48},{80,64},{96,80},{112,96},{1... | collective-permute-start | bytes 589832 | tf_op jit(solution)/shard_map/ppermute | solution.py:281
  125.8 2.4 %collective-permute-start.23 = (bf16[2,384,512]{2,1,0:T(8,128)(2,1)S(1)}, bf16[2,384,512]{2,1,0:T(8,128)(2,1)S(1)}, u32[]{:S(2)}, u32[]{:S(2)}) collective-permute-start(bf16[2,384,512]{2,1,0:T(8,128)(2,1)S(1)} %get-tuple-element.12), channel_id=1, source_target_pairs={{0,4},{4,0},{1,5},{5,1},{2,6},{6,2},{3,7},{7,3},{8,12},{12,8},{9,1... | collective-permute-start | bytes 2359304 | tf_op jit(solution)/shard_map/ppermute | solution.py:287
  (1 other events, 1.6 us)
Sparse Core Ops, SparseCore 0:
  18.4 35.3 all-gather.2

commit v2 on v1

v2 whole, which is shorter than its diff:
```python
import jax
import jax.numpy as jnp
from jax import lax
from jax.experimental import pallas as pl
from jax.experimental.pallas import tpu as pltpu
from jax.sharding import Mesh, PartitionSpec as P

DH = 128
BLOCK = 128
SLOTS = 256
PART = 1152
masked_score = -1e30
exp2_scale = DH ** -0.5 * 1.4426950408889634

VMEM = pl.BlockSpec(memory_space=pltpu.VMEM)
SMEM = pl.BlockSpec(memory_space=pltpu.SMEM)
PARAMS = pltpu.CompilerParams(vmem_limit_bytes=48 * 1024 * 1024)


def columns_of(index):
    return pl.ds(pl.multiple_of(index * DH, DH), DH)


def location():
    return {name: lax.axis_index(name) for name in ("yh", "z", "yl", "co")}


def bring(outside, held, arrived):
    copies = [
        pltpu.make_async_copy(source, target, arrived.at[index])
        for index, (source, target) in enumerate(zip(outside, held))
    ]
    for copy in copies:
        copy.start()
    for copy in copies:
        copy.wait()


def pack_kernel(*refs):
    outside, (own, other, split_queries), held, arrived = refs[:5], refs[5:8], refs[8:13], refs[13]
    bring(outside, held, arrived)
    cache_keys, cache_values, new_keys, new_values, queries = held
    high = location()["yh"]
    for target, head in ((own, high), (other, 1 - high)):
        columns = columns_of(head)
        for row in range(2):
            target[SLOTS * row : SLOTS * (row + 1)] = cache_keys[row, :, columns]
            target[512 + SLOTS * row : 512 + SLOTS * (row + 1)] = cache_values[row, :, columns]
        target[1024:1088] = new_keys[:, :, columns].reshape(64, DH)
        target[1088:1152] = new_values[:, :, columns].reshape(64, DH)
    for head in range(16):
        piece = queries[:, :, DH * head : DH * (head + 1)].reshape(64, DH)
        split_queries[head, 0] = piece
        split_queries[head // 8 * 8 + (head + 4) % 8, 1] = piece


def with_copies(kernel, arrays, out_shape, **options):
    return pl.pallas_call(
        kernel,
        out_shape=out_shape,
        in_specs=[pl.BlockSpec(memory_space=pl.ANY)] * len(arrays),
        out_specs=jax.tree.map(lambda _: VMEM, out_shape),
        scratch_shapes=[pltpu.VMEM(array.shape, array.dtype) for array in arrays]
        + [pltpu.SemaphoreType.DMA((len(arrays),))],
        compiler_params=pltpu.CompilerParams(vmem_limit_bytes=60 * 1024 * 1024),
        **options,
    )(*arrays)


def pack(*arrays):
    shape = jax.ShapeDtypeStruct((PART, DH), jnp.bfloat16)
    return with_copies(
        pack_kernel, arrays, (shape, shape, jax.ShapeDtypeStruct((16, 2, 64, DH), jnp.bfloat16))
    )


def score(query, key):
    return lax.dot_general(
        query, key, (((1,), (1,)), ((), ())), preferred_element_type=jnp.float32
    )


def sort_rows(flat):
    target = lax.broadcasted_iota(jnp.int32, (256, 256), 0)
    origin = lax.broadcasted_iota(jnp.int32, (256, 256), 1)
    wanted = jnp.where(target < 128, 2 * target, 2 * target - 255)
    permute = (origin == wanted).astype(jnp.float32).astype(jnp.bfloat16)
    moved = jnp.dot(permute, flat, preferred_element_type=jnp.float32).astype(jnp.bfloat16)
    return moved[:128], moved[128:]


def attend_kernel(offsets, head, skip_blocks, cache_len, queries, *refs):
    high, ring = location()["yh"], location()["z"]
    sources = [
        (high if is_own else 1 - high) * 8 + lax.rem(ring + distance, 8)
        for distance, is_own in offsets
    ]
    parts, refs = refs[: len(offsets)], refs[len(offsets) :]
    if head == 0:
        mine, own_level, sorted_queries, new_keys, new_values, scores = refs
    else:
        message, sorted_queries, new_keys, new_values, scores, statistics = refs
        statistics[...] = jnp.zeros_like(statistics)
    for group in range(4):
        flat = queries[4 * group : 4 * group + 4, head].reshape(256, DH)
        first_row, second_row = sort_rows(flat)
        sorted_queries[0, 128 * group : 128 * (group + 1)] = first_row
        sorted_queries[1, 128 * group : 128 * (group + 1)] = second_row
    for group in range(2):
        for start, sorted_rows in ((1024, new_keys), (1088, new_values)):
            flat = jnp.concatenate(
                [part[start : start + 64] for part in parts[4 * group : 4 * group + 4]], axis=0
            )
            first_row, second_row = sort_rows(flat)
            sorted_rows[0, 128 * group : 128 * (group + 1)] = first_row
            sorted_rows[1, 128 * group : 128 * (group + 1)] = second_row
    lane = lax.broadcasted_iota(jnp.int32, (1, 256), 1)
    new_token = lane % 32
    for index, source in enumerate(sources):
        new_token = new_token + jnp.where(lane // 32 == index, source * 32, 0)
    larger = (skip_blocks[1] > skip_blocks[0]).astype(jnp.int32)
    most = jnp.maximum(skip_blocks[0], skip_blocks[1])
    fewer = jnp.minimum(skip_blocks[0], skip_blocks[1])
    diagonal = lax.broadcasted_iota(jnp.int32, (128, 128), 0) == lax.broadcasted_iota(
        jnp.int32, (128, 128), 1
    )

    for index in range(3):
        row = 1 - larger if index == 1 else larger
        count = fewer if index == 1 else most
        block = 2 if index == 2 else 0
        slot = 2 if index == 2 else row
        first = jnp.where(row == 0, cache_len[0], cache_len[1]) - count * BLOCK
        key_rows = pl.ds(pl.multiple_of(row * SLOTS, SLOTS), SLOTS)
        value_rows = pl.ds(pl.multiple_of(row * SLOTS + 512, SLOTS), SLOTS)
        query = sorted_queries[row, pl.ds(block * 128, 256), :]
        peak = jnp.full((256, 128), masked_score, jnp.float32)
        spans = []
        for place_in, (part, source) in enumerate(zip(parts, sources)):
            bias = jnp.where(lane < first - source * SLOTS, 0.0, masked_score)
            found = score(query, part[key_rows]) + bias
            span = slice(SLOTS * place_in, SLOTS * (place_in + 1))
            scores[index, :, span] = found
            spans.append((span, lambda part=part: part[value_rows]))
            peak = jnp.maximum(peak, jnp.maximum(found[:, :128], found[:, 128:]))
        token = lax.broadcasted_iota(jnp.int32, (256, 1), 0) + block * 128
        found = score(query, new_keys[row])
        found = jnp.where(new_token <= token, found, masked_score)
        span = slice(SLOTS * len(parts), SLOTS * (len(parts) + 1))
        scores[index, :, span] = found
        spans.append((span, lambda: new_values[row]))
        peak = jnp.maximum(peak, jnp.maximum(found[:, :128], found[:, 128:]))
        top = jnp.broadcast_to(jnp.max(peak, axis=1, keepdims=True), (256, 128))
        total = jnp.zeros((256, 128), jnp.float32)
        mixed = jnp.zeros((256, DH), jnp.float32)
        wide = jnp.concatenate([top, top], axis=1)
        for span, values in spans:
            weight = jnp.exp2((scores[index, :, span] - wide) * exp2_scale)
            total = total + (weight[:, :128] + weight[:, 128:])
            mixed = mixed + jnp.dot(
                weight.astype(jnp.bfloat16), values(), preferred_element_type=jnp.float32
            )
        whole = jnp.broadcast_to(jnp.sum(total, axis=1, keepdims=True), (256, 128))
        result = mixed / whole
        level = top * exp2_scale + jnp.log2(whole)
        result = jnp.concatenate(
            [
                jnp.where(count > block, result[:128], 0.0),
                jnp.where(count > block + 1, result[128:], 0.0),
            ],
            axis=0,
        )
        for half in range(2):
            here = slot + 3 * half
            rows = pl.ds(here * 128, 128)
            if index < 2:
                rows = pl.ds(pl.multiple_of(here * 128, 128), 128)
            piece = result[128 * half : 128 * (half + 1)]
            piece_level = level[128 * half : 128 * (half + 1)]
            if head == 0:
                mine[rows, :] = piece
                own_level[rows, :] = piece_level
            else:
                message[rows, :] = piece.astype(jnp.bfloat16)
                flat = jnp.sum(jnp.where(diagonal, piece_level, 0.0), axis=0, keepdims=True)
                for term in range(3):
                    rounded = flat.astype(jnp.bfloat16).astype(jnp.float32)
                    statistics[pl.ds(term * 8 + here, 1), :] = rounded
                    flat = flat - rounded
    if head == 1:
        message[768:800] = statistics[...].astype(jnp.bfloat16)


def attend(counts, queries, parts, offsets, head):
    scratch = [
        pltpu.VMEM((2, 512, DH), jnp.bfloat16),
        pltpu.VMEM((2, 256, DH), jnp.bfloat16),
        pltpu.VMEM((2, 256, DH), jnp.bfloat16),
        pltpu.VMEM((3, 256, SLOTS * (len(parts) + 1)), jnp.float32),
    ]
    if head == 0:
        out_shape = (jax.ShapeDtypeStruct((768, DH), jnp.float32),) * 2
        out_specs = (VMEM,) * 2
    else:
        out_shape = jax.ShapeDtypeStruct((800, DH), jnp.bfloat16)
        out_specs = VMEM
        scratch.append(pltpu.VMEM((32, DH), jnp.float32))
    return pl.pallas_call(
        lambda *refs: attend_kernel(offsets, head, *refs),
        out_shape=out_shape,
        in_specs=[SMEM] * 2 + [VMEM] * (1 + len(parts)),
        out_specs=out_specs,
        scratch_shapes=scratch,
        compiler_params=PARAMS,
        cost_estimate=pl.CostEstimate(
            flops=5 * 10**9, bytes_accessed=6 * 2**20, transcendentals=2 * 10**6
        ),
    )(*counts, queries, *parts)


def merge_kernel(mine, own_level, message, out):
    diagonal = lax.broadcasted_iota(jnp.int32, (128, 128), 0) == lax.broadcasted_iota(
        jnp.int32, (128, 128), 1
    )
    statistics = message[768:800].astype(jnp.float32)
    for slot in range(6):
        rows = slice(128 * slot, 128 * (slot + 1))
        flat = (
            statistics[slot : slot + 1]
            + statistics[8 + slot : 9 + slot]
            + statistics[16 + slot : 17 + slot]
        )
        level = jnp.sum(jnp.where(diagonal, flat, 0.0), axis=1, keepdims=True)
        top = jnp.maximum(own_level[rows], level)
        own_weight = jnp.exp2(own_level[rows] - top)
        other_weight = jnp.exp2(level - top)
        mixed = own_weight * mine[rows] + other_weight * message[rows].astype(jnp.float32)
        out[rows] = (mixed / (own_weight + other_weight)).astype(jnp.bfloat16)


def merge(mine, own_level, message):
    return pl.pallas_call(
        merge_kernel,
        out_shape=jax.ShapeDtypeStruct((768, DH), jnp.bfloat16),
        in_specs=[VMEM] * 3,
        out_specs=VMEM,
        compiler_params=PARAMS,
    )(mine, own_level, message)


def project_kernel(*refs):
    attended = refs[:9]
    kept_half, got_half, kept, sent, gathered = refs[9:]
    ring, core = location()["z"], location()["co"]
    for distance in range(8):
        columns = columns_of(lax.rem(ring + distance, 8))
        if distance == 4:
            gathered[:384, columns] = attended[4][...]
            gathered[384:, columns] = attended[8][...]
        else:
            gathered[:, columns] = attended[distance][...]
    for target, owner in ((sent, 1 - core), (kept, core)):
        rows = gathered[pl.ds(pl.multiple_of(owner * 384, 128), 384), :]
        for side, weights in enumerate((kept_half, got_half)):
            for pair in range(2):
                block = jnp.concatenate([weights[2 * pair], weights[2 * pair + 1]], axis=1)
                target[side, :, 256 * pair : 256 * (pair + 1)] = jnp.dot(
                    rows, block, preferred_element_type=jnp.float32
                ).astype(target.dtype)


def project(attended, kept_half, got_half):
    return pl.pallas_call(
        project_kernel,
        out_shape=(
            jax.ShapeDtypeStruct((2, 384, 512), jnp.float32),
            jax.ShapeDtypeStruct((2, 384, 512), jnp.bfloat16),
        ),
        in_specs=[VMEM] * 11,
        out_specs=(VMEM, VMEM),
        scratch_shapes=[pltpu.VMEM((768, 1024), jnp.bfloat16)],
        compiler_params=PARAMS,
    )(*attended, kept_half, got_half)


def add_kernel(kept, arrived, mine, near, far, cross):
    low = location()["yl"]
    for side, targets in ((0, (mine, near)), (1, (far, cross))):
        total = kept[side] + arrived[side].astype(jnp.float32)
        pair = total[:256]
        single = jnp.concatenate([total[256:], jnp.zeros((128, 512), jnp.float32)], axis=0)
        targets[0][...] = jnp.where(low == 0, pair, single).astype(targets[0].dtype)
        targets[1][...] = jnp.where(low == 0, single, pair).astype(targets[1].dtype)


def add_cores(kept, arrived):
    shape = jax.ShapeDtypeStruct((256, 512), jnp.bfloat16)
    return pl.pallas_call(
        add_kernel,
        out_shape=(jax.ShapeDtypeStruct((256, 512), jnp.float32), shape, shape, shape),
        in_specs=[VMEM, VMEM],
        out_specs=(VMEM,) * 4,
        compiler_params=PARAMS,
    )(kept, arrived)


def final_kernel(skip_blocks, mine, near, far, cross, out):
    low = location()["yl"]
    total = mine[...]
    for share in (near, far, cross):
        total = total + share[...].astype(jnp.float32)
    larger = skip_blocks[1] > skip_blocks[0]
    first, second = total[:128], total[128:]
    zero = jnp.zeros_like(first)
    first_row = jnp.where(low == 0, first, jnp.where(larger, zero, first))
    second_row = jnp.where(low == 0, second, jnp.where(larger, first, zero))
    out[:, 0, :] = first_row
    out[:, 1, :] = second_row


def finish(skip_blocks, *shares):
    return pl.pallas_call(
        final_kernel,
        out_shape=jax.ShapeDtypeStruct((128, 2, 512), jnp.float32),
        in_specs=[SMEM] + [VMEM] * 4,
        out_specs=VMEM,
        compiler_params=PARAMS,
    )(skip_blocks, *shares)


SWAP = [(0, 1), (1, 0)]


def ring_send(array, hops):
    return lax.ppermute(array, "z", [(index, (index + hops) % 8) for index in range(8)])


def on_device(
    queries, new_keys, new_values, cache_keys, cache_values, out_proj, skip_blocks, cache_len
):
    high = lax.axis_index("yh")
    counts = (skip_blocks, cache_len)
    own, other, split_queries = pack(cache_keys, cache_values, new_keys, new_values, queries)
    partner = lax.ppermute(other, "yh", SWAP)
    own_up, own_down = ring_send(own, 1), ring_send(own, -1)
    got_queries = lax.all_to_all(
        split_queries, ("yh", "z"), split_axis=0, concat_axis=0, tiled=True
    )
    partner_up, partner_down = ring_send(partner, 1), ring_send(partner, -1)
    own_down_two = ring_send(own_down, -1)
    tied_up, own_up = lax.optimization_barrier((partner_up, own_up))
    partner_up_two = ring_send(tied_up, 1)
    parts = [own, partner, own_up, own_down, own_down_two, partner_up, partner_down, partner_up_two]
    offsets = [
        (0, True), (0, False), (7, True), (1, True), (2, True), (7, False), (1, False), (6, False)
    ]
    out_proj, own = lax.optimization_barrier((out_proj, own))
    weights = lax.all_gather(out_proj, "row", axis=0, tiled=False)
    weights, _ = lax.optimization_barrier((weights, tied_up))
    sent_half = lax.dynamic_slice_in_dim(weights, (1 - high) * 1024, 1024, 1)
    kept_half = lax.dynamic_slice_in_dim(weights, high * 1024, 1024, 1)
    got_half = lax.ppermute(sent_half, "yh", SWAP)
    message = attend(counts, got_queries, parts, offsets, 1)
    mine, own_level = attend(counts, got_queries, parts, offsets, 0)
    attended = merge(mine, own_level, ring_send(message, 4))

    from_below, from_above = ring_send(attended, 1), ring_send(attended, -1)
    two_below, two_above = ring_send(attended, 2), ring_send(attended, -2)
    gathered = [
        attended,
        from_above,
        two_above,
        ring_send(two_above, -1),
        ring_send(two_below[:384], 2),
        ring_send(two_below, 1),
        two_below,
        from_below,
        ring_send(two_above[384:], -2),
    ]
    kept, sent = project(gathered, kept_half, got_half)
    arrived = lax.ppermute(sent, "co", SWAP)
    mine, near, far, cross = add_cores(kept, arrived)
    far = lax.ppermute(far, "yh", SWAP)
    cross = lax.ppermute(cross, ("yh", "yl"), [(0, 3), (1, 2), (2, 1), (3, 0)])
    near = lax.ppermute(near, "yl", SWAP)
    return finish(skip_blocks, mine, near, far, cross)


def solution(mesh):
    split = Mesh(mesh.devices.reshape(2, 8, 2, 2, 4), ("yh", "z", "yl", "co", "row"))
    ctx, tp = ("yh", "z"), ("yl", "co")
    placed = (
        P(ctx, "row", tp),
        P(ctx, "row", tp),
        P(ctx, "row", tp),
        P("row", ctx, tp),
        P("row", ctx, tp),
        P(tp, ("yh", "z", "row")),
        P("row"),
        P("row"),
    )
    return jax.shard_map(
        on_device, mesh=split, in_specs=placed, out_specs=P(tp, "row", ctx), check_vma=False
    )
```

time: 157 us -> 134 us (0.85)
  blocking collectives: 19.8 us -> 0 us
  starting transfers between devices: 51.6 us -> 46.7 us
    all_to_all x1 -> x0, blocking collectives: 19.8 us -> none  [on_device(): lax.all_to_all(merged, ('yh', 'yl'), split_axis=0, concat_axis=0, tiled=T...]
    ppermute x1, waiting for transfers between devices: 0.33 us -> 9.19 us  [on_device(): partner = lax.ppermute(other, 'yh', SWAP)]
    ppermute x22 -> x19, starting transfers between devices: 39 us -> 31.9 us  [the longest x15 24.2 us: ring_send(): lax.ppermute(array, 'z', [(index, (index + hops) % 8) for index in range(...]
    all_to_all x1, waiting for transfers between devices: 6.63 us -> 0.01 us  [on_device(): lax.all_to_all(split_queries, ('yh', 'z'), split_axis=0, concat_axis=0, t...]
    dynamic_slice x0 -> x1, local copies, waits for them, and re-layouts: none -> 2.73 us  [on_device(): sent_half = lax.dynamic_slice_in_dim(weights, (1 - high) * 1024, 1024, 1)]
    all_to_all x1, starting transfers between devices: 9.14 us -> 11.2 us  [on_device(): lax.all_to_all(split_queries, ('yh', 'z'), split_axis=0, concat_axis=0, t...]
    pallas_call x3 -> x5, Pallas kernels: 10.3 us -> 12.2 us  [the longest x2 9.28 us: attend(): pl.pallas_call(lambda *refs: attend_kernel(offsets, head, *refs), out_sha...]
    ppermute x22 -> x19, waiting for transfers between devices: 42.5 us -> 41.7 us  [the longest x15 27.2 us: ring_send(): lax.ppermute(array, 'z', [(index, (index + hops) % 8) for index in range(...]
  transfers between devices with their start and end apart: 26 -> 23, of which waited for: 17 -> 12; matrix products, arithmetic and copies ran while one was open for 1% -> 2% of each run, Pallas kernels for 6% -> 7%
where the time goes in v2:
time: 134 us
  waiting for transfers between devices  53.2 us (40%)
  starting transfers between devices  46.7 us (35%)
  Pallas kernels  16.1 us (12%)
  between operations  13.5 us (10%)
  local copies, waits for them, and re-layouts  4.44 us (3%)
    ppermute x15, waiting for transfers between devices, ring_send(): lax.ppermute(array, 'z', [(index, (index + hops) % 8) for index in range(...  27.2 us
    ppermute x15, starting transfers between devices, ring_send(): lax.ppermute(array, 'z', [(index, (index + hops) % 8) for index in range(...  24.2 us
    all_to_all x1, starting transfers between devices, on_device(): lax.all_to_all(split_queries, ('yh', 'z'), split_axis=0, concat_axis=0, t...  11.2 us
    pallas_call x2, Pallas kernels, attend(): pl.pallas_call(lambda *refs: attend_kernel(offsets, head, *refs), out_sha...  9.28 us
    ppermute x1, waiting for transfers between devices, on_device(): partner = lax.ppermute(other, 'yh', SWAP)  9.19 us
    ppermute x1, waiting for transfers between devices, on_device(): far = lax.ppermute(far, 'yh', SWAP)  7.48 us
    ppermute x1, waiting for transfers between devices, on_device(): near = lax.ppermute(near, 'yl', SWAP)  4.45 us
    ppermute x1, starting transfers between devices, on_device(): far = lax.ppermute(far, 'yh', SWAP)  3.91 us
  transfers between devices with their start and end apart: 23, of which 12 were waited for; matrix products, arithmetic and copies ran while one was open for 2% of the time, Pallas kernels for 7%

profile of v2, /device:TPU:2, one launch (start us, length us, event | category | flops | bytes accessed | tf_op | source)
XLA Modules:
  0.0 133.9 jit_solution(10678370374902584346)
XLA Ops:
  6.5 2.5 %shard_map.82 = (bf16[1152,128]{1,0:T(8,128)(2,1)}, bf16[1152,128]{1,0:T(8,128)(2,1)}, bf16[16,2,64,128]{3,2,1,0:T(8,128)(2,1)}) custom-call(bf16[2,256,256]{2,1,0:T(8,128)(2,1)} %refs_0_.3, bf16[2,256,256]{2,1,0:T(8,128)(2,1)} %refs_1_.3, bf16[32,2,256]{2,1,0:T(2,128)(2,1)} %refs_2_.1, bf16[32,2,256]{2,1,0:T(2,128)(2,1)} %refs_3_.1, ...), custom_call_target="tpu_custom_call" | custom-call | tf_op jit(solution)/shard_map/pallas_call | solution.py:58
  9.0 11.2 %all-to-all-start = ((bf16[16,2,64,128]{3,2,1,0:T(8,128)(2,1)}), bf16[16,2,64,128]{3,2,1,0:T(8,128)(2,1)S(1)}, u32[]{:S(2)}, u32[]{:S(2)}) async-start(bf16[16,2,64,128]{3,2,1,0:T(8,128)(2,1)} %get-tuple-element.20), calls=%async_computation | async-start | bytes 1048576 | tf_op jit(solution)/shard_map/all_to_all | solution.py:346
  20.3 3.4 %collective-permute-start = (bf16[1152,128]{1,0:T(8,128)(2,1)}, bf16[1152,128]{1,0:T(8,128)(2,1)S(1)}, u32[]{:S(2)}, u32[]{:S(2)}) collective-permute-start(bf16[1152,128]{1,0:T(8,128)(2,1)} %get-tuple-element.22), channel_id=1, source_target_pairs={{0,128},{128,0},{1,129},{129,1},{2,130},{130,2},{3,131},{131,3},{4... | collective-permute-start | bytes 884744 | tf_op jit(solution)/shard_map/ppermute | solution.py:344
  23.7 2.7 %collective-permute-start.3 = (bf16[1152,128]{1,0:T(8,128)(2,1)}, bf16[1152,128]{1,0:T(8,128)(2,1)S(1)}, u32[]{:S(2)}, u32[]{:S(2)}) collective-permute-start(bf16[1152,128]{1,0:T(8,128)(2,1)} %get-tuple-element.21.refs_3_), channel_id=1, source_target_pairs={{0,112},{16,0},{32,16},{48,32},{64,48},{80,64},{96,80},{112,96},{1... | collective-permute-start | bytes 884744 | tf_op jit(solution)/shard_map/ppermute | solution.py:335
  26.4 9.2 %collective-permute-done.refs_4_ = bf16[1152,128]{1,0:T(8,128)(2,1)S(1)} collective-permute-done((bf16[1152,128]{1,0:T(8,128)(2,1)}, bf16[1152,128]{1,0:T(8,128)(2,1)S(1)}, u32[]{:S(2)}, u32[]{:S(2)}) %collective-permute-start) | collective-permute-done | bytes 294944 | tf_op jit(solution)/shard_map/ppermute | solution.py:344
  35.6 1.1 collective-permute-start.1
  36.7 2.1 %collective-permute-start.5 = (bf16[1152,128]{1,0:T(8,128)(2,1)S(1)}, bf16[1152,128]{1,0:T(8,128)(2,1)}, u32[]{:S(2)}, u32[]{:S(2)}) collective-permute-start(bf16[1152,128]{1,0:T(8,128)(2,1)S(1)} %collective-permute-done.refs_4_), channel_id=1, source_target_pairs={{0,112},{16,0},{32,16},{48,32},{64,48},{80,64},{96,80},{112,96},{1... | collective-permute-start | bytes 884744 | tf_op jit(solution)/shard_map/ppermute | solution.py:335
  38.8 2.3 %collective-permute-done.3.refs_6_ = bf16[1152,128]{1,0:T(8,128)(2,1)S(1)} collective-permute-done((bf16[1152,128]{1,0:T(8,128)(2,1)}, bf16[1152,128]{1,0:T(8,128)(2,1)S(1)}, u32[]{:S(2)}, u32[]{:S(2)}) %collective-permute-start.3) | collective-permute-done | bytes 294944 | tf_op jit(solution)/shard_map/ppermute | solution.py:335
  41.1 1.6 %collective-permute-start.4 = (bf16[1152,128]{1,0:T(8,128)(2,1)S(1)}, bf16[1152,128]{1,0:T(8,128)(2,1)}, u32[]{:S(2)}, u32[]{:S(2)}) collective-permute-start(bf16[1152,128]{1,0:T(8,128)(2,1)S(1)} %collective-permute-done.3.refs_6_), channel_id=1, source_target_pairs={{0,112},{16,0},{32,16},{48,32},{64,48},{80,64},{96,80},{112,96},{1... | collective-permute-start | bytes 884744 | tf_op jit(solution)/shard_map/ppermute | solution.py:335
  43.4 4.3 %collective-permute-done.1.refs_8_ = bf16[1152,128]{1,0:T(8,128)(2,1)} collective-permute-done((bf16[1152,128]{1,0:T(8,128)(2,1)S(1)}, bf16[1152,128]{1,0:T(8,128)(2,1)}, u32[]{:S(2)}, u32[]{:S(2)}) %collective-permute-start.1) | collective-permute-done | bytes 294944 | tf_op jit(solution)/shard_map/ppermute | solution.py:335
  47.7 2.7 %constant_dynamic-slice_fusion = (bf16[4,1024,128]{2,1,0:T(8,128)(2,1)}, bf16[4,1024,128]{2,1,0:T(8,128)(2,1)S(1)}) fusion(bf16[4,2048,128]{2,1,0:T(8,128)(2,1)} %bitcast.1, s32[]{:T(128)S(6)} %select_n.7, s32[]{:T(128)S(6)} %select_n.6), kind=kLoop, calls=%fused_computation | loop fusion | bytes 4194312 | tf_op jit(solution)/shard_map/dynamic_slice | solution.py:360
  50.5 3.0 %collective-permute-start.16 = (bf16[4,1024,128]{2,1,0:T(8,128)(2,1)}, bf16[4,1024,128]{2,1,0:T(8,128)(2,1)S(1)}, u32[]{:S(2)}, u32[]{:S(2)}) collective-permute-start(bf16[4,1024,128]{2,1,0:T(8,128)(2,1)} %get-tuple-element.35), channel_id=1, source_target_pairs={{0,128},{128,0},{1,129},{129,1},{2,130},{130,2},{3,131},{131,3},{4... | collective-permute-start | bytes 3145736 | tf_op jit(solution)/shard_map/ppermute | solution.py:362
  53.4 3.8 %collective-permute-done.6.refs_10_ = bf16[1152,128]{1,0:T(8,128)(2,1)} collective-permute-done((bf16[1152,128]{1,0:T(8,128)(2,1)}, bf16[1152,128]{1,0:T(8,128)(2,1)}, u32[]{:S(2)}, u32[]{:S(2)}) %collective-permute-start.6) | collective-permute-done | bytes 294944 | tf_op jit(solution)/shard_map/ppermute | solution.py:335
  58.2 4.7 %shard_map.84 = bf16[800,128]{1,0:T(8,128)(2,1)S(1)} custom-call(s32[2]{0:T(128)S(1)} %copy-done, s32[2]{0:T(128)S(1)} %copy-done.4, bf16[16,2,64,128]{3,2,1,0:T(8,128)(2,1)S(1)} %all-to-all-done.refs_2_, bf16[1152,128]{1,0:T(8,128)(2,1)S(1)} %copy-done.1, bf16[1152,128]{1,0:T(8,128)(2,1)S(1)} %collective-permute-done.refs_4_, ...), custom_call_target="tpu_custom_call" | custom-call | flops 5000000000 | bytes 6291456 | tf_op jit(solution)/shard_map/pallas_call | solution.py:208
  62.8 2.8 %collective-permute-start.7 = (bf16[800,128]{1,0:T(8,128)(2,1)S(1)}, bf16[800,128]{1,0:T(8,128)(2,1)S(1)}, u32[]{:S(2)}, u32[]{:S(2)}) collective-permute-start(bf16[800,128]{1,0:T(8,128)(2,1)S(1)} %shard_map.84), channel_id=1, source_target_pairs={{0,64},{16,80},{32,96},{48,112},{64,0},{80,16},{96,32},{112,48},{1... | collective-permute-start | bytes 614408 | tf_op jit(solution)/shard_map/ppermute | solution.py:335
  65.7 4.6 %shard_map.83 = (f32[768,128]{1,0:T(8,128)S(1)}, f32[768,128]{1,0:T(8,128)S(1)}) custom-call(s32[2]{0:T(128)S(1)} %copy-done, s32[2]{0:T(128)S(1)} %copy-done.4, bf16[16,2,64,128]{3,2,1,0:T(8,128)(2,1)S(1)} %all-to-all-done.refs_2_, bf16[1152,128]{1,0:T(8,128)(2,1)S(1)} %copy-done.1, bf16[1152,128]{1,0:T(8,128)(2,1)S(1)} %collective-permute-done.refs_4_, ...), custom_call_target="tpu_custom_call" | custom-call | flops 5000000000 | bytes 6291456 | tf_op jit(solution)/shard_map/pallas_call | solution.py:208
  70.3 6.2 %collective-permute-done.7.message = bf16[800,128]{1,0:T(8,128)(2,1)S(1)} collective-permute-done((bf16[800,128]{1,0:T(8,128)(2,1)S(1)}, bf16[800,128]{1,0:T(8,128)(2,1)S(1)}, u32[]{:S(2)}, u32[]{:S(2)}) %collective-permute-start.7) | collective-permute-done | bytes 204832 | tf_op jit(solution)/shard_map/ppermute | solution.py:335
  76.9 2.9 %collective-permute-start.11 = (bf16[768,128]{1,0:T(8,128)(2,1)S(1)}, bf16[768,128]{1,0:T(8,128)(2,1)S(1)}, u32[]{:S(2)}, u32[]{:S(2)}) collective-permute-start(bf16[768,128]{1,0:T(8,128)(2,1)S(1)} %shard_map.85.refs_0_), channel_id=1, source_target_pairs={{0,32},{16,48},{32,64},{48,80},{64,96},{80,112},{96,0},{112,16},{1... | collective-permute-start | bytes 589832 | tf_op jit(solution)/shard_map/ppermute | solution.py:335
  79.8 3.2 %collective-permute-start.8 = (bf16[768,128]{1,0:T(8,128)(2,1)S(1)}, bf16[768,128]{1,0:T(8,128)(2,1)S(1)}, u32[]{:S(2)}, u32[]{:S(2)}) collective-permute-start(bf16[768,128]{1,0:T(8,128)(2,1)S(1)} %shard_map.85.refs_0_), channel_id=1, source_target_pairs={{0,112},{16,0},{32,16},{48,32},{64,48},{80,64},{96,80},{112,96},{1... | collective-permute-start | bytes 589832 | tf_op jit(solution)/shard_map/ppermute | solution.py:335
  83.0 3.5 %collective-permute-done.9.refs_2_ = bf16[768,128]{1,0:T(8,128)(2,1)S(1)} collective-permute-done((bf16[768,128]{1,0:T(8,128)(2,1)S(1)}, bf16[768,128]{1,0:T(8,128)(2,1)S(1)}, u32[]{:S(2)}, u32[]{:S(2)}) %collective-permute-start.9) | collective-permute-done | bytes 196640 | tf_op jit(solution)/shard_map/ppermute | solution.py:335
  86.5 1.4 %collective-permute-start.10 = (bf16[768,128]{1,0:T(8,128)(2,1)S(1)}, bf16[768,128]{1,0:T(8,128)(2,1)S(1)}, u32[]{:S(2)}, u32[]{:S(2)}) collective-permute-start(bf16[768,128]{1,0:T(8,128)(2,1)S(1)} %collective-permute-done.9.refs_2_), channel_id=1, source_target_pairs={{0,112},{16,0},{32,16},{48,32},{64,48},{80,64},{96,80},{112,96},{1... | collective-permute-start | bytes 589832 | tf_op jit(solution)/shard_map/ppermute | solution.py:335
  87.9 2.0 %collective-permute-start.13 = (bf16[768,128]{1,0:T(8,128)(2,1)S(1)}, bf16[768,128]{1,0:T(8,128)(2,1)S(1)}, u32[]{:S(2)}, u32[]{:S(2)}) collective-permute-start(bf16[768,128]{1,0:T(8,128)(2,1)S(1)} %collective-permute-done.11.refs_6_), channel_id=1, source_target_pairs={{0,16},{16,32},{32,48},{48,64},{64,80},{80,96},{96,112},{112,0},{1... | collective-permute-start | bytes 589832 | tf_op jit(solution)/shard_map/ppermute | solution.py:335
  90.0 2.0 %collective-permute-done.14.refs_7_ = bf16[768,128]{1,0:T(8,128)(2,1)S(1)} collective-permute-done((bf16[768,128]{1,0:T(8,128)(2,1)S(1)}, bf16[768,128]{1,0:T(8,128)(2,1)S(1)}, u32[]{:S(2)}, u32[]{:S(2)}) %collective-permute-start.14) | collective-permute-done | bytes 196640 | tf_op jit(solution)/shard_map/ppermute | solution.py:335
  92.9 3.2 %collective-permute-start.15 = (bf16[384,128]{1,0:T(8,128)(2,1)S(1)}, bf16[384,128]{1,0:T(8,128)(2,1)S(1)}, u32[]{:S(2)}, u32[]{:S(2)}) collective-permute-start(bf16[384,128]{1,0:T(8,128)(2,1)S(1)} %slice.9), channel_id=1, source_target_pairs={{0,96},{16,112},{32,0},{48,16},{64,32},{80,48},{96,64},{112,80},{1... | collective-permute-start | bytes 294920 | tf_op jit(solution)/shard_map/ppermute | solution.py:335
  96.1 5.2 %collective-permute-done.12.refs_4_ = bf16[384,128]{1,0:T(8,128)(2,1)S(1)} collective-permute-done((bf16[384,128]{1,0:T(8,128)(2,1)S(1)}, bf16[384,128]{1,0:T(8,128)(2,1)S(1)}, u32[]{:S(2)}, u32[]{:S(2)}) %collective-permute-start.12) | collective-permute-done | bytes 98336 | tf_op jit(solution)/shard_map/ppermute | solution.py:335
  101.3 2.3 %shard_map.86 = (f32[2,384,512]{2,1,0:T(8,128)S(1)}, bf16[2,384,512]{2,1,0:T(8,128)(2,1)S(1)}) custom-call(bf16[768,128]{1,0:T(8,128)(2,1)S(1)} %shard_map.85.refs_0_, bf16[768,128]{1,0:T(8,128)(2,1)S(1)} %collective-permute-done.8.refs_1_, bf16[768,128]{1,0:T(8,128)(2,1)S(1)} %collective-permute-done.9.refs_2_, ...), custom_call_target="tpu_custom_call" | custom-call | tf_op jit(solution)/shard_map/pallas_call | solution.py:273
  103.7 2.3 %collective-permute-done.17.arrived = bf16[2,384,512]{2,1,0:T(8,128)(2,1)S(1)} collective-permute-done((bf16[2,384,512]{2,1,0:T(8,128)(2,1)S(1)}, bf16[2,384,512]{2,1,0:T(8,128)(2,1)S(1)}, u32[]{:S(2)}, u32[]{:S(2)}) %collective-permute-start.17) | collective-permute-done | bytes 786464 | tf_op jit(solution)/shard_map/ppermute | solution.py:381
  107.0 3.9 %collective-permute-start.19 = (bf16[256,512]{1,0:T(8,128)(2,1)S(1)}, bf16[256,512]{1,0:T(8,128)(2,1)S(1)}, u32[]{:S(2)}, u32[]{:S(2)}) collective-permute-start(bf16[256,512]{1,0:T(8,128)(2,1)S(1)} %get-tuple-element.33), channel_id=1, source_target_pairs={{0,128},{128,0},{1,129},{129,1},{2,130},{130,2},{3,131},{131,3},{4... | collective-permute-start | bytes 786440 | tf_op jit(solution)/shard_map/ppermute | solution.py:383
  111.0 4.4 %collective-permute-done.18.near = bf16[256,512]{1,0:T(8,128)(2,1)S(1)} collective-permute-done((bf16[256,512]{1,0:T(8,128)(2,1)S(1)}, bf16[256,512]{1,0:T(8,128)(2,1)S(1)}, u32[]{:S(2)}, u32[]{:S(2)}) %collective-permute-start.18) | collective-permute-done | bytes 262176 | tf_op jit(solution)/shard_map/ppermute | solution.py:385
  115.5 7.5 %collective-permute-done.19.far = bf16[256,512]{1,0:T(8,128)(2,1)S(1)} collective-permute-done((bf16[256,512]{1,0:T(8,128)(2,1)S(1)}, bf16[256,512]{1,0:T(8,128)(2,1)S(1)}, u32[]{:S(2)}, u32[]{:S(2)}) %collective-permute-start.19) | collective-permute-done | bytes 262176 | tf_op jit(solution)/shard_map/ppermute | solution.py:383
  122.9 2.6 %collective-permute-done.20.cross = bf16[256,512]{1,0:T(8,128)(2,1)S(1)} collective-permute-done((bf16[256,512]{1,0:T(8,128)(2,1)S(1)}, bf16[256,512]{1,0:T(8,128)(2,1)S(1)}, u32[]{:S(2)}, u32[]{:S(2)}) %collective-permute-start.20) | collective-permute-done | bytes 262176 | tf_op jit(solution)/shard_map/ppermute | solution.py:384
  125.5 1.6 %shard_map.88 = f32[128,2,512]{2,1,0:T(2,128)} custom-call(s32[2]{0:T(128)S(1)} %copy-done, f32[256,512]{1,0:T(8,128)S(1)} %get-tuple-element.31.mine, bf16[256,512]{1,0:T(8,128)(2,1)S(1)} %collective-permute-done.18.near, bf16[256,512]{1,0:T(8,128)(2,1)S(1)} %collective-permute-done.19.far, bf16[256,512]{1,0:T(8,128)(2,1)S(1)} %collective-permute-done.20.cross), custom_call_target="tpu_custom_call" | custom-call | tf_op jit(solution)/shard_map/pallas_call | solution.py:322
  (35 shorter events, 4.2 us)
Async XLA Ops:
  6.5 41.2 %all-gather.3.cloned.1.call-start = ((), (), s32[]{:S(2)}) async-start(), calls=%async_computation.1 | async-start | bytes 2621440 | tf_op jit(solution)/shard_map/all_gather | solution.py:358
  9.0 48.2 %all-to-all-start = ((bf16[16,2,64,128]{3,2,1,0:T(8,128)(2,1)}), bf16[16,2,64,128]{3,2,1,0:T(8,128)(2,1)S(1)}, u32[]{:S(2)}, u32[]{:S(2)}) async-start(bf16[16,2,64,128]{3,2,1,0:T(8,128)(2,1)} %get-tuple-element.20), calls=%async_computation | async-start | bytes 1048576 | tf_op jit(solution)/shard_map/all_to_all | solution.py:346
  20.3 15.3 %collective-permute-start = (bf16[1152,128]{1,0:T(8,128)(2,1)}, bf16[1152,128]{1,0:T(8,128)(2,1)S(1)}, u32[]{:S(2)}, u32[]{:S(2)}) collective-permute-start(bf16[1152,128]{1,0:T(8,128)(2,1)} %get-tuple-element.22), channel_id=1, source_target_pairs={{0,128},{128,0},{1,129},{129,1},{2,130},{130,2},{3,131},{131,3},{4... | collective-permute-start | bytes 884744 | tf_op jit(solution)/shard_map/ppermute | solution.py:344
  23.7 17.4 %collective-permute-start.3 = (bf16[1152,128]{1,0:T(8,128)(2,1)}, bf16[1152,128]{1,0:T(8,128)(2,1)S(1)}, u32[]{:S(2)}, u32[]{:S(2)}) collective-permute-start(bf16[1152,128]{1,0:T(8,128)(2,1)} %get-tuple-element.21.refs_3_), channel_id=1, source_target_pairs={{0,112},{16,0},{32,16},{48,32},{64,48},{80,64},{96,80},{112,96},{1... | collective-permute-start | bytes 884744 | tf_op jit(solution)/shard_map/ppermute | solution.py:335
  26.4 16.3 %collective-permute-start.2 = (bf16[1152,128]{1,0:T(8,128)(2,1)}, bf16[1152,128]{1,0:T(8,128)(2,1)S(1)}, u32[]{:S(2)}, u32[]{:S(2)}) collective-permute-start(bf16[1152,128]{1,0:T(8,128)(2,1)} %get-tuple-element.21.refs_3_), channel_id=1, source_target_pairs={{0,16},{16,32},{32,48},{48,64},{64,80},{80,96},{96,112},{112,0},{1... | collective-permute-start | bytes 884744 | tf_op jit(solution)/shard_map/ppermute | solution.py:335
  35.6 12.1 %collective-permute-start.1 = (bf16[1152,128]{1,0:T(8,128)(2,1)S(1)}, bf16[1152,128]{1,0:T(8,128)(2,1)}, u32[]{:S(2)}, u32[]{:S(2)}) collective-permute-start(bf16[1152,128]{1,0:T(8,128)(2,1)S(1)} %collective-permute-done.refs_4_), channel_id=1, source_target_pairs={{0,16},{16,32},{32,48},{48,64},{64,80},{80,96},{96,112},{112,0},{1... | collective-permute-start | bytes 884744 | tf_op jit(solution)/shard_map/ppermute | solution.py:335
  36.7 16.7 %collective-permute-start.5 = (bf16[1152,128]{1,0:T(8,128)(2,1)S(1)}, bf16[1152,128]{1,0:T(8,128)(2,1)}, u32[]{:S(2)}, u32[]{:S(2)}) collective-permute-start(bf16[1152,128]{1,0:T(8,128)(2,1)S(1)} %collective-permute-done.refs_4_), channel_id=1, source_target_pairs={{0,112},{16,0},{32,16},{48,32},{64,48},{80,64},{96,80},{112,96},{1... | collective-permute-start | bytes 884744 | tf_op jit(solution)/shard_map/ppermute | solution.py:335
  41.1 12.3 %collective-permute-start.4 = (bf16[1152,128]{1,0:T(8,128)(2,1)S(1)}, bf16[1152,128]{1,0:T(8,128)(2,1)}, u32[]{:S(2)}, u32[]{:S(2)}) collective-permute-start(bf16[1152,128]{1,0:T(8,128)(2,1)S(1)} %collective-permute-done.3.refs_6_), channel_id=1, source_target_pairs={{0,112},{16,0},{32,16},{48,32},{64,48},{80,64},{96,80},{112,96},{1... | collective-permute-start | bytes 884744 | tf_op jit(solution)/shard_map/ppermute | solution.py:335
  42.7 0.7 copy-start.2
  47.7 9.5 %collective-permute-start.6 = (bf16[1152,128]{1,0:T(8,128)(2,1)}, bf16[1152,128]{1,0:T(8,128)(2,1)}, u32[]{:S(2)}, u32[]{:S(2)}) collective-permute-start(bf16[1152,128]{1,0:T(8,128)(2,1)} %collective-permute-done.1.refs_8_), channel_id=1, source_target_pairs={{0,16},{16,32},{32,48},{48,64},{64,80},{80,96},{96,112},{112,0},{1... | collective-permute-start | bytes 884744 | tf_op jit(solution)/shard_map/ppermute | solution.py:335
  47.7 9.5 %copy-start = (s32[2]{0:T(128)S(1)}, s32[2]{0:T(128)}, u32[]{:S(2)}) copy-start(s32[2]{0:T(128)} %skip_blocks.1) | copy-start | bytes 28
  47.7 9.5 %copy-start.1 = (bf16[1152,128]{1,0:T(8,128)(2,1)S(1)}, bf16[1152,128]{1,0:T(8,128)(2,1)}, u32[]{:S(2)}) copy-start(bf16[1152,128]{1,0:T(8,128)(2,1)} %get-tuple-element.21.refs_3_) | copy-start | bytes 884740
  47.7 9.5 %copy-start.4 = (s32[2]{0:T(128)S(1)}, s32[2]{0:T(128)}, u32[]{:S(2)}) copy-start(s32[2]{0:T(128)} %refs_1_.5) | copy-start | bytes 28
  50.5 50.9 %collective-permute-start.16 = (bf16[4,1024,128]{2,1,0:T(8,128)(2,1)}, bf16[4,1024,128]{2,1,0:T(8,128)(2,1)S(1)}, u32[]{:S(2)}, u32[]{:S(2)}) collective-permute-start(bf16[4,1024,128]{2,1,0:T(8,128)(2,1)} %get-tuple-element.35), channel_id=1, source_target_pairs={{0,128},{128,0},{1,129},{129,1},{2,130},{130,2},{3,131},{131,3},{4... | collective-permute-start | bytes 3145736 | tf_op jit(solution)/shard_map/ppermute | solution.py:362
  57.2 1.0 copy-start.3
  62.8 13.7 %collective-permute-start.7 = (bf16[800,128]{1,0:T(8,128)(2,1)S(1)}, bf16[800,128]{1,0:T(8,128)(2,1)S(1)}, u32[]{:S(2)}, u32[]{:S(2)}) collective-permute-start(bf16[800,128]{1,0:T(8,128)(2,1)S(1)} %shard_map.84), channel_id=1, source_target_pairs={{0,64},{16,80},{32,96},{48,112},{64,0},{80,16},{96,32},{112,48},{1... | collective-permute-start | bytes 614408 | tf_op jit(solution)/shard_map/ppermute | solution.py:335
  76.8 9.7 %collective-permute-start.9 = (bf16[768,128]{1,0:T(8,128)(2,1)S(1)}, bf16[768,128]{1,0:T(8,128)(2,1)S(1)}, u32[]{:S(2)}, u32[]{:S(2)}) collective-permute-start(bf16[768,128]{1,0:T(8,128)(2,1)S(1)} %shard_map.85.refs_0_), channel_id=1, source_target_pairs={{0,96},{16,112},{32,0},{48,16},{64,32},{80,48},{96,64},{112,80},{1... | collective-permute-start | bytes 589832 | tf_op jit(solution)/shard_map/ppermute | solution.py:335
  76.9 11.1 %collective-permute-start.11 = (bf16[768,128]{1,0:T(8,128)(2,1)S(1)}, bf16[768,128]{1,0:T(8,128)(2,1)S(1)}, u32[]{:S(2)}, u32[]{:S(2)}) collective-permute-start(bf16[768,128]{1,0:T(8,128)(2,1)S(1)} %shard_map.85.refs_0_), channel_id=1, source_target_pairs={{0,32},{16,48},{32,64},{48,80},{64,96},{80,112},{96,0},{112,16},{1... | collective-permute-start | bytes 589832 | tf_op jit(solution)/shard_map/ppermute | solution.py:335
  79.8 12.2 %collective-permute-start.14 = (bf16[768,128]{1,0:T(8,128)(2,1)S(1)}, bf16[768,128]{1,0:T(8,128)(2,1)S(1)}, u32[]{:S(2)}, u32[]{:S(2)}) collective-permute-start(bf16[768,128]{1,0:T(8,128)(2,1)S(1)} %shard_map.85.refs_0_), channel_id=1, source_target_pairs={{0,16},{16,32},{32,48},{48,64},{64,80},{80,96},{96,112},{112,0},{1... | collective-permute-start | bytes 589832 | tf_op jit(solution)/shard_map/ppermute | solution.py:335
  79.8 13.1 %collective-permute-start.8 = (bf16[768,128]{1,0:T(8,128)(2,1)S(1)}, bf16[768,128]{1,0:T(8,128)(2,1)S(1)}, u32[]{:S(2)}, u32[]{:S(2)}) collective-permute-start(bf16[768,128]{1,0:T(8,128)(2,1)S(1)} %shard_map.85.refs_0_), channel_id=1, source_target_pairs={{0,112},{16,0},{32,16},{48,32},{64,48},{80,64},{96,80},{112,96},{1... | collective-permute-start | bytes 589832 | tf_op jit(solution)/shard_map/ppermute | solution.py:335
  86.5 14.8 %collective-permute-start.10 = (bf16[768,128]{1,0:T(8,128)(2,1)S(1)}, bf16[768,128]{1,0:T(8,128)(2,1)S(1)}, u32[]{:S(2)}, u32[]{:S(2)}) collective-permute-start(bf16[768,128]{1,0:T(8,128)(2,1)S(1)} %collective-permute-done.9.refs_2_), channel_id=1, source_target_pairs={{0,112},{16,0},{32,16},{48,32},{64,48},{80,64},{96,80},{112,96},{1... | collective-permute-start | bytes 589832 | tf_op jit(solution)/shard_map/ppermute | solution.py:335
  87.9 13.4 %collective-permute-start.13 = (bf16[768,128]{1,0:T(8,128)(2,1)S(1)}, bf16[768,128]{1,0:T(8,128)(2,1)S(1)}, u32[]{:S(2)}, u32[]{:S(2)}) collective-permute-start(bf16[768,128]{1,0:T(8,128)(2,1)S(1)} %collective-permute-done.11.refs_6_), channel_id=1, source_target_pairs={{0,16},{16,32},{32,48},{48,64},{64,80},{80,96},{96,112},{112,0},{1... | collective-permute-start | bytes 589832 | tf_op jit(solution)/shard_map/ppermute | solution.py:335
  92.0 9.3 %collective-permute-start.12 = (bf16[384,128]{1,0:T(8,128)(2,1)S(1)}, bf16[384,128]{1,0:T(8,128)(2,1)S(1)}, u32[]{:S(2)}, u32[]{:S(2)}) collective-permute-start(bf16[384,128]{1,0:T(8,128)(2,1)S(1)} %slice.8), channel_id=1, source_target_pairs={{0,32},{16,48},{32,64},{48,80},{64,96},{80,112},{96,0},{112,16},{1... | collective-permute-start | bytes 294920 | tf_op jit(solution)/shard_map/ppermute | solution.py:335
  92.9 8.4 %collective-permute-start.15 = (bf16[384,128]{1,0:T(8,128)(2,1)S(1)}, bf16[384,128]{1,0:T(8,128)(2,1)S(1)}, u32[]{:S(2)}, u32[]{:S(2)}) collective-permute-start(bf16[384,128]{1,0:T(8,128)(2,1)S(1)} %slice.9), channel_id=1, source_target_pairs={{0,96},{16,112},{32,0},{48,16},{64,32},{80,48},{96,64},{112,80},{1... | collective-permute-start | bytes 294920 | tf_op jit(solution)/shard_map/ppermute | solution.py:335
  103.6 2.4 %collective-permute-start.17 = (bf16[2,384,512]{2,1,0:T(8,128)(2,1)S(1)}, bf16[2,384,512]{2,1,0:T(8,128)(2,1)S(1)}, u32[]{:S(2)}, u32[]{:S(2)}) collective-permute-start(bf16[2,384,512]{2,1,0:T(8,128)(2,1)S(1)} %get-tuple-element.30), channel_id=1, source_target_pairs={{0,4},{4,0},{1,5},{5,1},{2,6},{6,2},{3,7},{7,3},{8,12},{12,8},{9,1... | collective-permute-start | bytes 2359304 | tf_op jit(solution)/shard_map/ppermute | solution.py:381
  106.2 9.2 %collective-permute-start.18 = (bf16[256,512]{1,0:T(8,128)(2,1)S(1)}, bf16[256,512]{1,0:T(8,128)(2,1)S(1)}, u32[]{:S(2)}, u32[]{:S(2)}) collective-permute-start(bf16[256,512]{1,0:T(8,128)(2,1)S(1)} %get-tuple-element.32), channel_id=1, source_target_pairs={{0,8},{8,0},{1,9},{9,1},{2,10},{10,2},{3,11},{11,3},{4,12},{12,4},... | collective-permute-start | bytes 786440 | tf_op jit(solution)/shard_map/ppermute | solution.py:385
  107.0 16.0 %collective-permute-start.19 = (bf16[256,512]{1,0:T(8,128)(2,1)S(1)}, bf16[256,512]{1,0:T(8,128)(2,1)S(1)}, u32[]{:S(2)}, u32[]{:S(2)}) collective-permute-start(bf16[256,512]{1,0:T(8,128)(2,1)S(1)} %get-tuple-element.33), channel_id=1, source_target_pairs={{0,128},{128,0},{1,129},{129,1},{2,130},{130,2},{3,131},{131,3},{4... | collective-permute-start | bytes 786440 | tf_op jit(solution)/shard_map/ppermute | solution.py:383
  110.9 14.6 %collective-permute-start.20 = (bf16[256,512]{1,0:T(8,128)(2,1)S(1)}, bf16[256,512]{1,0:T(8,128)(2,1)S(1)}, u32[]{:S(2)}, u32[]{:S(2)}) collective-permute-start(bf16[256,512]{1,0:T(8,128)(2,1)S(1)} %get-tuple-element.34), channel_id=1, source_target_pairs={{0,136},{8,128},{128,8},{136,0},{1,137},{9,129},{129,9},{137,1},{2... | collective-permute-start | bytes 786440 | tf_op jit(solution)/shard_map/ppermute | solution.py:384
Sparse Core Ops, SparseCore 0:
  9.2 35.3 all-gather.2

commit v3 on v2

--- a/solution.py
+++ b/solution.py
@@ -248,58 +248,63 @@
     )(mine, own_level, message)
 
 
-def project_kernel(*refs):
-    attended = refs[:9]
-    kept_half, got_half, kept, sent, gathered = refs[9:]
+def project_kernel(first, *refs):
     ring, core = location()["z"], location()["co"]
-    for distance in range(8):
-        columns = columns_of(lax.rem(ring + distance, 8))
-        if distance == 4:
-            gathered[:384, columns] = attended[4][...]
-            gathered[384:, columns] = attended[8][...]
-        else:
-            gathered[:, columns] = attended[distance][...]
+    if first:
+        attended, (weights, gathered, kept, sent) = refs[:9], refs[9:]
+        for distance in range(8):
+            columns = columns_of(lax.rem(ring + distance, 8))
+            if distance == 4:
+                gathered[:384, columns] = attended[4][...]
+                gathered[384:, columns] = attended[8][...]
+            else:
+                gathered[:, columns] = attended[distance][...]
+    else:
+        gathered, weights, kept, sent = refs
     for target, owner in ((sent, 1 - core), (kept, core)):
         rows = gathered[pl.ds(pl.multiple_of(owner * 384, 128), 384), :]
-        for side, weights in enumerate((kept_half, got_half)):
-            for pair in range(2):
-                block = jnp.concatenate([weights[2 * pair], weights[2 * pair + 1]], axis=1)
-                target[side, :, 256 * pair : 256 * (pair + 1)] = jnp.dot(
-                    rows, block, preferred_element_type=jnp.float32
-                ).astype(target.dtype)
-
-
-def project(attended, kept_half, got_half):
-    return pl.pallas_call(
-        project_kernel,
+        for pair in range(2):
+            block = jnp.concatenate([weights[2 * pair], weights[2 * pair + 1]], axis=1)
+            target[:, 256 * pair : 256 * (pair + 1)] = jnp.dot(
+                rows, block, preferred_element_type=jnp.float32
+            ).astype(target.dtype)
+
+
+def project(arrays, weights, first):
+    kept = jax.ShapeDtypeStruct((384, 512), jnp.float32)
+    sent = jax.ShapeDtypeStruct((384, 512), jnp.bfloat16)
+    gathered = jax.ShapeDtypeStruct((768, 1024), jnp.bfloat16)
+    out_shape = (gathered, kept, sent) if first else (kept, sent)
+    return pl.pallas_call(
+        lambda *refs: project_kernel(first, *refs),
+        out_shape=out_shape,
+        in_specs=[VMEM] * (len(arrays) + 1),
+        out_specs=(VMEM,) * len(out_shape),
+        compiler_params=PARAMS,
+        cost_estimate=pl.CostEstimate(
+            flops=2 * 10**9, bytes_accessed=4 * 2**20, transcendentals=0
+        ),
+    )(*arrays, weights)
+
+
+def add_kernel(kept, arrived, same, opposite):
+    low = location()["yl"]
+    total = kept[...] + arrived[...].astype(jnp.float32)
+    pair = total[:256]
+    single = jnp.concatenate([total[256:], jnp.zeros((128, 512), jnp.float32)], axis=0)
+    same[...] = jnp.where(low == 0, pair, single).astype(same.dtype)
+    opposite[...] = jnp.where(low == 0, single, pair).astype(opposite.dtype)
+
+
+def add_cores(kept, arrived, dtype):
+    return pl.pallas_call(
+        add_kernel,
         out_shape=(
-            jax.ShapeDtypeStruct((2, 384, 512), jnp.float32),
-            jax.ShapeDtypeStruct((2, 384, 512), jnp.bfloat16),
+            jax.ShapeDtypeStruct((256, 512), dtype),
+            jax.ShapeDtypeStruct((256, 512), jnp.bfloat16),
         ),
-        in_specs=[VMEM] * 11,
-        out_specs=(VMEM, VMEM),
-        scratch_shapes=[pltpu.VMEM((768, 1024), jnp.bfloat16)],
-        compiler_params=PARAMS,
-    )(*attended, kept_half, got_half)
-
-
-def add_kernel(kept, arrived, mine, near, far, cross):
-    low = location()["yl"]
-    for side, targets in ((0, (mine, near)), (1, (far, cross))):
-        total = kept[side] + arrived[side].astype(jnp.float32)
-        pair = total[:256]
-        single = jnp.concatenate([total[256:], jnp.zeros((128, 512), jnp.float32)], axis=0)
-        targets[0][...] = jnp.where(low == 0, pair, single).astype(targets[0].dtype)
-        targets[1][...] = jnp.where(low == 0, single, pair).astype(targets[1].dtype)
-
-
-def add_cores(kept, arrived):
-    shape = jax.ShapeDtypeStruct((256, 512), jnp.bfloat16)
-    return pl.pallas_call(
-        add_kernel,
-        out_shape=(jax.ShapeDtypeStruct((256, 512), jnp.float32), shape, shape, shape),
         in_specs=[VMEM, VMEM],
-        out_specs=(VMEM,) * 4,
+        out_specs=(VMEM,) * 2,
         compiler_params=PARAMS,
     )(kept, arrived)
 
@@ -377,9 +382,13 @@
         from_below,
         ring_send(two_above[384:], -2),
     ]
-    kept, sent = project(gathered, kept_half, got_half)
+    joined, kept, sent = project(gathered, got_half, True)
     arrived = lax.ppermute(sent, "co", SWAP)
-    mine, near, far, cross = add_cores(kept, arrived)
+    far, cross = add_cores(kept, arrived, jnp.bfloat16)
+    joined, far = lax.optimization_barrier((joined, far))
+    kept, sent = project([joined], kept_half, False)
+    arrived = lax.ppermute(sent, "co", SWAP)
+    mine, near = add_cores(kept, arrived, jnp.float32)
     far = lax.ppermute(far, "yh", SWAP)
     cross = lax.ppermute(cross, ("yh", "yl"), [(0, 3), (1, 2), (2, 1), (3, 0)])
     near = lax.ppermute(near, "yl", SWAP)

time: 134 us -> 131 us (0.978)
  waiting for transfers between devices: 53.2 us -> 50.2 us
    ppermute x1, waiting for transfers between devices: 4.45 us -> 0.44 us  [on_device(): near = lax.ppermute(near, 'yl', SWAP)]
    ppermute x1, waiting for transfers between devices: 2.57 us -> 5.09 us  [on_device(): cross = lax.ppermute(cross, ('yh', 'yl'), [(0, 3), (1, 2), (2, 1), (3, 0)])]
  transfers between devices with their start and end apart: 23 -> 24, of which waited for: 12 -> 12; matrix products, arithmetic and copies ran while one was open for 2% -> 2% of each run, Pallas kernels for 7% -> 7%
where the time goes in v3:
time: 131 us
  waiting for transfers between devices  50.2 us (38%)
  starting transfers between devices  46.2 us (35%)
  Pallas kernels  16.2 us (12%)
  between operations  13.5 us (10%)
  local copies, waits for them, and re-layouts  4.42 us (3%)
    ppermute x15, waiting for transfers between devices, ring_send(): lax.ppermute(array, 'z', [(index, (index + hops) % 8) for index in range(...  27.2 us
    ppermute x15, starting transfers between devices, ring_send(): lax.ppermute(array, 'z', [(index, (index + hops) % 8) for index in range(...  24.2 us
    all_to_all x1, starting transfers between devices, on_device(): lax.all_to_all(split_queries, ('yh', 'z'), split_axis=0, concat_axis=0, t...  11.2 us
    pallas_call x2, Pallas kernels, attend(): pl.pallas_call(lambda *refs: attend_kernel(offsets, head, *refs), out_sha...  9.28 us
    ppermute x1, waiting for transfers between devices, on_device(): partner = lax.ppermute(other, 'yh', SWAP)  9.19 us
    ppermute x1, waiting for transfers between devices, on_device(): far = lax.ppermute(far, 'yh', SWAP)  6.47 us
    ppermute x1, waiting for transfers between devices, on_device(): cross = lax.ppermute(cross, ('yh', 'yl'), [(0, 3), (1, 2), (2, 1), (3, 0)])  5.09 us
    ppermute x1, starting transfers between devices, on_device(): partner = lax.ppermute(other, 'yh', SWAP)  3.43 us
  transfers between devices with their start and end apart: 24, of which 12 were waited for; matrix products, arithmetic and copies ran while one was open for 2% of the time, Pallas kernels for 7%

profile of v3, /device:TPU:2, one launch (start us, length us, event | category | flops | bytes accessed | tf_op | source)
XLA Modules:
  0.0 130.6 jit_solution(8513664204561698055)
XLA Ops:
  6.5 2.5 %shard_map.82 = (bf16[1152,128]{1,0:T(8,128)(2,1)}, bf16[1152,128]{1,0:T(8,128)(2,1)}, bf16[16,2,64,128]{3,2,1,0:T(8,128)(2,1)}) custom-call(bf16[2,256,256]{2,1,0:T(8,128)(2,1)} %refs_0_.3, bf16[2,256,256]{2,1,0:T(8,128)(2,1)} %refs_1_.3, bf16[32,2,256]{2,1,0:T(2,128)(2,1)} %refs_2_.1, bf16[32,2,256]{2,1,0:T(2,128)(2,1)} %refs_3_.1, ...), custom_call_target="tpu_custom_call" | custom-call | tf_op jit(solution)/shard_map/pallas_call | solution.py:58
  9.0 11.2 %all-to-all-start = ((bf16[16,2,64,128]{3,2,1,0:T(8,128)(2,1)}), bf16[16,2,64,128]{3,2,1,0:T(8,128)(2,1)S(1)}, u32[]{:S(2)}, u32[]{:S(2)}) async-start(bf16[16,2,64,128]{3,2,1,0:T(8,128)(2,1)} %get-tuple-element.25), calls=%async_computation | async-start | bytes 1048576 | tf_op jit(solution)/shard_map/all_to_all | solution.py:351
  20.3 3.4 %collective-permute-start = (bf16[1152,128]{1,0:T(8,128)(2,1)}, bf16[1152,128]{1,0:T(8,128)(2,1)S(1)}, u32[]{:S(2)}, u32[]{:S(2)}) collective-permute-start(bf16[1152,128]{1,0:T(8,128)(2,1)} %get-tuple-element.27), channel_id=1, source_target_pairs={{0,128},{128,0},{1,129},{129,1},{2,130},{130,2},{3,131},{131,3},{4... | collective-permute-start | bytes 884744 | tf_op jit(solution)/shard_map/ppermute | solution.py:349
  23.7 2.7 %collective-permute-start.3 = (bf16[1152,128]{1,0:T(8,128)(2,1)}, bf16[1152,128]{1,0:T(8,128)(2,1)S(1)}, u32[]{:S(2)}, u32[]{:S(2)}) collective-permute-start(bf16[1152,128]{1,0:T(8,128)(2,1)} %get-tuple-element.26.refs_3_), channel_id=1, source_target_pairs={{0,112},{16,0},{32,16},{48,32},{64,48},{80,64},{96,80},{112,96},{1... | collective-permute-start | bytes 884744 | tf_op jit(solution)/shard_map/ppermute | solution.py:340
  26.4 9.2 %collective-permute-done.refs_4_ = bf16[1152,128]{1,0:T(8,128)(2,1)S(1)} collective-permute-done((bf16[1152,128]{1,0:T(8,128)(2,1)}, bf16[1152,128]{1,0:T(8,128)(2,1)S(1)}, u32[]{:S(2)}, u32[]{:S(2)}) %collective-permute-start) | collective-permute-done | bytes 294944 | tf_op jit(solution)/shard_map/ppermute | solution.py:349
  35.6 1.1 collective-permute-start.1
  36.7 2.1 %collective-permute-start.5 = (bf16[1152,128]{1,0:T(8,128)(2,1)S(1)}, bf16[1152,128]{1,0:T(8,128)(2,1)}, u32[]{:S(2)}, u32[]{:S(2)}) collective-permute-start(bf16[1152,128]{1,0:T(8,128)(2,1)S(1)} %collective-permute-done.refs_4_), channel_id=1, source_target_pairs={{0,112},{16,0},{32,16},{48,32},{64,48},{80,64},{96,80},{112,96},{1... | collective-permute-start | bytes 884744 | tf_op jit(solution)/shard_map/ppermute | solution.py:340
  38.8 2.3 %collective-permute-done.3.refs_6_ = bf16[1152,128]{1,0:T(8,128)(2,1)S(1)} collective-permute-done((bf16[1152,128]{1,0:T(8,128)(2,1)}, bf16[1152,128]{1,0:T(8,128)(2,1)S(1)}, u32[]{:S(2)}, u32[]{:S(2)}) %collective-permute-start.3) | collective-permute-done | bytes 294944 | tf_op jit(solution)/shard_map/ppermute | solution.py:340
  41.1 1.6 %collective-permute-start.4 = (bf16[1152,128]{1,0:T(8,128)(2,1)S(1)}, bf16[1152,128]{1,0:T(8,128)(2,1)}, u32[]{:S(2)}, u32[]{:S(2)}) collective-permute-start(bf16[1152,128]{1,0:T(8,128)(2,1)S(1)} %collective-permute-done.3.refs_6_), channel_id=1, source_target_pairs={{0,112},{16,0},{32,16},{48,32},{64,48},{80,64},{96,80},{112,96},{1... | collective-permute-start | bytes 884744 | tf_op jit(solution)/shard_map/ppermute | solution.py:340
  43.4 4.3 %collective-permute-done.1.refs_8_ = bf16[1152,128]{1,0:T(8,128)(2,1)} collective-permute-done((bf16[1152,128]{1,0:T(8,128)(2,1)S(1)}, bf16[1152,128]{1,0:T(8,128)(2,1)}, u32[]{:S(2)}, u32[]{:S(2)}) %collective-permute-start.1) | collective-permute-done | bytes 294944 | tf_op jit(solution)/shard_map/ppermute | solution.py:340
  47.7 2.7 %constant_dynamic-slice_fusion = (bf16[4,1024,128]{2,1,0:T(8,128)(2,1)S(1)}, bf16[4,1024,128]{2,1,0:T(8,128)(2,1)}) fusion(bf16[4,2048,128]{2,1,0:T(8,128)(2,1)} %bitcast.1, s32[]{:T(128)S(6)} %select_n.7, s32[]{:T(128)S(6)} %select_n.6), kind=kLoop, calls=%fused_computation | loop fusion | bytes 4194312 | tf_op jit(solution)/shard_map/dynamic_slice | solution.py:366
  50.4 3.0 %collective-permute-start.16 = (bf16[4,1024,128]{2,1,0:T(8,128)(2,1)}, bf16[4,1024,128]{2,1,0:T(8,128)(2,1)S(1)}, u32[]{:S(2)}, u32[]{:S(2)}) collective-permute-start(bf16[4,1024,128]{2,1,0:T(8,128)(2,1)} %get-tuple-element.46), channel_id=1, source_target_pairs={{0,128},{128,0},{1,129},{129,1},{2,130},{130,2},{3,131},{131,3},{4... | collective-permute-start | bytes 3145736 | tf_op jit(solution)/shard_map/ppermute | solution.py:367
  53.4 3.8 %collective-permute-done.6.refs_10_ = bf16[1152,128]{1,0:T(8,128)(2,1)} collective-permute-done((bf16[1152,128]{1,0:T(8,128)(2,1)}, bf16[1152,128]{1,0:T(8,128)(2,1)}, u32[]{:S(2)}, u32[]{:S(2)}) %collective-permute-start.6) | collective-permute-done | bytes 294944 | tf_op jit(solution)/shard_map/ppermute | solution.py:340
  58.2 4.7 %shard_map.84 = bf16[800,128]{1,0:T(8,128)(2,1)S(1)} custom-call(s32[2]{0:T(128)S(1)} %copy-done, s32[2]{0:T(128)S(1)} %copy-done.4, bf16[16,2,64,128]{3,2,1,0:T(8,128)(2,1)S(1)} %all-to-all-done.refs_2_, bf16[1152,128]{1,0:T(8,128)(2,1)S(1)} %copy-done.1, bf16[1152,128]{1,0:T(8,128)(2,1)S(1)} %collective-permute-done.refs_4_, ...), custom_call_target="tpu_custom_call" | custom-call | flops 5000000000 | bytes 6291456 | tf_op jit(solution)/shard_map/pallas_call | solution.py:208
  62.8 2.8 %collective-permute-start.7 = (bf16[800,128]{1,0:T(8,128)(2,1)S(1)}, bf16[800,128]{1,0:T(8,128)(2,1)S(1)}, u32[]{:S(2)}, u32[]{:S(2)}) collective-permute-start(bf16[800,128]{1,0:T(8,128)(2,1)S(1)} %shard_map.84), channel_id=1, source_target_pairs={{0,64},{16,80},{32,96},{48,112},{64,0},{80,16},{96,32},{112,48},{1... | collective-permute-start | bytes 614408 | tf_op jit(solution)/shard_map/ppermute | solution.py:340
  65.7 4.6 %shard_map.83 = (f32[768,128]{1,0:T(8,128)S(1)}, f32[768,128]{1,0:T(8,128)S(1)}) custom-call(s32[2]{0:T(128)S(1)} %copy-done, s32[2]{0:T(128)S(1)} %copy-done.4, bf16[16,2,64,128]{3,2,1,0:T(8,128)(2,1)S(1)} %all-to-all-done.refs_2_, bf16[1152,128]{1,0:T(8,128)(2,1)S(1)} %copy-done.1, bf16[1152,128]{1,0:T(8,128)(2,1)S(1)} %collective-permute-done.refs_4_, ...), custom_call_target="tpu_custom_call" | custom-call | flops 5000000000 | bytes 6291456 | tf_op jit(solution)/shard_map/pallas_call | solution.py:208
  70.3 6.2 %collective-permute-done.7.message = bf16[800,128]{1,0:T(8,128)(2,1)S(1)} collective-permute-done((bf16[800,128]{1,0:T(8,128)(2,1)S(1)}, bf16[800,128]{1,0:T(8,128)(2,1)S(1)}, u32[]{:S(2)}, u32[]{:S(2)}) %collective-permute-start.7) | collective-permute-done | bytes 204832 | tf_op jit(solution)/shard_map/ppermute | solution.py:340
  76.9 2.9 %collective-permute-start.11 = (bf16[768,128]{1,0:T(8,128)(2,1)S(1)}, bf16[768,128]{1,0:T(8,128)(2,1)S(1)}, u32[]{:S(2)}, u32[]{:S(2)}) collective-permute-start(bf16[768,128]{1,0:T(8,128)(2,1)S(1)} %shard_map.85.refs_0_), channel_id=1, source_target_pairs={{0,32},{16,48},{32,64},{48,80},{64,96},{80,112},{96,0},{112,16},{1... | collective-permute-start | bytes 589832 | tf_op jit(solution)/shard_map/ppermute | solution.py:340
  79.8 3.2 %collective-permute-start.8 = (bf16[768,128]{1,0:T(8,128)(2,1)S(1)}, bf16[768,128]{1,0:T(8,128)(2,1)S(1)}, u32[]{:S(2)}, u32[]{:S(2)}) collective-permute-start(bf16[768,128]{1,0:T(8,128)(2,1)S(1)} %shard_map.85.refs_0_), channel_id=1, source_target_pairs={{0,112},{16,0},{32,16},{48,32},{64,48},{80,64},{96,80},{112,96},{1... | collective-permute-start | bytes 589832 | tf_op jit(solution)/shard_map/ppermute | solution.py:340
  83.0 3.5 %collective-permute-done.9.refs_2_ = bf16[768,128]{1,0:T(8,128)(2,1)S(1)} collective-permute-done((bf16[768,128]{1,0:T(8,128)(2,1)S(1)}, bf16[768,128]{1,0:T(8,128)(2,1)S(1)}, u32[]{:S(2)}, u32[]{:S(2)}) %collective-permute-start.9) | collective-permute-done | bytes 196640 | tf_op jit(solution)/shard_map/ppermute | solution.py:340
  86.5 1.4 %collective-permute-start.10 = (bf16[768,128]{1,0:T(8,128)(2,1)S(1)}, bf16[768,128]{1,0:T(8,128)(2,1)S(1)}, u32[]{:S(2)}, u32[]{:S(2)}) collective-permute-start(bf16[768,128]{1,0:T(8,128)(2,1)S(1)} %collective-permute-done.9.refs_2_), channel_id=1, source_target_pairs={{0,112},{16,0},{32,16},{48,32},{64,48},{80,64},{96,80},{112,96},{1... | collective-permute-start | bytes 589832 | tf_op jit(solution)/shard_map/ppermute | solution.py:340
  88.0 2.0 %collective-permute-start.13 = (bf16[768,128]{1,0:T(8,128)(2,1)S(1)}, bf16[768,128]{1,0:T(8,128)(2,1)S(1)}, u32[]{:S(2)}, u32[]{:S(2)}) collective-permute-start(bf16[768,128]{1,0:T(8,128)(2,1)S(1)} %collective-permute-done.11.refs_6_), channel_id=1, source_target_pairs={{0,16},{16,32},{32,48},{48,64},{64,80},{80,96},{96,112},{112,0},{1... | collective-permute-start | bytes 589832 | tf_op jit(solution)/shard_map/ppermute | solution.py:340
  90.0 1.9 %collective-permute-done.14.refs_7_ = bf16[768,128]{1,0:T(8,128)(2,1)S(1)} collective-permute-done((bf16[768,128]{1,0:T(8,128)(2,1)S(1)}, bf16[768,128]{1,0:T(8,128)(2,1)S(1)}, u32[]{:S(2)}, u32[]{:S(2)}) %collective-permute-start.14) | collective-permute-done | bytes 196640 | tf_op jit(solution)/shard_map/ppermute | solution.py:340
  92.9 3.2 %collective-permute-start.15 = (bf16[384,128]{1,0:T(8,128)(2,1)S(1)}, bf16[384,128]{1,0:T(8,128)(2,1)S(1)}, u32[]{:S(2)}, u32[]{:S(2)}) collective-permute-start(bf16[384,128]{1,0:T(8,128)(2,1)S(1)} %slice.9), channel_id=1, source_target_pairs={{0,96},{16,112},{32,0},{48,16},{64,32},{80,48},{96,64},{112,80},{1... | collective-permute-start | bytes 294920 | tf_op jit(solution)/shard_map/ppermute | solution.py:340
  96.1 5.2 %collective-permute-done.12.refs_4_ = bf16[384,128]{1,0:T(8,128)(2,1)S(1)} collective-permute-done((bf16[384,128]{1,0:T(8,128)(2,1)S(1)}, bf16[384,128]{1,0:T(8,128)(2,1)S(1)}, u32[]{:S(2)}, u32[]{:S(2)}) %collective-permute-start.12) | collective-permute-done | bytes 98336 | tf_op jit(solution)/shard_map/ppermute | solution.py:340
  101.3 1.5 %shard_map.86 = (bf16[768,1024]{1,0:T(8,128)(2,1)S(1)}, f32[384,512]{1,0:T(8,128)S(1)}, bf16[384,512]{1,0:T(8,128)(2,1)S(1)}) custom-call(bf16[768,128]{1,0:T(8,128)(2,1)S(1)} %shard_map.85.refs_0_, bf16[768,128]{1,0:T(8,128)(2,1)S(1)} %collective-permute-done.8.refs_1_, bf16[768,128]{1,0:T(8,128)(2,1)S(1)} %collective-permute-done.9.refs_2_, ...), custom_call_target="tpu_custom_call" | custom-call | flops 2000000000 | bytes 4194304 | tf_op jit(solution)/shard_map/pallas_call | solution.py:278
  102.9 1.7 %collective-permute-done.17.arrived = bf16[384,512]{1,0:T(8,128)(2,1)S(1)} collective-permute-done((bf16[384,512]{1,0:T(8,128)(2,1)S(1)}, bf16[384,512]{1,0:T(8,128)(2,1)S(1)}, u32[]{:S(2)}, u32[]{:S(2)}) %collective-permute-start.17) | collective-permute-done | bytes 393248 | tf_op jit(solution)/shard_map/ppermute | solution.py:386
  104.7 1.0 shard_map.88
  106.0 3.3 %collective-permute-start.20 = (bf16[256,512]{1,0:T(8,128)(2,1)S(1)}, bf16[256,512]{1,0:T(8,128)(2,1)S(1)}, u32[]{:S(2)}, u32[]{:S(2)}) collective-permute-start(bf16[256,512]{1,0:T(8,128)(2,1)S(1)} %get-tuple-element.43), channel_id=1, source_target_pairs={{0,128},{128,0},{1,129},{129,1},{2,130},{130,2},{3,131},{131,3},{4... | collective-permute-start | bytes 786440 | tf_op jit(solution)/shard_map/ppermute | solution.py:392
  110.2 6.5 %collective-permute-done.20.far = bf16[256,512]{1,0:T(8,128)(2,1)S(1)} collective-permute-done((bf16[256,512]{1,0:T(8,128)(2,1)S(1)}, bf16[256,512]{1,0:T(8,128)(2,1)S(1)}, u32[]{:S(2)}, u32[]{:S(2)}) %collective-permute-start.20) | collective-permute-done | bytes 262176 | tf_op jit(solution)/shard_map/ppermute | solution.py:392
  116.6 5.1 %collective-permute-done.21.cross = bf16[256,512]{1,0:T(8,128)(2,1)S(1)} collective-permute-done((bf16[256,512]{1,0:T(8,128)(2,1)S(1)}, bf16[256,512]{1,0:T(8,128)(2,1)S(1)}, u32[]{:S(2)}, u32[]{:S(2)}) %collective-permute-start.21) | collective-permute-done | bytes 262176 | tf_op jit(solution)/shard_map/ppermute | solution.py:393
  122.2 1.6 %shard_map.90 = f32[128,2,512]{2,1,0:T(2,128)} custom-call(s32[2]{0:T(128)S(1)} %copy-done, f32[256,512]{1,0:T(8,128)S(1)} %get-tuple-element.41.mine, bf16[256,512]{1,0:T(8,128)(2,1)S(1)} %collective-permute-done.19.near, bf16[256,512]{1,0:T(8,128)(2,1)S(1)} %collective-permute-done.20.far, bf16[256,512]{1,0:T(8,128)(2,1)S(1)} %collective-permute-done.21.cross), custom_call_target="tpu_custom_call" | custom-call | tf_op jit(solution)/shard_map/pallas_call | solution.py:327
  (39 shorter events, 4.8 us)
Async XLA Ops:
  6.5 41.2 %all-gather.3.cloned.1.call-start = ((), (), s32[]{:S(2)}) async-start(), calls=%async_computation.1 | async-start | bytes 2621440 | tf_op jit(solution)/shard_map/all_gather | solution.py:363
  9.0 48.2 %all-to-all-start = ((bf16[16,2,64,128]{3,2,1,0:T(8,128)(2,1)}), bf16[16,2,64,128]{3,2,1,0:T(8,128)(2,1)S(1)}, u32[]{:S(2)}, u32[]{:S(2)}) async-start(bf16[16,2,64,128]{3,2,1,0:T(8,128)(2,1)} %get-tuple-element.25), calls=%async_computation | async-start | bytes 1048576 | tf_op jit(solution)/shard_map/all_to_all | solution.py:351
  20.3 15.3 %collective-permute-start = (bf16[1152,128]{1,0:T(8,128)(2,1)}, bf16[1152,128]{1,0:T(8,128)(2,1)S(1)}, u32[]{:S(2)}, u32[]{:S(2)}) collective-permute-start(bf16[1152,128]{1,0:T(8,128)(2,1)} %get-tuple-element.27), channel_id=1, source_target_pairs={{0,128},{128,0},{1,129},{129,1},{2,130},{130,2},{3,131},{131,3},{4... | collective-permute-start | bytes 884744 | tf_op jit(solution)/shard_map/ppermute | solution.py:349
  23.7 17.4 %collective-permute-start.3 = (bf16[1152,128]{1,0:T(8,128)(2,1)}, bf16[1152,128]{1,0:T(8,128)(2,1)S(1)}, u32[]{:S(2)}, u32[]{:S(2)}) collective-permute-start(bf16[1152,128]{1,0:T(8,128)(2,1)} %get-tuple-element.26.refs_3_), channel_id=1, source_target_pairs={{0,112},{16,0},{32,16},{48,32},{64,48},{80,64},{96,80},{112,96},{1... | collective-permute-start | bytes 884744 | tf_op jit(solution)/shard_map/ppermute | solution.py:340
  26.4 16.3 %collective-permute-start.2 = (bf16[1152,128]{1,0:T(8,128)(2,1)}, bf16[1152,128]{1,0:T(8,128)(2,1)S(1)}, u32[]{:S(2)}, u32[]{:S(2)}) collective-permute-start(bf16[1152,128]{1,0:T(8,128)(2,1)} %get-tuple-element.26.refs_3_), channel_id=1, source_target_pairs={{0,16},{16,32},{32,48},{48,64},{64,80},{80,96},{96,112},{112,0},{1... | collective-permute-start | bytes 884744 | tf_op jit(solution)/shard_map/ppermute | solution.py:340
  35.6 12.1 %collective-permute-start.1 = (bf16[1152,128]{1,0:T(8,128)(2,1)S(1)}, bf16[1152,128]{1,0:T(8,128)(2,1)}, u32[]{:S(2)}, u32[]{:S(2)}) collective-permute-start(bf16[1152,128]{1,0:T(8,128)(2,1)S(1)} %collective-permute-done.refs_4_), channel_id=1, source_target_pairs={{0,16},{16,32},{32,48},{48,64},{64,80},{80,96},{96,112},{112,0},{1... | collective-permute-start | bytes 884744 | tf_op jit(solution)/shard_map/ppermute | solution.py:340
  36.7 16.7 %collective-permute-start.5 = (bf16[1152,128]{1,0:T(8,128)(2,1)S(1)}, bf16[1152,128]{1,0:T(8,128)(2,1)}, u32[]{:S(2)}, u32[]{:S(2)}) collective-permute-start(bf16[1152,128]{1,0:T(8,128)(2,1)S(1)} %collective-permute-done.refs_4_), channel_id=1, source_target_pairs={{0,112},{16,0},{32,16},{48,32},{64,48},{80,64},{96,80},{112,96},{1... | collective-permute-start | bytes 884744 | tf_op jit(solution)/shard_map/ppermute | solution.py:340
  41.1 12.3 %collective-permute-start.4 = (bf16[1152,128]{1,0:T(8,128)(2,1)S(1)}, bf16[1152,128]{1,0:T(8,128)(2,1)}, u32[]{:S(2)}, u32[]{:S(2)}) collective-permute-start(bf16[1152,128]{1,0:T(8,128)(2,1)S(1)} %collective-permute-done.3.refs_6_), channel_id=1, source_target_pairs={{0,112},{16,0},{32,16},{48,32},{64,48},{80,64},{96,80},{112,96},{1... | collective-permute-start | bytes 884744 | tf_op jit(solution)/shard_map/ppermute | solution.py:340
  42.7 0.7 copy-start.2
  47.7 9.5 %collective-permute-start.6 = (bf16[1152,128]{1,0:T(8,128)(2,1)}, bf16[1152,128]{1,0:T(8,128)(2,1)}, u32[]{:S(2)}, u32[]{:S(2)}) collective-permute-start(bf16[1152,128]{1,0:T(8,128)(2,1)} %collective-permute-done.1.refs_8_), channel_id=1, source_target_pairs={{0,16},{16,32},{32,48},{48,64},{64,80},{80,96},{96,112},{112,0},{1... | collective-permute-start | bytes 884744 | tf_op jit(solution)/shard_map/ppermute | solution.py:340
  47.7 9.5 %copy-start = (s32[2]{0:T(128)S(1)}, s32[2]{0:T(128)}, u32[]{:S(2)}) copy-start(s32[2]{0:T(128)} %skip_blocks.1) | copy-start | bytes 28
  47.7 9.5 %copy-start.1 = (bf16[1152,128]{1,0:T(8,128)(2,1)S(1)}, bf16[1152,128]{1,0:T(8,128)(2,1)}, u32[]{:S(2)}) copy-start(bf16[1152,128]{1,0:T(8,128)(2,1)} %get-tuple-element.26.refs_3_) | copy-start | bytes 884740
  47.7 9.5 %copy-start.4 = (s32[2]{0:T(128)S(1)}, s32[2]{0:T(128)}, u32[]{:S(2)}) copy-start(s32[2]{0:T(128)} %refs_1_.5) | copy-start | bytes 28
  50.4 50.9 %collective-permute-start.16 = (bf16[4,1024,128]{2,1,0:T(8,128)(2,1)}, bf16[4,1024,128]{2,1,0:T(8,128)(2,1)S(1)}, u32[]{:S(2)}, u32[]{:S(2)}) collective-permute-start(bf16[4,1024,128]{2,1,0:T(8,128)(2,1)} %get-tuple-element.46), channel_id=1, source_target_pairs={{0,128},{128,0},{1,129},{129,1},{2,130},{130,2},{3,131},{131,3},{4... | collective-permute-start | bytes 3145736 | tf_op jit(solution)/shard_map/ppermute | solution.py:367
  57.2 1.0 copy-start.3
  62.8 13.7 %collective-permute-start.7 = (bf16[800,128]{1,0:T(8,128)(2,1)S(1)}, bf16[800,128]{1,0:T(8,128)(2,1)S(1)}, u32[]{:S(2)}, u32[]{:S(2)}) collective-permute-start(bf16[800,128]{1,0:T(8,128)(2,1)S(1)} %shard_map.84), channel_id=1, source_target_pairs={{0,64},{16,80},{32,96},{48,112},{64,0},{80,16},{96,32},{112,48},{1... | collective-permute-start | bytes 614408 | tf_op jit(solution)/shard_map/ppermute | solution.py:340
  76.8 9.7 %collective-permute-start.9 = (bf16[768,128]{1,0:T(8,128)(2,1)S(1)}, bf16[768,128]{1,0:T(8,128)(2,1)S(1)}, u32[]{:S(2)}, u32[]{:S(2)}) collective-permute-start(bf16[768,128]{1,0:T(8,128)(2,1)S(1)} %shard_map.85.refs_0_), channel_id=1, source_target_pairs={{0,96},{16,112},{32,0},{48,16},{64,32},{80,48},{96,64},{112,80},{1... | collective-permute-start | bytes 589832 | tf_op jit(solution)/shard_map/ppermute | solution.py:340
  76.9 11.1 %collective-permute-start.11 = (bf16[768,128]{1,0:T(8,128)(2,1)S(1)}, bf16[768,128]{1,0:T(8,128)(2,1)S(1)}, u32[]{:S(2)}, u32[]{:S(2)}) collective-permute-start(bf16[768,128]{1,0:T(8,128)(2,1)S(1)} %shard_map.85.refs_0_), channel_id=1, source_target_pairs={{0,32},{16,48},{32,64},{48,80},{64,96},{80,112},{96,0},{112,16},{1... | collective-permute-start | bytes 589832 | tf_op jit(solution)/shard_map/ppermute | solution.py:340
  79.8 12.2 %collective-permute-start.14 = (bf16[768,128]{1,0:T(8,128)(2,1)S(1)}, bf16[768,128]{1,0:T(8,128)(2,1)S(1)}, u32[]{:S(2)}, u32[]{:S(2)}) collective-permute-start(bf16[768,128]{1,0:T(8,128)(2,1)S(1)} %shard_map.85.refs_0_), channel_id=1, source_target_pairs={{0,16},{16,32},{32,48},{48,64},{64,80},{80,96},{96,112},{112,0},{1... | collective-permute-start | bytes 589832 | tf_op jit(solution)/shard_map/ppermute | solution.py:340
  79.8 13.1 %collective-permute-start.8 = (bf16[768,128]{1,0:T(8,128)(2,1)S(1)}, bf16[768,128]{1,0:T(8,128)(2,1)S(1)}, u32[]{:S(2)}, u32[]{:S(2)}) collective-permute-start(bf16[768,128]{1,0:T(8,128)(2,1)S(1)} %shard_map.85.refs_0_), channel_id=1, source_target_pairs={{0,112},{16,0},{32,16},{48,32},{64,48},{80,64},{96,80},{112,96},{1... | collective-permute-start | bytes 589832 | tf_op jit(solution)/shard_map/ppermute | solution.py:340
  86.5 14.8 %collective-permute-start.10 = (bf16[768,128]{1,0:T(8,128)(2,1)S(1)}, bf16[768,128]{1,0:T(8,128)(2,1)S(1)}, u32[]{:S(2)}, u32[]{:S(2)}) collective-permute-start(bf16[768,128]{1,0:T(8,128)(2,1)S(1)} %collective-permute-done.9.refs_2_), channel_id=1, source_target_pairs={{0,112},{16,0},{32,16},{48,32},{64,48},{80,64},{96,80},{112,96},{1... | collective-permute-start | bytes 589832 | tf_op jit(solution)/shard_map/ppermute | solution.py:340
  88.0 13.4 %collective-permute-start.13 = (bf16[768,128]{1,0:T(8,128)(2,1)S(1)}, bf16[768,128]{1,0:T(8,128)(2,1)S(1)}, u32[]{:S(2)}, u32[]{:S(2)}) collective-permute-start(bf16[768,128]{1,0:T(8,128)(2,1)S(1)} %collective-permute-done.11.refs_6_), channel_id=1, source_target_pairs={{0,16},{16,32},{32,48},{48,64},{64,80},{80,96},{96,112},{112,0},{1... | collective-permute-start | bytes 589832 | tf_op jit(solution)/shard_map/ppermute | solution.py:340
  92.0 9.3 %collective-permute-start.12 = (bf16[384,128]{1,0:T(8,128)(2,1)S(1)}, bf16[384,128]{1,0:T(8,128)(2,1)S(1)}, u32[]{:S(2)}, u32[]{:S(2)}) collective-permute-start(bf16[384,128]{1,0:T(8,128)(2,1)S(1)} %slice.8), channel_id=1, source_target_pairs={{0,32},{16,48},{32,64},{48,80},{64,96},{80,112},{96,0},{112,16},{1... | collective-permute-start | bytes 294920 | tf_op jit(solution)/shard_map/ppermute | solution.py:340
  92.9 8.4 %collective-permute-start.15 = (bf16[384,128]{1,0:T(8,128)(2,1)S(1)}, bf16[384,128]{1,0:T(8,128)(2,1)S(1)}, u32[]{:S(2)}, u32[]{:S(2)}) collective-permute-start(bf16[384,128]{1,0:T(8,128)(2,1)S(1)} %slice.9), channel_id=1, source_target_pairs={{0,96},{16,112},{32,0},{48,16},{64,32},{80,48},{96,64},{112,80},{1... | collective-permute-start | bytes 294920 | tf_op jit(solution)/shard_map/ppermute | solution.py:340
  102.8 1.8 %collective-permute-start.17 = (bf16[384,512]{1,0:T(8,128)(2,1)S(1)}, bf16[384,512]{1,0:T(8,128)(2,1)S(1)}, u32[]{:S(2)}, u32[]{:S(2)}) collective-permute-start(bf16[384,512]{1,0:T(8,128)(2,1)S(1)} %get-tuple-element.36), channel_id=1, source_target_pairs={{0,4},{4,0},{1,5},{5,1},{2,6},{6,2},{3,7},{7,3},{8,12},{12,8},{9,1... | collective-permute-start | bytes 1179656 | tf_op jit(solution)/shard_map/ppermute | solution.py:386
  105.7 3.6 %collective-permute-start.18 = (bf16[384,512]{1,0:T(8,128)(2,1)S(1)}, bf16[384,512]{1,0:T(8,128)(2,1)S(1)}, u32[]{:S(2)}, u32[]{:S(2)}) collective-permute-start(bf16[384,512]{1,0:T(8,128)(2,1)S(1)} %get-tuple-element.40), channel_id=1, source_target_pairs={{0,4},{4,0},{1,5},{5,1},{2,6},{6,2},{3,7},{7,3},{8,12},{12,8},{9,1... | collective-permute-start | bytes 1179656 | tf_op jit(solution)/shard_map/ppermute | solution.py:390
  106.0 10.7 %collective-permute-start.20 = (bf16[256,512]{1,0:T(8,128)(2,1)S(1)}, bf16[256,512]{1,0:T(8,128)(2,1)S(1)}, u32[]{:S(2)}, u32[]{:S(2)}) collective-permute-start(bf16[256,512]{1,0:T(8,128)(2,1)S(1)} %get-tuple-element.43), channel_id=1, source_target_pairs={{0,128},{128,0},{1,129},{129,1},{2,130},{130,2},{3,131},{131,3},{4... | collective-permute-start | bytes 786440 | tf_op jit(solution)/shard_map/ppermute | solution.py:392
  109.3 12.4 %collective-permute-start.21 = (bf16[256,512]{1,0:T(8,128)(2,1)S(1)}, bf16[256,512]{1,0:T(8,128)(2,1)S(1)}, u32[]{:S(2)}, u32[]{:S(2)}) collective-permute-start(bf16[256,512]{1,0:T(8,128)(2,1)S(1)} %get-tuple-element.44), channel_id=1, source_target_pairs={{0,136},{8,128},{128,8},{136,0},{1,137},{9,129},{129,9},{137,1},{2... | collective-permute-start | bytes 786440 | tf_op jit(solution)/shard_map/ppermute | solution.py:393
  109.4 12.7 %collective-permute-start.19 = (bf16[256,512]{1,0:T(8,128)(2,1)S(1)}, bf16[256,512]{1,0:T(8,128)(2,1)S(1)}, u32[]{:S(2)}, u32[]{:S(2)}) collective-permute-start(bf16[256,512]{1,0:T(8,128)(2,1)S(1)} %get-tuple-element.42), channel_id=1, source_target_pairs={{0,8},{8,0},{1,9},{9,1},{2,10},{10,2},{3,11},{11,3},{4,12},{12,4},... | collective-permute-start | bytes 786440 | tf_op jit(solution)/shard_map/ppermute | solution.py:394
Sparse Core Ops, SparseCore 0:
  9.2 35.3 all-gather.2

commit v4 on v3

--- a/solution.py
+++ b/solution.py
@@ -352,16 +352,16 @@
         split_queries, ("yh", "z"), split_axis=0, concat_axis=0, tiled=True
     )
     partner_up, partner_down = ring_send(partner, 1), ring_send(partner, -1)
+    own_down, own_up = lax.optimization_barrier((own_down, own_up))
     own_down_two = ring_send(own_down, -1)
-    tied_up, own_up = lax.optimization_barrier((partner_up, own_up))
-    partner_up_two = ring_send(tied_up, 1)
+    partner_up_two = ring_send(partner_up, 1)
     parts = [own, partner, own_up, own_down, own_down_two, partner_up, partner_down, partner_up_two]
     offsets = [
         (0, True), (0, False), (7, True), (1, True), (2, True), (7, False), (1, False), (6, False)
     ]
     out_proj, own = lax.optimization_barrier((out_proj, own))
     weights = lax.all_gather(out_proj, "row", axis=0, tiled=False)
-    weights, _ = lax.optimization_barrier((weights, tied_up))
+    weights, _ = lax.optimization_barrier((weights, partner_up))
     sent_half = lax.dynamic_slice_in_dim(weights, (1 - high) * 1024, 1024, 1)
     kept_half = lax.dynamic_slice_in_dim(weights, high * 1024, 1024, 1)
     got_half = lax.ppermute(sent_half, "yh", SWAP)

time: 131 us -> 131 us (level)
  local copies, waits for them, and re-layouts: 4.42 us -> 2.74 us
    unnamed x10 -> x6, local copies, waits for them, and re-layouts: 1.69 us -> 0.01 us
  transfers between devices with their start and end apart: 24 -> 24, of which waited for: 12 -> 13; matrix products, arithmetic and copies ran while one was open for 2% -> 2% of each run, Pallas kernels for 7% -> 8%
where the time goes in v4:
time: 131 us; the launch traced here: 130 us
  waiting for transfers between devices  50.7 us (39%)
  starting transfers between devices  47 us (36%)
  Pallas kernels  16.4 us (13%)
  between operations  13.5 us (10%)
  local copies, waits for them, and re-layouts  2.74 us (2%)
    ppermute x15, waiting for transfers between devices, ring_send(): lax.ppermute(array, 'z', [(index, (index + hops) % 8) for index in range(...  28.4 us
    ppermute x15, starting transfers between devices, ring_send(): lax.ppermute(array, 'z', [(index, (index + hops) % 8) for index in range(...  25.1 us
    all_to_all x1, starting transfers between devices, on_device(): lax.all_to_all(split_queries, ('yh', 'z'), split_axis=0, concat_axis=0, t...  11.2 us
    pallas_call x2, Pallas kernels, attend(): pl.pallas_call(lambda *refs: attend_kernel(offsets, head, *refs), out_sha...  9.47 us
    ppermute x1, waiting for transfers between devices, on_device(): partner = lax.ppermute(other, 'yh', SWAP)  8.64 us
    ppermute x1, waiting for transfers between devices, on_device(): far = lax.ppermute(far, 'yh', SWAP)  6.63 us
    ppermute x1, waiting for transfers between devices, on_device(): cross = lax.ppermute(cross, ('yh', 'yl'), [(0, 3), (1, 2), (2, 1), (3, 0)])  5.01 us
    ppermute x1, starting transfers between devices, on_device(): partner = lax.ppermute(other, 'yh', SWAP)  3.43 us
  transfers between devices with their start and end apart: 24, of which 13 were waited for; matrix products, arithmetic and copies ran while one was open for 2% of the time, Pallas kernels for 8%

profile of v4, /device:TPU:2, one launch (start us, length us, event | category | flops | bytes accessed | tf_op | source)
XLA Modules:
  0.0 130.4 jit_solution(4812041800213032681)
XLA Ops:
  6.5 2.5 %shard_map.82 = (bf16[1152,128]{1,0:T(8,128)(2,1)}, bf16[1152,128]{1,0:T(8,128)(2,1)}, bf16[16,2,64,128]{3,2,1,0:T(8,128)(2,1)}) custom-call(bf16[2,256,256]{2,1,0:T(8,128)(2,1)} %refs_0_.3, bf16[2,256,256]{2,1,0:T(8,128)(2,1)} %refs_1_.3, bf16[32,2,256]{2,1,0:T(2,128)(2,1)} %refs_2_.1, bf16[32,2,256]{2,1,0:T(2,128)(2,1)} %refs_3_.1, ...), custom_call_target="tpu_custom_call" | custom-call | tf_op jit(solution)/shard_map/pallas_call | solution.py:58
  9.0 11.2 %all-to-all-start = ((bf16[16,2,64,128]{3,2,1,0:T(8,128)(2,1)}), bf16[16,2,64,128]{3,2,1,0:T(8,128)(2,1)S(1)}, u32[]{:S(2)}, u32[]{:S(2)}) async-start(bf16[16,2,64,128]{3,2,1,0:T(8,128)(2,1)} %get-tuple-element.25), calls=%async_computation | async-start | bytes 1048576 | tf_op jit(solution)/shard_map/all_to_all | solution.py:351
  20.3 3.4 %collective-permute-start = (bf16[1152,128]{1,0:T(8,128)(2,1)}, bf16[1152,128]{1,0:T(8,128)(2,1)S(1)}, u32[]{:S(2)}, u32[]{:S(2)}) collective-permute-start(bf16[1152,128]{1,0:T(8,128)(2,1)} %get-tuple-element.27), channel_id=1, source_target_pairs={{0,128},{128,0},{1,129},{129,1},{2,130},{130,2},{3,131},{131,3},{4... | collective-permute-start | bytes 884744 | tf_op jit(solution)/shard_map/ppermute | solution.py:349
  23.7 1.5 %collective-permute-start.2 = (bf16[1152,128]{1,0:T(8,128)(2,1)}, bf16[1152,128]{1,0:T(8,128)(2,1)S(1)}, u32[]{:S(2)}, u32[]{:S(2)}) collective-permute-start(bf16[1152,128]{1,0:T(8,128)(2,1)} %get-tuple-element.26.refs_3_), channel_id=1, source_target_pairs={{0,16},{16,32},{32,48},{48,64},{64,80},{80,96},{96,112},{112,0},{1... | collective-permute-start | bytes 884744 | tf_op jit(solution)/shard_map/ppermute | solution.py:340
  25.2 1.8 %collective-permute-start.1 = (bf16[1152,128]{1,0:T(8,128)(2,1)}, bf16[1152,128]{1,0:T(8,128)(2,1)}, u32[]{:S(2)}, u32[]{:S(2)}) collective-permute-start(bf16[1152,128]{1,0:T(8,128)(2,1)} %get-tuple-element.26.refs_3_), channel_id=1, source_target_pairs={{0,112},{16,0},{32,16},{48,32},{64,48},{80,64},{96,80},{112,96},{1... | collective-permute-start | bytes 884744 | tf_op jit(solution)/shard_map/ppermute | solution.py:340
  26.9 8.6 %collective-permute-done.refs_4_ = bf16[1152,128]{1,0:T(8,128)(2,1)S(1)} collective-permute-done((bf16[1152,128]{1,0:T(8,128)(2,1)}, bf16[1152,128]{1,0:T(8,128)(2,1)S(1)}, u32[]{:S(2)}, u32[]{:S(2)}) %collective-permute-start) | collective-permute-done | bytes 294944 | tf_op jit(solution)/shard_map/ppermute | solution.py:349
  36.7 5.6 %collective-permute-done.2.refs_5_ = bf16[1152,128]{1,0:T(8,128)(2,1)S(1)} collective-permute-done((bf16[1152,128]{1,0:T(8,128)(2,1)}, bf16[1152,128]{1,0:T(8,128)(2,1)S(1)}, u32[]{:S(2)}, u32[]{:S(2)}) %collective-permute-start.2) | collective-permute-done | bytes 294944 | tf_op jit(solution)/shard_map/ppermute | solution.py:340
  42.3 1.5 %collective-permute-start.3 = (bf16[1152,128]{1,0:T(8,128)(2,1)}, bf16[1152,128]{1,0:T(8,128)(2,1)}, u32[]{:S(2)}, u32[]{:S(2)}) collective-permute-start(bf16[1152,128]{1,0:T(8,128)(2,1)} %collective-permute-done.1.refs_6_), channel_id=1, source_target_pairs={{0,112},{16,0},{32,16},{48,32},{64,48},{80,64},{96,80},{112,96},{1... | collective-permute-start | bytes 884744 | tf_op jit(solution)/shard_map/ppermute | solution.py:340
  43.9 1.4 %collective-permute-start.5 = (bf16[1152,128]{1,0:T(8,128)(2,1)S(1)}, bf16[1152,128]{1,0:T(8,128)(2,1)}, u32[]{:S(2)}, u32[]{:S(2)}) collective-permute-start(bf16[1152,128]{1,0:T(8,128)(2,1)S(1)} %collective-permute-done.refs_4_), channel_id=1, source_target_pairs={{0,112},{16,0},{32,16},{48,32},{64,48},{80,64},{96,80},{112,96},{1... | collective-permute-start | bytes 884744 | tf_op jit(solution)/shard_map/ppermute | solution.py:340
  45.2 2.4 %collective-permute-done.4.refs_8_ = bf16[1152,128]{1,0:T(8,128)(2,1)} collective-permute-done((bf16[1152,128]{1,0:T(8,128)(2,1)S(1)}, bf16[1152,128]{1,0:T(8,128)(2,1)}, u32[]{:S(2)}, u32[]{:S(2)}) %collective-permute-start.4) | collective-permute-done | bytes 294944 | tf_op jit(solution)/shard_map/ppermute | solution.py:340
  47.7 2.7 %constant_dynamic-slice_fusion = (bf16[4,1024,128]{2,1,0:T(8,128)(2,1)S(1)}, bf16[4,1024,128]{2,1,0:T(8,128)(2,1)}) fusion(bf16[4,2048,128]{2,1,0:T(8,128)(2,1)} %bitcast.1, s32[]{:T(128)S(6)} %select_n.7, s32[]{:T(128)S(6)} %select_n.6), kind=kLoop, calls=%fused_computation | loop fusion | bytes 4194312 | tf_op jit(solution)/shard_map/dynamic_slice | solution.py:366
  50.4 3.0 %collective-permute-start.16 = (bf16[4,1024,128]{2,1,0:T(8,128)(2,1)}, bf16[4,1024,128]{2,1,0:T(8,128)(2,1)S(1)}, u32[]{:S(2)}, u32[]{:S(2)}) collective-permute-start(bf16[4,1024,128]{2,1,0:T(8,128)(2,1)} %get-tuple-element.46), channel_id=1, source_target_pairs={{0,128},{128,0},{1,129},{129,1},{2,130},{130,2},{3,131},{131,3},{4... | collective-permute-start | bytes 3145736 | tf_op jit(solution)/shard_map/ppermute | solution.py:367
  53.4 2.5 %collective-permute-done.5.refs_9_ = bf16[1152,128]{1,0:T(8,128)(2,1)} collective-permute-done((bf16[1152,128]{1,0:T(8,128)(2,1)S(1)}, bf16[1152,128]{1,0:T(8,128)(2,1)}, u32[]{:S(2)}, u32[]{:S(2)}) %collective-permute-start.5) | collective-permute-done | bytes 294944 | tf_op jit(solution)/shard_map/ppermute | solution.py:340
  55.9 1.3 %collective-permute-done.6.refs_10_ = bf16[1152,128]{1,0:T(8,128)(2,1)} collective-permute-done((bf16[1152,128]{1,0:T(8,128)(2,1)}, bf16[1152,128]{1,0:T(8,128)(2,1)}, u32[]{:S(2)}, u32[]{:S(2)}) %collective-permute-start.6) | collective-permute-done | bytes 294944 | tf_op jit(solution)/shard_map/ppermute | solution.py:340
  57.2 4.7 %shard_map.84 = bf16[800,128]{1,0:T(8,128)(2,1)S(1)} custom-call(s32[2]{0:T(128)S(1)} %copy-done, s32[2]{0:T(128)S(1)} %copy-done.2, bf16[16,2,64,128]{3,2,1,0:T(8,128)(2,1)S(1)} %all-to-all-done.refs_2_, bf16[1152,128]{1,0:T(8,128)(2,1)S(1)} %copy-done.1, bf16[1152,128]{1,0:T(8,128)(2,1)S(1)} %collective-permute-done.refs_4_, ...), custom_call_target="tpu_custom_call" | custom-call | flops 5000000000 | bytes 6291456 | tf_op jit(solution)/shard_map/pallas_call | solution.py:208
  62.0 2.9 %collective-permute-start.7 = (bf16[800,128]{1,0:T(8,128)(2,1)S(1)}, bf16[800,128]{1,0:T(8,128)(2,1)S(1)}, u32[]{:S(2)}, u32[]{:S(2)}) collective-permute-start(bf16[800,128]{1,0:T(8,128)(2,1)S(1)} %shard_map.84), channel_id=1, source_target_pairs={{0,64},{16,80},{32,96},{48,112},{64,0},{80,16},{96,32},{112,48},{1... | collective-permute-start | bytes 614408 | tf_op jit(solution)/shard_map/ppermute | solution.py:340
  64.9 4.7 %shard_map.83 = (f32[768,128]{1,0:T(8,128)S(1)}, f32[768,128]{1,0:T(8,128)S(1)}) custom-call(s32[2]{0:T(128)S(1)} %copy-done, s32[2]{0:T(128)S(1)} %copy-done.2, bf16[16,2,64,128]{3,2,1,0:T(8,128)(2,1)S(1)} %all-to-all-done.refs_2_, bf16[1152,128]{1,0:T(8,128)(2,1)S(1)} %copy-done.1, bf16[1152,128]{1,0:T(8,128)(2,1)S(1)} %collective-permute-done.refs_4_, ...), custom_call_target="tpu_custom_call" | custom-call | flops 5000000000 | bytes 6291456 | tf_op jit(solution)/shard_map/pallas_call | solution.py:208
  69.6 6.1 %collective-permute-done.7.message = bf16[800,128]{1,0:T(8,128)(2,1)S(1)} collective-permute-done((bf16[800,128]{1,0:T(8,128)(2,1)S(1)}, bf16[800,128]{1,0:T(8,128)(2,1)S(1)}, u32[]{:S(2)}, u32[]{:S(2)}) %collective-permute-start.7) | collective-permute-done | bytes 204832 | tf_op jit(solution)/shard_map/ppermute | solution.py:340
  76.0 1.2 collective-permute-start.11
  77.2 3.0 %collective-permute-start.9 = (bf16[768,128]{1,0:T(8,128)(2,1)S(1)}, bf16[768,128]{1,0:T(8,128)(2,1)S(1)}, u32[]{:S(2)}, u32[]{:S(2)}) collective-permute-start(bf16[768,128]{1,0:T(8,128)(2,1)S(1)} %shard_map.85.refs_0_), channel_id=1, source_target_pairs={{0,96},{16,112},{32,0},{48,16},{64,32},{80,48},{96,64},{112,80},{1... | collective-permute-start | bytes 589832 | tf_op jit(solution)/shard_map/ppermute | solution.py:340
  80.3 3.2 %collective-permute-start.8 = (bf16[768,128]{1,0:T(8,128)(2,1)S(1)}, bf16[768,128]{1,0:T(8,128)(2,1)S(1)}, u32[]{:S(2)}, u32[]{:S(2)}) collective-permute-start(bf16[768,128]{1,0:T(8,128)(2,1)S(1)} %shard_map.85.refs_0_), channel_id=1, source_target_pairs={{0,112},{16,0},{32,16},{48,32},{64,48},{80,64},{96,80},{112,96},{1... | collective-permute-start | bytes 589832 | tf_op jit(solution)/shard_map/ppermute | solution.py:340
  83.4 6.7 %collective-permute-done.11.refs_6_ = bf16[768,128]{1,0:T(8,128)(2,1)S(1)} collective-permute-done((bf16[768,128]{1,0:T(8,128)(2,1)S(1)}, bf16[768,128]{1,0:T(8,128)(2,1)S(1)}, u32[]{:S(2)}, u32[]{:S(2)}) %collective-permute-start.11) | collective-permute-done | bytes 196640 | tf_op jit(solution)/shard_map/ppermute | solution.py:340
  90.1 3.2 %collective-permute-start.10 = (bf16[768,128]{1,0:T(8,128)(2,1)S(1)}, bf16[768,128]{1,0:T(8,128)(2,1)S(1)}, u32[]{:S(2)}, u32[]{:S(2)}) collective-permute-start(bf16[768,128]{1,0:T(8,128)(2,1)S(1)} %collective-permute-done.9.refs_2_), channel_id=1, source_target_pairs={{0,112},{16,0},{32,16},{48,32},{64,48},{80,64},{96,80},{112,96},{1... | collective-permute-start | bytes 589832 | tf_op jit(solution)/shard_map/ppermute | solution.py:340
  93.4 1.2 collective-permute-start.12
  94.6 3.0 %collective-permute-start.15 = (bf16[384,128]{1,0:T(8,128)(2,1)S(1)}, bf16[384,128]{1,0:T(8,128)(2,1)S(1)}, u32[]{:S(2)}, u32[]{:S(2)}) collective-permute-start(bf16[384,128]{1,0:T(8,128)(2,1)S(1)} %slice.9), channel_id=1, source_target_pairs={{0,96},{16,112},{32,0},{48,16},{64,32},{80,48},{96,64},{112,80},{1... | collective-permute-start | bytes 294920 | tf_op jit(solution)/shard_map/ppermute | solution.py:340
  97.6 3.5 %collective-permute-done.12.refs_4_ = bf16[384,128]{1,0:T(8,128)(2,1)S(1)} collective-permute-done((bf16[384,128]{1,0:T(8,128)(2,1)S(1)}, bf16[384,128]{1,0:T(8,128)(2,1)S(1)}, u32[]{:S(2)}, u32[]{:S(2)}) %collective-permute-start.12) | collective-permute-done | bytes 98336 | tf_op jit(solution)/shard_map/ppermute | solution.py:340
  101.3 1.5 %shard_map.86 = (bf16[768,1024]{1,0:T(8,128)(2,1)S(1)}, f32[384,512]{1,0:T(8,128)S(1)}, bf16[384,512]{1,0:T(8,128)(2,1)S(1)}) custom-call(bf16[768,128]{1,0:T(8,128)(2,1)S(1)} %shard_map.85.refs_0_, bf16[768,128]{1,0:T(8,128)(2,1)S(1)} %collective-permute-done.8.refs_1_, bf16[768,128]{1,0:T(8,128)(2,1)S(1)} %collective-permute-done.9.refs_2_, ...), custom_call_target="tpu_custom_call" | custom-call | flops 2000000000 | bytes 4194304 | tf_op jit(solution)/shard_map/pallas_call | solution.py:278
  102.9 1.7 %collective-permute-done.17.arrived = bf16[384,512]{1,0:T(8,128)(2,1)S(1)} collective-permute-done((bf16[384,512]{1,0:T(8,128)(2,1)S(1)}, bf16[384,512]{1,0:T(8,128)(2,1)S(1)}, u32[]{:S(2)}, u32[]{:S(2)}) %collective-permute-start.17) | collective-permute-done | bytes 393248 | tf_op jit(solution)/shard_map/ppermute | solution.py:386
  105.9 3.2 %collective-permute-start.20 = (bf16[256,512]{1,0:T(8,128)(2,1)S(1)}, bf16[256,512]{1,0:T(8,128)(2,1)S(1)}, u32[]{:S(2)}, u32[]{:S(2)}) collective-permute-start(bf16[256,512]{1,0:T(8,128)(2,1)S(1)} %get-tuple-element.43), channel_id=1, source_target_pairs={{0,128},{128,0},{1,129},{129,1},{2,130},{130,2},{3,131},{131,3},{4... | collective-permute-start | bytes 786440 | tf_op jit(solution)/shard_map/ppermute | solution.py:392
  110.0 6.6 %collective-permute-done.20.far = bf16[256,512]{1,0:T(8,128)(2,1)S(1)} collective-permute-done((bf16[256,512]{1,0:T(8,128)(2,1)S(1)}, bf16[256,512]{1,0:T(8,128)(2,1)S(1)}, u32[]{:S(2)}, u32[]{:S(2)}) %collective-permute-start.20) | collective-permute-done | bytes 262176 | tf_op jit(solution)/shard_map/ppermute | solution.py:392
  116.6 5.0 %collective-permute-done.21.cross = bf16[256,512]{1,0:T(8,128)(2,1)S(1)} collective-permute-done((bf16[256,512]{1,0:T(8,128)(2,1)S(1)}, bf16[256,512]{1,0:T(8,128)(2,1)S(1)}, u32[]{:S(2)}, u32[]{:S(2)}) %collective-permute-start.21) | collective-permute-done | bytes 262176 | tf_op jit(solution)/shard_map/ppermute | solution.py:393
  122.0 1.6 %shard_map.90 = f32[128,2,512]{2,1,0:T(2,128)} custom-call(s32[2]{0:T(128)S(1)} %copy-done, f32[256,512]{1,0:T(8,128)S(1)} %get-tuple-element.41.mine, bf16[256,512]{1,0:T(8,128)(2,1)S(1)} %collective-permute-done.19.near, bf16[256,512]{1,0:T(8,128)(2,1)S(1)} %collective-permute-done.20.far, bf16[256,512]{1,0:T(8,128)(2,1)S(1)} %collective-permute-done.21.cross), custom_call_target="tpu_custom_call" | custom-call | tf_op jit(solution)/shard_map/pallas_call | solution.py:327
  (35 shorter events, 4.3 us)
Async XLA Ops:
  6.5 41.2 %all-gather.3.cloned.1.call-start = ((), (), s32[]{:S(2)}) async-start(), calls=%async_computation.1 | async-start | bytes 2621440 | tf_op jit(solution)/shard_map/all_gather | solution.py:363
  9.0 48.2 %all-to-all-start = ((bf16[16,2,64,128]{3,2,1,0:T(8,128)(2,1)}), bf16[16,2,64,128]{3,2,1,0:T(8,128)(2,1)S(1)}, u32[]{:S(2)}, u32[]{:S(2)}) async-start(bf16[16,2,64,128]{3,2,1,0:T(8,128)(2,1)} %get-tuple-element.25), calls=%async_computation | async-start | bytes 1048576 | tf_op jit(solution)/shard_map/all_to_all | solution.py:351
  20.3 15.3 %collective-permute-start = (bf16[1152,128]{1,0:T(8,128)(2,1)}, bf16[1152,128]{1,0:T(8,128)(2,1)S(1)}, u32[]{:S(2)}, u32[]{:S(2)}) collective-permute-start(bf16[1152,128]{1,0:T(8,128)(2,1)} %get-tuple-element.27), channel_id=1, source_target_pairs={{0,128},{128,0},{1,129},{129,1},{2,130},{130,2},{3,131},{131,3},{4... | collective-permute-start | bytes 884744 | tf_op jit(solution)/shard_map/ppermute | solution.py:349
  23.7 18.6 %collective-permute-start.2 = (bf16[1152,128]{1,0:T(8,128)(2,1)}, bf16[1152,128]{1,0:T(8,128)(2,1)S(1)}, u32[]{:S(2)}, u32[]{:S(2)}) collective-permute-start(bf16[1152,128]{1,0:T(8,128)(2,1)} %get-tuple-element.26.refs_3_), channel_id=1, source_target_pairs={{0,16},{16,32},{32,48},{48,64},{64,80},{80,96},{96,112},{112,0},{1... | collective-permute-start | bytes 884744 | tf_op jit(solution)/shard_map/ppermute | solution.py:340
  25.2 17.2 %collective-permute-start.1 = (bf16[1152,128]{1,0:T(8,128)(2,1)}, bf16[1152,128]{1,0:T(8,128)(2,1)}, u32[]{:S(2)}, u32[]{:S(2)}) collective-permute-start(bf16[1152,128]{1,0:T(8,128)(2,1)} %get-tuple-element.26.refs_3_), channel_id=1, source_target_pairs={{0,112},{16,0},{32,16},{48,32},{64,48},{80,64},{96,80},{112,96},{1... | collective-permute-start | bytes 884744 | tf_op jit(solution)/shard_map/ppermute | solution.py:340
  35.6 12.1 %collective-permute-start.4 = (bf16[1152,128]{1,0:T(8,128)(2,1)S(1)}, bf16[1152,128]{1,0:T(8,128)(2,1)}, u32[]{:S(2)}, u32[]{:S(2)}) collective-permute-start(bf16[1152,128]{1,0:T(8,128)(2,1)S(1)} %collective-permute-done.refs_4_), channel_id=1, source_target_pairs={{0,16},{16,32},{32,48},{48,64},{64,80},{80,96},{96,112},{112,0},{1... | collective-permute-start | bytes 884744 | tf_op jit(solution)/shard_map/ppermute | solution.py:340
  42.3 13.6 %collective-permute-start.3 = (bf16[1152,128]{1,0:T(8,128)(2,1)}, bf16[1152,128]{1,0:T(8,128)(2,1)}, u32[]{:S(2)}, u32[]{:S(2)}) collective-permute-start(bf16[1152,128]{1,0:T(8,128)(2,1)} %collective-permute-done.1.refs_6_), channel_id=1, source_target_pairs={{0,112},{16,0},{32,16},{48,32},{64,48},{80,64},{96,80},{112,96},{1... | collective-permute-start | bytes 884744 | tf_op jit(solution)/shard_map/ppermute | solution.py:340
  43.9 12.0 %collective-permute-start.5 = (bf16[1152,128]{1,0:T(8,128)(2,1)S(1)}, bf16[1152,128]{1,0:T(8,128)(2,1)}, u32[]{:S(2)}, u32[]{:S(2)}) collective-permute-start(bf16[1152,128]{1,0:T(8,128)(2,1)S(1)} %collective-permute-done.refs_4_), channel_id=1, source_target_pairs={{0,112},{16,0},{32,16},{48,32},{64,48},{80,64},{96,80},{112,96},{1... | collective-permute-start | bytes 884744 | tf_op jit(solution)/shard_map/ppermute | solution.py:340
  47.7 9.5 %collective-permute-start.6 = (bf16[1152,128]{1,0:T(8,128)(2,1)}, bf16[1152,128]{1,0:T(8,128)(2,1)}, u32[]{:S(2)}, u32[]{:S(2)}) collective-permute-start(bf16[1152,128]{1,0:T(8,128)(2,1)} %collective-permute-done.4.refs_8_), channel_id=1, source_target_pairs={{0,16},{16,32},{32,48},{48,64},{64,80},{80,96},{96,112},{112,0},{1... | collective-permute-start | bytes 884744 | tf_op jit(solution)/shard_map/ppermute | solution.py:340
  47.7 9.5 %copy-start = (s32[2]{0:T(128)S(1)}, s32[2]{0:T(128)}, u32[]{:S(2)}) copy-start(s32[2]{0:T(128)} %skip_blocks.1) | copy-start | bytes 28
  47.7 9.5 %copy-start.1 = (bf16[1152,128]{1,0:T(8,128)(2,1)S(1)}, bf16[1152,128]{1,0:T(8,128)(2,1)}, u32[]{:S(2)}) copy-start(bf16[1152,128]{1,0:T(8,128)(2,1)} %get-tuple-element.26.refs_3_) | copy-start | bytes 884740
  47.7 9.5 %copy-start.2 = (s32[2]{0:T(128)S(1)}, s32[2]{0:T(128)}, u32[]{:S(2)}) copy-start(s32[2]{0:T(128)} %refs_1_.5) | copy-start | bytes 28
  50.4 50.9 %collective-permute-start.16 = (bf16[4,1024,128]{2,1,0:T(8,128)(2,1)}, bf16[4,1024,128]{2,1,0:T(8,128)(2,1)S(1)}, u32[]{:S(2)}, u32[]{:S(2)}) collective-permute-start(bf16[4,1024,128]{2,1,0:T(8,128)(2,1)} %get-tuple-element.46), channel_id=1, source_target_pairs={{0,128},{128,0},{1,129},{129,1},{2,130},{130,2},{3,131},{131,3},{4... | collective-permute-start | bytes 3145736 | tf_op jit(solution)/shard_map/ppermute | solution.py:367
  62.0 13.7 %collective-permute-start.7 = (bf16[800,128]{1,0:T(8,128)(2,1)S(1)}, bf16[800,128]{1,0:T(8,128)(2,1)S(1)}, u32[]{:S(2)}, u32[]{:S(2)}) collective-permute-start(bf16[800,128]{1,0:T(8,128)(2,1)S(1)} %shard_map.84), channel_id=1, source_target_pairs={{0,64},{16,80},{32,96},{48,112},{64,0},{80,16},{96,32},{112,48},{1... | collective-permute-start | bytes 614408 | tf_op jit(solution)/shard_map/ppermute | solution.py:340
  76.0 14.1 %collective-permute-start.11 = (bf16[768,128]{1,0:T(8,128)(2,1)S(1)}, bf16[768,128]{1,0:T(8,128)(2,1)S(1)}, u32[]{:S(2)}, u32[]{:S(2)}) collective-permute-start(bf16[768,128]{1,0:T(8,128)(2,1)S(1)} %shard_map.85.refs_0_), channel_id=1, source_target_pairs={{0,32},{16,48},{32,64},{48,80},{64,96},{80,112},{96,0},{112,16},{1... | collective-permute-start | bytes 589832 | tf_op jit(solution)/shard_map/ppermute | solution.py:340
  77.2 12.9 %collective-permute-start.9 = (bf16[768,128]{1,0:T(8,128)(2,1)S(1)}, bf16[768,128]{1,0:T(8,128)(2,1)S(1)}, u32[]{:S(2)}, u32[]{:S(2)}) collective-permute-start(bf16[768,128]{1,0:T(8,128)(2,1)S(1)} %shard_map.85.refs_0_), channel_id=1, source_target_pairs={{0,96},{16,112},{32,0},{48,16},{64,32},{80,48},{96,64},{112,80},{1... | collective-permute-start | bytes 589832 | tf_op jit(solution)/shard_map/ppermute | solution.py:340
  80.2 13.2 %collective-permute-start.14 = (bf16[768,128]{1,0:T(8,128)(2,1)S(1)}, bf16[768,128]{1,0:T(8,128)(2,1)S(1)}, u32[]{:S(2)}, u32[]{:S(2)}) collective-permute-start(bf16[768,128]{1,0:T(8,128)(2,1)S(1)} %shard_map.85.refs_0_), channel_id=1, source_target_pairs={{0,16},{16,32},{32,48},{48,64},{64,80},{80,96},{96,112},{112,0},{1... | collective-permute-start | bytes 589832 | tf_op jit(solution)/shard_map/ppermute | solution.py:340
  80.3 14.4 %collective-permute-start.8 = (bf16[768,128]{1,0:T(8,128)(2,1)S(1)}, bf16[768,128]{1,0:T(8,128)(2,1)S(1)}, u32[]{:S(2)}, u32[]{:S(2)}) collective-permute-start(bf16[768,128]{1,0:T(8,128)(2,1)S(1)} %shard_map.85.refs_0_), channel_id=1, source_target_pairs={{0,112},{16,0},{32,16},{48,32},{64,48},{80,64},{96,80},{112,96},{1... | collective-permute-start | bytes 589832 | tf_op jit(solution)/shard_map/ppermute | solution.py:340
  90.1 11.2 %collective-permute-start.13 = (bf16[768,128]{1,0:T(8,128)(2,1)S(1)}, bf16[768,128]{1,0:T(8,128)(2,1)S(1)}, u32[]{:S(2)}, u32[]{:S(2)}) collective-permute-start(bf16[768,128]{1,0:T(8,128)(2,1)S(1)} %collective-permute-done.11.refs_6_), channel_id=1, source_target_pairs={{0,16},{16,32},{32,48},{48,64},{64,80},{80,96},{96,112},{112,0},{1... | collective-permute-start | bytes 589832 | tf_op jit(solution)/shard_map/ppermute | solution.py:340
  90.1 11.2 %collective-permute-start.10 = (bf16[768,128]{1,0:T(8,128)(2,1)S(1)}, bf16[768,128]{1,0:T(8,128)(2,1)S(1)}, u32[]{:S(2)}, u32[]{:S(2)}) collective-permute-start(bf16[768,128]{1,0:T(8,128)(2,1)S(1)} %collective-permute-done.9.refs_2_), channel_id=1, source_target_pairs={{0,112},{16,0},{32,16},{48,32},{64,48},{80,64},{96,80},{112,96},{1... | collective-permute-start | bytes 589832 | tf_op jit(solution)/shard_map/ppermute | solution.py:340
  93.4 7.8 %collective-permute-start.12 = (bf16[384,128]{1,0:T(8,128)(2,1)S(1)}, bf16[384,128]{1,0:T(8,128)(2,1)S(1)}, u32[]{:S(2)}, u32[]{:S(2)}) collective-permute-start(bf16[384,128]{1,0:T(8,128)(2,1)S(1)} %slice.8), channel_id=1, source_target_pairs={{0,32},{16,48},{32,64},{48,80},{64,96},{80,112},{96,0},{112,16},{1... | collective-permute-start | bytes 294920 | tf_op jit(solution)/shard_map/ppermute | solution.py:340
  94.6 6.7 %collective-permute-start.15 = (bf16[384,128]{1,0:T(8,128)(2,1)S(1)}, bf16[384,128]{1,0:T(8,128)(2,1)S(1)}, u32[]{:S(2)}, u32[]{:S(2)}) collective-permute-start(bf16[384,128]{1,0:T(8,128)(2,1)S(1)} %slice.9), channel_id=1, source_target_pairs={{0,96},{16,112},{32,0},{48,16},{64,32},{80,48},{96,64},{112,80},{1... | collective-permute-start | bytes 294920 | tf_op jit(solution)/shard_map/ppermute | solution.py:340
  102.8 1.8 %collective-permute-start.17 = (bf16[384,512]{1,0:T(8,128)(2,1)S(1)}, bf16[384,512]{1,0:T(8,128)(2,1)S(1)}, u32[]{:S(2)}, u32[]{:S(2)}) collective-permute-start(bf16[384,512]{1,0:T(8,128)(2,1)S(1)} %get-tuple-element.36), channel_id=1, source_target_pairs={{0,4},{4,0},{1,5},{5,1},{2,6},{6,2},{3,7},{7,3},{8,12},{12,8},{9,1... | collective-permute-start | bytes 1179656 | tf_op jit(solution)/shard_map/ppermute | solution.py:386
  105.7 3.6 %collective-permute-start.18 = (bf16[384,512]{1,0:T(8,128)(2,1)S(1)}, bf16[384,512]{1,0:T(8,128)(2,1)S(1)}, u32[]{:S(2)}, u32[]{:S(2)}) collective-permute-start(bf16[384,512]{1,0:T(8,128)(2,1)S(1)} %get-tuple-element.40), channel_id=1, source_target_pairs={{0,4},{4,0},{1,5},{5,1},{2,6},{6,2},{3,7},{7,3},{8,12},{12,8},{9,1... | collective-permute-start | bytes 1179656 | tf_op jit(solution)/shard_map/ppermute | solution.py:390
  105.9 10.7 %collective-permute-start.20 = (bf16[256,512]{1,0:T(8,128)(2,1)S(1)}, bf16[256,512]{1,0:T(8,128)(2,1)S(1)}, u32[]{:S(2)}, u32[]{:S(2)}) collective-permute-start(bf16[256,512]{1,0:T(8,128)(2,1)S(1)} %get-tuple-element.43), channel_id=1, source_target_pairs={{0,128},{128,0},{1,129},{129,1},{2,130},{130,2},{3,131},{131,3},{4... | collective-permute-start | bytes 786440 | tf_op jit(solution)/shard_map/ppermute | solution.py:392
  109.1 12.5 %collective-permute-start.21 = (bf16[256,512]{1,0:T(8,128)(2,1)S(1)}, bf16[256,512]{1,0:T(8,128)(2,1)S(1)}, u32[]{:S(2)}, u32[]{:S(2)}) collective-permute-start(bf16[256,512]{1,0:T(8,128)(2,1)S(1)} %get-tuple-element.44), channel_id=1, source_target_pairs={{0,136},{8,128},{128,8},{136,0},{1,137},{9,129},{129,9},{137,1},{2... | collective-permute-start | bytes 786440 | tf_op jit(solution)/shard_map/ppermute | solution.py:393
  109.4 12.6 %collective-permute-start.19 = (bf16[256,512]{1,0:T(8,128)(2,1)S(1)}, bf16[256,512]{1,0:T(8,128)(2,1)S(1)}, u32[]{:S(2)}, u32[]{:S(2)}) collective-permute-start(bf16[256,512]{1,0:T(8,128)(2,1)S(1)} %get-tuple-element.42), channel_id=1, source_target_pairs={{0,8},{8,0},{1,9},{9,1},{2,10},{10,2},{3,11},{11,3},{4,12},{12,4},... | collective-permute-start | bytes 786440 | tf_op jit(solution)/shard_map/ppermute | solution.py:394
Sparse Core Ops, SparseCore 0:
  9.2 35.3 all-gather.2

commit v5 on v3

--- a/solution.py
+++ b/solution.py
@@ -211,7 +211,7 @@
         in_specs=[SMEM] * 2 + [VMEM] * (1 + len(parts)),
         out_specs=out_specs,
         scratch_shapes=scratch,
-        compiler_params=PARAMS,
+        compiler_params=pltpu.CompilerParams(vmem_limit_bytes=56 * 1024 * 1024),
         cost_estimate=pl.CostEstimate(
             flops=5 * 10**9, bytes_accessed=6 * 2**20, transcendentals=2 * 10**6
         ),

time: 131 us -> 134 us (1.023)
  Pallas kernels: 16.2 us -> 18.6 us
    pallas_call x2, Pallas kernels: 9.28 us -> 11.7 us  [attend(): pl.pallas_call(lambda *refs: attend_kernel(offsets, head, *refs), out_sha...]
  transfers between devices with their start and end apart: 24 -> 24, of which waited for: 12 -> 14; matrix products, arithmetic and copies ran while one was open for 2% -> 1% of each run, Pallas kernels for 7% -> 9%
where the time goes in v5:
time: 134 us; the launch traced here: 133 us
  waiting for transfers between devices  51.3 us (38%)
  starting transfers between devices  45.5 us (34%)
  Pallas kernels  18.6 us (14%)
  between operations  13.5 us (10%)
  local copies, waits for them, and re-layouts  3.72 us (3%)
    ppermute x15, waiting for transfers between devices, ring_send(): lax.ppermute(array, 'z', [(index, (index + hops) % 8) for index in range(...  28.4 us
    ppermute x15, starting transfers between devices, ring_send(): lax.ppermute(array, 'z', [(index, (index + hops) % 8) for index in range(...  23.5 us
    pallas_call x2, Pallas kernels, attend(): pl.pallas_call(lambda *refs: attend_kernel(offsets, head, *refs), out_sha...  11.7 us
    all_to_all x1, starting transfers between devices, on_device(): lax.all_to_all(split_queries, ('yh', 'z'), split_axis=0, concat_axis=0, t...  11.3 us
    ppermute x1, waiting for transfers between devices, on_device(): partner = lax.ppermute(other, 'yh', SWAP)  9.19 us
    ppermute x1, waiting for transfers between devices, on_device(): far = lax.ppermute(far, 'yh', SWAP)  6.6 us
    ppermute x1, waiting for transfers between devices, on_device(): cross = lax.ppermute(cross, ('yh', 'yl'), [(0, 3), (1, 2), (2, 1), (3, 0)])  5.02 us
    ppermute x1, starting transfers between devices, on_device(): partner = lax.ppermute(other, 'yh', SWAP)  3.38 us
  transfers between devices with their start and end apart: 24, of which 14 were waited for; matrix products, arithmetic and copies ran while one was open for 1% of the time, Pallas kernels for 9%

profile of v5, /device:TPU:2, one launch (start us, length us, event | category | flops | bytes accessed | tf_op | source)
XLA Modules:
  0.0 132.7 jit_solution(11069930703846201708)
XLA Ops:
  6.5 2.5 %shard_map.82 = (bf16[1152,128]{1,0:T(8,128)(2,1)}, bf16[1152,128]{1,0:T(8,128)(2,1)}, bf16[16,2,64,128]{3,2,1,0:T(8,128)(2,1)}) custom-call(bf16[2,256,256]{2,1,0:T(8,128)(2,1)} %refs_0_.3, bf16[2,256,256]{2,1,0:T(8,128)(2,1)} %refs_1_.3, bf16[32,2,256]{2,1,0:T(2,128)(2,1)} %refs_2_.1, bf16[32,2,256]{2,1,0:T(2,128)(2,1)} %refs_3_.1, ...), custom_call_target="tpu_custom_call" | custom-call | tf_op jit(solution)/shard_map/pallas_call | solution.py:58
  9.0 11.3 %all-to-all-start = ((bf16[16,2,64,128]{3,2,1,0:T(8,128)(2,1)}), bf16[16,2,64,128]{3,2,1,0:T(8,128)(2,1)}, u32[]{:S(2)}, u32[]{:S(2)}) async-start(bf16[16,2,64,128]{3,2,1,0:T(8,128)(2,1)} %get-tuple-element.25), calls=%async_computation | async-start | bytes 1048576 | tf_op jit(solution)/shard_map/all_to_all | solution.py:351
  20.3 3.4 %collective-permute-start = (bf16[1152,128]{1,0:T(8,128)(2,1)}, bf16[1152,128]{1,0:T(8,128)(2,1)S(1)}, u32[]{:S(2)}, u32[]{:S(2)}) collective-permute-start(bf16[1152,128]{1,0:T(8,128)(2,1)} %get-tuple-element.27), channel_id=1, source_target_pairs={{0,128},{128,0},{1,129},{129,1},{2,130},{130,2},{3,131},{131,3},{4... | collective-permute-start | bytes 884744 | tf_op jit(solution)/shard_map/ppermute | solution.py:349
  23.7 2.7 %collective-permute-start.3 = (bf16[1152,128]{1,0:T(8,128)(2,1)}, bf16[1152,128]{1,0:T(8,128)(2,1)}, u32[]{:S(2)}, u32[]{:S(2)}) collective-permute-start(bf16[1152,128]{1,0:T(8,128)(2,1)} %get-tuple-element.26.refs_3_), channel_id=1, source_target_pairs={{0,112},{16,0},{32,16},{48,32},{64,48},{80,64},{96,80},{112,96},{1... | collective-permute-start | bytes 884744 | tf_op jit(solution)/shard_map/ppermute | solution.py:340
  26.4 9.2 %collective-permute-done.refs_4_ = bf16[1152,128]{1,0:T(8,128)(2,1)S(1)} collective-permute-done((bf16[1152,128]{1,0:T(8,128)(2,1)}, bf16[1152,128]{1,0:T(8,128)(2,1)S(1)}, u32[]{:S(2)}, u32[]{:S(2)}) %collective-permute-start) | collective-permute-done | bytes 294944 | tf_op jit(solution)/shard_map/ppermute | solution.py:349
  35.6 1.1 collective-permute-start.1
  36.7 2.1 %collective-permute-start.5 = (bf16[1152,128]{1,0:T(8,128)(2,1)S(1)}, bf16[1152,128]{1,0:T(8,128)(2,1)}, u32[]{:S(2)}, u32[]{:S(2)}) collective-permute-start(bf16[1152,128]{1,0:T(8,128)(2,1)S(1)} %collective-permute-done.refs_4_), channel_id=1, source_target_pairs={{0,112},{16,0},{32,16},{48,32},{64,48},{80,64},{96,80},{112,96},{1... | collective-permute-start | bytes 884744 | tf_op jit(solution)/shard_map/ppermute | solution.py:340
  38.8 2.4 %collective-permute-done.3.refs_6_ = bf16[1152,128]{1,0:T(8,128)(2,1)} collective-permute-done((bf16[1152,128]{1,0:T(8,128)(2,1)}, bf16[1152,128]{1,0:T(8,128)(2,1)}, u32[]{:S(2)}, u32[]{:S(2)}) %collective-permute-start.3) | collective-permute-done | bytes 294944 | tf_op jit(solution)/shard_map/ppermute | solution.py:340
  41.2 1.6 %collective-permute-start.4 = (bf16[1152,128]{1,0:T(8,128)(2,1)}, bf16[1152,128]{1,0:T(8,128)(2,1)}, u32[]{:S(2)}, u32[]{:S(2)}) collective-permute-start(bf16[1152,128]{1,0:T(8,128)(2,1)} %collective-permute-done.3.refs_6_), channel_id=1, source_target_pairs={{0,112},{16,0},{32,16},{48,32},{64,48},{80,64},{96,80},{112,96},{1... | collective-permute-start | bytes 884744 | tf_op jit(solution)/shard_map/ppermute | solution.py:340
  42.8 4.9 %collective-permute-done.1.refs_8_ = bf16[1152,128]{1,0:T(8,128)(2,1)} collective-permute-done((bf16[1152,128]{1,0:T(8,128)(2,1)S(1)}, bf16[1152,128]{1,0:T(8,128)(2,1)}, u32[]{:S(2)}, u32[]{:S(2)}) %collective-permute-start.1) | collective-permute-done | bytes 294944 | tf_op jit(solution)/shard_map/ppermute | solution.py:340
  47.7 1.7 %constant_dynamic-slice_fusion = (bf16[4,1024,128]{2,1,0:T(8,128)(2,1)S(1)}, bf16[4,1024,128]{2,1,0:T(8,128)(2,1)S(1)}) fusion(bf16[4,2048,128]{2,1,0:T(8,128)(2,1)} %bitcast.1, s32[]{:T(128)S(6)} %select_n.7, s32[]{:T(128)S(6)} %select_n.6), kind=kLoop, calls=%fused_computation | loop fusion | bytes 4194312 | tf_op jit(solution)/shard_map/dynamic_slice | solution.py:366
  49.4 3.1 %collective-permute-start.16 = (bf16[4,1024,128]{2,1,0:T(8,128)(2,1)S(1)}, bf16[4,1024,128]{2,1,0:T(8,128)(2,1)S(1)}, u32[]{:S(2)}, u32[]{:S(2)}) collective-permute-start(bf16[4,1024,128]{2,1,0:T(8,128)(2,1)S(1)} %get-tuple-element.46), channel_id=1, source_target_pairs={{0,128},{128,0},{1,129},{129,1},{2,130},{130,2},{3,131},{131,3},{4... | collective-permute-start | bytes 3145736 | tf_op jit(solution)/shard_map/ppermute | solution.py:367
  52.8 4.4 %collective-permute-done.6.refs_10_ = bf16[1152,128]{1,0:T(8,128)(2,1)} collective-permute-done((bf16[1152,128]{1,0:T(8,128)(2,1)}, bf16[1152,128]{1,0:T(8,128)(2,1)}, u32[]{:S(2)}, u32[]{:S(2)}) %collective-permute-start.6) | collective-permute-done | bytes 294944 | tf_op jit(solution)/shard_map/ppermute | solution.py:340
  57.2 5.8 %shard_map.84 = bf16[800,128]{1,0:T(8,128)(2,1)} custom-call(s32[2]{0:T(128)} %skip_blocks.1, s32[2]{0:T(128)} %refs_1_.5, bf16[16,2,64,128]{3,2,1,0:T(8,128)(2,1)} %all-to-all-done.refs_2_, bf16[1152,128]{1,0:T(8,128)(2,1)} %get-tuple-element.26.refs_3_, bf16[1152,128]{1,0:T(8,128)(2,1)} %copy-done.3, bf16[1152,128]{1,0:T(8,128)(2,1)} %copy-done.4, ...), custom_call_target="tpu_custom_call" | custom-call | flops 5000000000 | bytes 6291456 | tf_op jit(solution)/shard_map/pallas_call | solution.py:208
  63.0 2.6 %collective-permute-start.7 = (bf16[800,128]{1,0:T(8,128)(2,1)}, bf16[800,128]{1,0:T(8,128)(2,1)S(1)}, u32[]{:S(2)}, u32[]{:S(2)}) collective-permute-start(bf16[800,128]{1,0:T(8,128)(2,1)} %shard_map.84), channel_id=1, source_target_pairs={{0,64},{16,80},{32,96},{48,112},{64,0},{80,16},{96,32},{112,48},{1... | collective-permute-start | bytes 614408 | tf_op jit(solution)/shard_map/ppermute | solution.py:340
  65.6 5.9 %shard_map.83 = (f32[768,128]{1,0:T(8,128)}, f32[768,128]{1,0:T(8,128)}) custom-call(s32[2]{0:T(128)} %skip_blocks.1, s32[2]{0:T(128)} %refs_1_.5, bf16[16,2,64,128]{3,2,1,0:T(8,128)(2,1)} %all-to-all-done.refs_2_, bf16[1152,128]{1,0:T(8,128)(2,1)} %get-tuple-element.26.refs_3_, bf16[1152,128]{1,0:T(8,128)(2,1)} %copy-done.3, bf16[1152,128]{1,0:T(8,128)(2,1)} %copy-done.4, ...), custom_call_target="tpu_custom_call" | custom-call | flops 5000000000 | bytes 6291456 | tf_op jit(solution)/shard_map/pallas_call | solution.py:208
  71.5 5.2 %collective-permute-done.7.message = bf16[800,128]{1,0:T(8,128)(2,1)S(1)} collective-permute-done((bf16[800,128]{1,0:T(8,128)(2,1)}, bf16[800,128]{1,0:T(8,128)(2,1)S(1)}, u32[]{:S(2)}, u32[]{:S(2)}) %collective-permute-start.7) | collective-permute-done | bytes 204832 | tf_op jit(solution)/shard_map/ppermute | solution.py:340
  79.0 2.9 %collective-permute-start.11 = (bf16[768,128]{1,0:T(8,128)(2,1)S(1)}, bf16[768,128]{1,0:T(8,128)(2,1)S(1)}, u32[]{:S(2)}, u32[]{:S(2)}) collective-permute-start(bf16[768,128]{1,0:T(8,128)(2,1)S(1)} %shard_map.85.refs_0_), channel_id=1, source_target_pairs={{0,32},{16,48},{32,64},{48,80},{64,96},{80,112},{96,0},{112,16},{1... | collective-permute-start | bytes 589832 | tf_op jit(solution)/shard_map/ppermute | solution.py:340
  81.9 3.2 %collective-permute-start.8 = (bf16[768,128]{1,0:T(8,128)(2,1)S(1)}, bf16[768,128]{1,0:T(8,128)(2,1)S(1)}, u32[]{:S(2)}, u32[]{:S(2)}) collective-permute-start(bf16[768,128]{1,0:T(8,128)(2,1)S(1)} %shard_map.85.refs_0_), channel_id=1, source_target_pairs={{0,112},{16,0},{32,16},{48,32},{64,48},{80,64},{96,80},{112,96},{1... | collective-permute-start | bytes 589832 | tf_op jit(solution)/shard_map/ppermute | solution.py:340
  85.2 3.8 %collective-permute-done.9.refs_2_ = bf16[768,128]{1,0:T(8,128)(2,1)S(1)} collective-permute-done((bf16[768,128]{1,0:T(8,128)(2,1)S(1)}, bf16[768,128]{1,0:T(8,128)(2,1)S(1)}, u32[]{:S(2)}, u32[]{:S(2)}) %collective-permute-start.9) | collective-permute-done | bytes 196640 | tf_op jit(solution)/shard_map/ppermute | solution.py:340
  88.9 1.4 %collective-permute-start.10 = (bf16[768,128]{1,0:T(8,128)(2,1)S(1)}, bf16[768,128]{1,0:T(8,128)(2,1)S(1)}, u32[]{:S(2)}, u32[]{:S(2)}) collective-permute-start(bf16[768,128]{1,0:T(8,128)(2,1)S(1)} %collective-permute-done.9.refs_2_), channel_id=1, source_target_pairs={{0,112},{16,0},{32,16},{48,32},{64,48},{80,64},{96,80},{112,96},{1... | collective-permute-start | bytes 589832 | tf_op jit(solution)/shard_map/ppermute | solution.py:340
  90.9 1.6 %collective-permute-start.13 = (bf16[768,128]{1,0:T(8,128)(2,1)S(1)}, bf16[768,128]{1,0:T(8,128)(2,1)S(1)}, u32[]{:S(2)}, u32[]{:S(2)}) collective-permute-start(bf16[768,128]{1,0:T(8,128)(2,1)S(1)} %collective-permute-done.11.refs_6_), channel_id=1, source_target_pairs={{0,16},{16,32},{32,48},{48,64},{64,80},{80,96},{96,112},{112,0},{1... | collective-permute-start | bytes 589832 | tf_op jit(solution)/shard_map/ppermute | solution.py:340
  92.5 2.0 %collective-permute-done.14.refs_7_ = bf16[768,128]{1,0:T(8,128)(2,1)S(1)} collective-permute-done((bf16[768,128]{1,0:T(8,128)(2,1)S(1)}, bf16[768,128]{1,0:T(8,128)(2,1)S(1)}, u32[]{:S(2)}, u32[]{:S(2)}) %collective-permute-start.14) | collective-permute-done | bytes 196640 | tf_op jit(solution)/shard_map/ppermute | solution.py:340
  94.6 2.0 %collective-permute-start.12 = (bf16[384,128]{1,0:T(8,128)(2,1)S(1)}, bf16[384,128]{1,0:T(8,128)(2,1)S(1)}, u32[]{:S(2)}, u32[]{:S(2)}) collective-permute-start(bf16[384,128]{1,0:T(8,128)(2,1)S(1)} %slice.8), channel_id=1, source_target_pairs={{0,32},{16,48},{32,64},{48,80},{64,96},{80,112},{96,0},{112,16},{1... | collective-permute-start | bytes 294920 | tf_op jit(solution)/shard_map/ppermute | solution.py:340
  96.6 2.1 %collective-permute-start.15 = (bf16[384,128]{1,0:T(8,128)(2,1)S(1)}, bf16[384,128]{1,0:T(8,128)(2,1)S(1)}, u32[]{:S(2)}, u32[]{:S(2)}) collective-permute-start(bf16[384,128]{1,0:T(8,128)(2,1)S(1)} %slice.9), channel_id=1, source_target_pairs={{0,96},{16,112},{32,0},{48,16},{64,32},{80,48},{96,64},{112,80},{1... | collective-permute-start | bytes 294920 | tf_op jit(solution)/shard_map/ppermute | solution.py:340
  98.7 4.9 %collective-permute-done.12.refs_4_ = bf16[384,128]{1,0:T(8,128)(2,1)S(1)} collective-permute-done((bf16[384,128]{1,0:T(8,128)(2,1)S(1)}, bf16[384,128]{1,0:T(8,128)(2,1)S(1)}, u32[]{:S(2)}, u32[]{:S(2)}) %collective-permute-start.12) | collective-permute-done | bytes 98336 | tf_op jit(solution)/shard_map/ppermute | solution.py:340
  103.6 1.4 %shard_map.86 = (bf16[768,1024]{1,0:T(8,128)(2,1)S(1)}, f32[384,512]{1,0:T(8,128)S(1)}, bf16[384,512]{1,0:T(8,128)(2,1)S(1)}) custom-call(bf16[768,128]{1,0:T(8,128)(2,1)S(1)} %shard_map.85.refs_0_, bf16[768,128]{1,0:T(8,128)(2,1)S(1)} %collective-permute-done.8.refs_1_, bf16[768,128]{1,0:T(8,128)(2,1)S(1)} %collective-permute-done.9.refs_2_, ...), custom_call_target="tpu_custom_call" | custom-call | flops 2000000000 | bytes 4194304 | tf_op jit(solution)/shard_map/pallas_call | solution.py:278
  105.2 1.7 %collective-permute-done.17.arrived = bf16[384,512]{1,0:T(8,128)(2,1)S(1)} collective-permute-done((bf16[384,512]{1,0:T(8,128)(2,1)S(1)}, bf16[384,512]{1,0:T(8,128)(2,1)S(1)}, u32[]{:S(2)}, u32[]{:S(2)}) %collective-permute-start.17) | collective-permute-done | bytes 393248 | tf_op jit(solution)/shard_map/ppermute | solution.py:386
  108.2 3.2 %collective-permute-start.20 = (bf16[256,512]{1,0:T(8,128)(2,1)S(1)}, bf16[256,512]{1,0:T(8,128)(2,1)S(1)}, u32[]{:S(2)}, u32[]{:S(2)}) collective-permute-start(bf16[256,512]{1,0:T(8,128)(2,1)S(1)} %get-tuple-element.43), channel_id=1, source_target_pairs={{0,128},{128,0},{1,129},{129,1},{2,130},{130,2},{3,131},{131,3},{4... | collective-permute-start | bytes 786440 | tf_op jit(solution)/shard_map/ppermute | solution.py:392
  112.3 6.6 %collective-permute-done.20.far = bf16[256,512]{1,0:T(8,128)(2,1)S(1)} collective-permute-done((bf16[256,512]{1,0:T(8,128)(2,1)S(1)}, bf16[256,512]{1,0:T(8,128)(2,1)S(1)}, u32[]{:S(2)}, u32[]{:S(2)}) %collective-permute-start.20) | collective-permute-done | bytes 262176 | tf_op jit(solution)/shard_map/ppermute | solution.py:392
  118.9 5.0 %collective-permute-done.21.cross = bf16[256,512]{1,0:T(8,128)(2,1)S(1)} collective-permute-done((bf16[256,512]{1,0:T(8,128)(2,1)S(1)}, bf16[256,512]{1,0:T(8,128)(2,1)S(1)}, u32[]{:S(2)}, u32[]{:S(2)}) %collective-permute-start.21) | collective-permute-done | bytes 262176 | tf_op jit(solution)/shard_map/ppermute | solution.py:393
  124.3 1.6 %shard_map.90 = f32[128,2,512]{2,1,0:T(2,128)} custom-call(s32[2]{0:T(128)S(1)} %copy-done.2, f32[256,512]{1,0:T(8,128)S(1)} %get-tuple-element.41.mine, bf16[256,512]{1,0:T(8,128)(2,1)S(1)} %collective-permute-done.19.near, bf16[256,512]{1,0:T(8,128)(2,1)S(1)} %collective-permute-done.20.far, bf16[256,512]{1,0:T(8,128)(2,1)S(1)} %collective-permute-done.21.cross), custom_call_target="tpu_custom_call" | custom-call | tf_op jit(solution)/shard_map/pallas_call | solution.py:327
  (39 shorter events, 5.9 us)
Async XLA Ops:
  6.5 41.2 %all-gather.3.cloned.1.call-start = ((), (), s32[]{:S(2)}) async-start(), calls=%async_computation.1 | async-start | bytes 2621440 | tf_op jit(solution)/shard_map/all_gather | solution.py:363
  9.0 48.2 %all-to-all-start = ((bf16[16,2,64,128]{3,2,1,0:T(8,128)(2,1)}), bf16[16,2,64,128]{3,2,1,0:T(8,128)(2,1)}, u32[]{:S(2)}, u32[]{:S(2)}) async-start(bf16[16,2,64,128]{3,2,1,0:T(8,128)(2,1)} %get-tuple-element.25), calls=%async_computation | async-start | bytes 1048576 | tf_op jit(solution)/shard_map/all_to_all | solution.py:351
  20.3 15.3 %collective-permute-start = (bf16[1152,128]{1,0:T(8,128)(2,1)}, bf16[1152,128]{1,0:T(8,128)(2,1)S(1)}, u32[]{:S(2)}, u32[]{:S(2)}) collective-permute-start(bf16[1152,128]{1,0:T(8,128)(2,1)} %get-tuple-element.27), channel_id=1, source_target_pairs={{0,128},{128,0},{1,129},{129,1},{2,130},{130,2},{3,131},{131,3},{4... | collective-permute-start | bytes 884744 | tf_op jit(solution)/shard_map/ppermute | solution.py:349
  23.7 17.5 %collective-permute-start.3 = (bf16[1152,128]{1,0:T(8,128)(2,1)}, bf16[1152,128]{1,0:T(8,128)(2,1)}, u32[]{:S(2)}, u32[]{:S(2)}) collective-permute-start(bf16[1152,128]{1,0:T(8,128)(2,1)} %get-tuple-element.26.refs_3_), channel_id=1, source_target_pairs={{0,112},{16,0},{32,16},{48,32},{64,48},{80,64},{96,80},{112,96},{1... | collective-permute-start | bytes 884744 | tf_op jit(solution)/shard_map/ppermute | solution.py:340
  26.4 16.4 %collective-permute-start.2 = (bf16[1152,128]{1,0:T(8,128)(2,1)}, bf16[1152,128]{1,0:T(8,128)(2,1)S(1)}, u32[]{:S(2)}, u32[]{:S(2)}) collective-permute-start(bf16[1152,128]{1,0:T(8,128)(2,1)} %get-tuple-element.26.refs_3_), channel_id=1, source_target_pairs={{0,16},{16,32},{32,48},{48,64},{64,80},{80,96},{96,112},{112,0},{1... | collective-permute-start | bytes 884744 | tf_op jit(solution)/shard_map/ppermute | solution.py:340
  35.6 13.9 %copy-start.3 = (bf16[1152,128]{1,0:T(8,128)(2,1)}, bf16[1152,128]{1,0:T(8,128)(2,1)S(1)}, u32[]{:S(2)}) copy-start(bf16[1152,128]{1,0:T(8,128)(2,1)S(1)} %collective-permute-done.refs_4_) | copy-start | bytes 884740
  35.6 12.1 %collective-permute-start.1 = (bf16[1152,128]{1,0:T(8,128)(2,1)S(1)}, bf16[1152,128]{1,0:T(8,128)(2,1)}, u32[]{:S(2)}, u32[]{:S(2)}) collective-permute-start(bf16[1152,128]{1,0:T(8,128)(2,1)S(1)} %collective-permute-done.refs_4_), channel_id=1, source_target_pairs={{0,16},{16,32},{32,48},{48,64},{64,80},{80,96},{96,112},{112,0},{1... | collective-permute-start | bytes 884744 | tf_op jit(solution)/shard_map/ppermute | solution.py:340
  36.7 16.1 %collective-permute-start.5 = (bf16[1152,128]{1,0:T(8,128)(2,1)S(1)}, bf16[1152,128]{1,0:T(8,128)(2,1)}, u32[]{:S(2)}, u32[]{:S(2)}) collective-permute-start(bf16[1152,128]{1,0:T(8,128)(2,1)S(1)} %collective-permute-done.refs_4_), channel_id=1, source_target_pairs={{0,112},{16,0},{32,16},{48,32},{64,48},{80,64},{96,80},{112,96},{1... | collective-permute-start | bytes 884744 | tf_op jit(solution)/shard_map/ppermute | solution.py:340
  41.2 11.6 %collective-permute-start.4 = (bf16[1152,128]{1,0:T(8,128)(2,1)}, bf16[1152,128]{1,0:T(8,128)(2,1)}, u32[]{:S(2)}, u32[]{:S(2)}) collective-permute-start(bf16[1152,128]{1,0:T(8,128)(2,1)} %collective-permute-done.3.refs_6_), channel_id=1, source_target_pairs={{0,112},{16,0},{32,16},{48,32},{64,48},{80,64},{96,80},{112,96},{1... | collective-permute-start | bytes 884744 | tf_op jit(solution)/shard_map/ppermute | solution.py:340
  42.8 4.9 %copy-start.4 = (bf16[1152,128]{1,0:T(8,128)(2,1)}, bf16[1152,128]{1,0:T(8,128)(2,1)S(1)}, u32[]{:S(2)}) copy-start(bf16[1152,128]{1,0:T(8,128)(2,1)S(1)} %collective-permute-done.2.refs_5_) | copy-start | bytes 884740
  47.7 9.5 %collective-permute-start.6 = (bf16[1152,128]{1,0:T(8,128)(2,1)}, bf16[1152,128]{1,0:T(8,128)(2,1)}, u32[]{:S(2)}, u32[]{:S(2)}) collective-permute-start(bf16[1152,128]{1,0:T(8,128)(2,1)} %collective-permute-done.1.refs_8_), channel_id=1, source_target_pairs={{0,16},{16,32},{32,48},{48,64},{64,80},{80,96},{96,112},{112,0},{1... | collective-permute-start | bytes 884744 | tf_op jit(solution)/shard_map/ppermute | solution.py:340
  49.4 54.2 %collective-permute-start.16 = (bf16[4,1024,128]{2,1,0:T(8,128)(2,1)S(1)}, bf16[4,1024,128]{2,1,0:T(8,128)(2,1)S(1)}, u32[]{:S(2)}, u32[]{:S(2)}) collective-permute-start(bf16[4,1024,128]{2,1,0:T(8,128)(2,1)S(1)} %get-tuple-element.46), channel_id=1, source_target_pairs={{0,128},{128,0},{1,129},{129,1},{2,130},{130,2},{3,131},{131,3},{4... | collective-permute-start | bytes 3145736 | tf_op jit(solution)/shard_map/ppermute | solution.py:367
  63.0 13.6 %collective-permute-start.7 = (bf16[800,128]{1,0:T(8,128)(2,1)}, bf16[800,128]{1,0:T(8,128)(2,1)S(1)}, u32[]{:S(2)}, u32[]{:S(2)}) collective-permute-start(bf16[800,128]{1,0:T(8,128)(2,1)} %shard_map.84), channel_id=1, source_target_pairs={{0,64},{16,80},{32,96},{48,112},{64,0},{80,16},{96,32},{112,48},{1... | collective-permute-start | bytes 614408 | tf_op jit(solution)/shard_map/ppermute | solution.py:340
  76.7 1.0 copy-start
  77.7 1.0 copy-start.1
  78.9 10.0 %collective-permute-start.9 = (bf16[768,128]{1,0:T(8,128)(2,1)S(1)}, bf16[768,128]{1,0:T(8,128)(2,1)S(1)}, u32[]{:S(2)}, u32[]{:S(2)}) collective-permute-start(bf16[768,128]{1,0:T(8,128)(2,1)S(1)} %shard_map.85.refs_0_), channel_id=1, source_target_pairs={{0,96},{16,112},{32,0},{48,16},{64,32},{80,48},{96,64},{112,80},{1... | collective-permute-start | bytes 589832 | tf_op jit(solution)/shard_map/ppermute | solution.py:340
  79.0 11.9 %collective-permute-start.11 = (bf16[768,128]{1,0:T(8,128)(2,1)S(1)}, bf16[768,128]{1,0:T(8,128)(2,1)S(1)}, u32[]{:S(2)}, u32[]{:S(2)}) collective-permute-start(bf16[768,128]{1,0:T(8,128)(2,1)S(1)} %shard_map.85.refs_0_), channel_id=1, source_target_pairs={{0,32},{16,48},{32,64},{48,80},{64,96},{80,112},{96,0},{112,16},{1... | collective-permute-start | bytes 589832 | tf_op jit(solution)/shard_map/ppermute | solution.py:340
  81.9 12.7 %collective-permute-start.14 = (bf16[768,128]{1,0:T(8,128)(2,1)S(1)}, bf16[768,128]{1,0:T(8,128)(2,1)S(1)}, u32[]{:S(2)}, u32[]{:S(2)}) collective-permute-start(bf16[768,128]{1,0:T(8,128)(2,1)S(1)} %shard_map.85.refs_0_), channel_id=1, source_target_pairs={{0,16},{16,32},{32,48},{48,64},{64,80},{80,96},{96,112},{112,0},{1... | collective-permute-start | bytes 589832 | tf_op jit(solution)/shard_map/ppermute | solution.py:340
  81.9 14.6 %collective-permute-start.8 = (bf16[768,128]{1,0:T(8,128)(2,1)S(1)}, bf16[768,128]{1,0:T(8,128)(2,1)S(1)}, u32[]{:S(2)}, u32[]{:S(2)}) collective-permute-start(bf16[768,128]{1,0:T(8,128)(2,1)S(1)} %shard_map.85.refs_0_), channel_id=1, source_target_pairs={{0,112},{16,0},{32,16},{48,32},{64,48},{80,64},{96,80},{112,96},{1... | collective-permute-start | bytes 589832 | tf_op jit(solution)/shard_map/ppermute | solution.py:340
  88.9 14.7 %collective-permute-start.10 = (bf16[768,128]{1,0:T(8,128)(2,1)S(1)}, bf16[768,128]{1,0:T(8,128)(2,1)S(1)}, u32[]{:S(2)}, u32[]{:S(2)}) collective-permute-start(bf16[768,128]{1,0:T(8,128)(2,1)S(1)} %collective-permute-done.9.refs_2_), channel_id=1, source_target_pairs={{0,112},{16,0},{32,16},{48,32},{64,48},{80,64},{96,80},{112,96},{1... | collective-permute-start | bytes 589832 | tf_op jit(solution)/shard_map/ppermute | solution.py:340
  90.9 12.7 %collective-permute-start.13 = (bf16[768,128]{1,0:T(8,128)(2,1)S(1)}, bf16[768,128]{1,0:T(8,128)(2,1)S(1)}, u32[]{:S(2)}, u32[]{:S(2)}) collective-permute-start(bf16[768,128]{1,0:T(8,128)(2,1)S(1)} %collective-permute-done.11.refs_6_), channel_id=1, source_target_pairs={{0,16},{16,32},{32,48},{48,64},{64,80},{80,96},{96,112},{112,0},{1... | collective-permute-start | bytes 589832 | tf_op jit(solution)/shard_map/ppermute | solution.py:340
  94.6 9.0 %collective-permute-start.12 = (bf16[384,128]{1,0:T(8,128)(2,1)S(1)}, bf16[384,128]{1,0:T(8,128)(2,1)S(1)}, u32[]{:S(2)}, u32[]{:S(2)}) collective-permute-start(bf16[384,128]{1,0:T(8,128)(2,1)S(1)} %slice.8), channel_id=1, source_target_pairs={{0,32},{16,48},{32,64},{48,80},{64,96},{80,112},{96,0},{112,16},{1... | collective-permute-start | bytes 294920 | tf_op jit(solution)/shard_map/ppermute | solution.py:340
  96.6 7.0 %collective-permute-start.15 = (bf16[384,128]{1,0:T(8,128)(2,1)S(1)}, bf16[384,128]{1,0:T(8,128)(2,1)S(1)}, u32[]{:S(2)}, u32[]{:S(2)}) collective-permute-start(bf16[384,128]{1,0:T(8,128)(2,1)S(1)} %slice.9), channel_id=1, source_target_pairs={{0,96},{16,112},{32,0},{48,16},{64,32},{80,48},{96,64},{112,80},{1... | collective-permute-start | bytes 294920 | tf_op jit(solution)/shard_map/ppermute | solution.py:340
  105.1 1.8 %collective-permute-start.17 = (bf16[384,512]{1,0:T(8,128)(2,1)S(1)}, bf16[384,512]{1,0:T(8,128)(2,1)S(1)}, u32[]{:S(2)}, u32[]{:S(2)}) collective-permute-start(bf16[384,512]{1,0:T(8,128)(2,1)S(1)} %get-tuple-element.36), channel_id=1, source_target_pairs={{0,4},{4,0},{1,5},{5,1},{2,6},{6,2},{3,7},{7,3},{8,12},{12,8},{9,1... | collective-permute-start | bytes 1179656 | tf_op jit(solution)/shard_map/ppermute | solution.py:386
  107.0 17.3 %copy-start.2 = (s32[2]{0:T(128)S(1)}, s32[2]{0:T(128)}, u32[]{:S(2)}) copy-start(s32[2]{0:T(128)} %skip_blocks.1) | copy-start | bytes 28
  108.0 3.6 %collective-permute-start.18 = (bf16[384,512]{1,0:T(8,128)(2,1)S(1)}, bf16[384,512]{1,0:T(8,128)(2,1)S(1)}, u32[]{:S(2)}, u32[]{:S(2)}) collective-permute-start(bf16[384,512]{1,0:T(8,128)(2,1)S(1)} %get-tuple-element.40), channel_id=1, source_target_pairs={{0,4},{4,0},{1,5},{5,1},{2,6},{6,2},{3,7},{7,3},{8,12},{12,8},{9,1... | collective-permute-start | bytes 1179656 | tf_op jit(solution)/shard_map/ppermute | solution.py:390
  108.2 10.7 %collective-permute-start.20 = (bf16[256,512]{1,0:T(8,128)(2,1)S(1)}, bf16[256,512]{1,0:T(8,128)(2,1)S(1)}, u32[]{:S(2)}, u32[]{:S(2)}) collective-permute-start(bf16[256,512]{1,0:T(8,128)(2,1)S(1)} %get-tuple-element.43), channel_id=1, source_target_pairs={{0,128},{128,0},{1,129},{129,1},{2,130},{130,2},{3,131},{131,3},{4... | collective-permute-start | bytes 786440 | tf_op jit(solution)/shard_map/ppermute | solution.py:392
  111.4 12.5 %collective-permute-start.21 = (bf16[256,512]{1,0:T(8,128)(2,1)S(1)}, bf16[256,512]{1,0:T(8,128)(2,1)S(1)}, u32[]{:S(2)}, u32[]{:S(2)}) collective-permute-start(bf16[256,512]{1,0:T(8,128)(2,1)S(1)} %get-tuple-element.44), channel_id=1, source_target_pairs={{0,136},{8,128},{128,8},{136,0},{1,137},{9,129},{129,9},{137,1},{2... | collective-permute-start | bytes 786440 | tf_op jit(solution)/shard_map/ppermute | solution.py:393
  111.7 12.6 %collective-permute-start.19 = (bf16[256,512]{1,0:T(8,128)(2,1)S(1)}, bf16[256,512]{1,0:T(8,128)(2,1)S(1)}, u32[]{:S(2)}, u32[]{:S(2)}) collective-permute-start(bf16[256,512]{1,0:T(8,128)(2,1)S(1)} %get-tuple-element.42), channel_id=1, source_target_pairs={{0,8},{8,0},{1,9},{9,1},{2,10},{10,2},{3,11},{11,3},{4,12},{12,4},... | collective-permute-start | bytes 786440 | tf_op jit(solution)/shard_map/ppermute | solution.py:394
Sparse Core Ops, SparseCore 0:
  9.2 35.3 all-gather.2
